TPU v7x, 32 devices: a whole 2x2x4 slice. The times are simulated.
32 devices in a mesh: groups: 2 (over x), block: 16 (over z, y, core).
Axes of the slice: x: 2, y: 2, z: 4, core: 2. Of those that a mesh axis runs over, the one named last changes fastest.
Arguments:
- slices: bfloat16 [4, 12288, 2048], P(None, ('groups', 'block')), parts along dimension 1, may hold values from -0.75 to 0.75
- slice_mix: float32 [4, 4], replicated, may hold values from -1 to 1
- lengths: int32 [32, 4], P(('groups', 'block')), parts along dimension 0, may hold values from 1 to 96, 288 in all within a row
- search_step: bfloat16 [4096], P('groups'), parts along dimension 0, may hold values from -0.125 to 0.125
Outputs:
- schur_matrix: float32 [4096, 2048], P(('groups', 'block')), parts along dimension 0
- schur_step: float32 [4096], P('groups'), parts along dimension 0
There are 2 independent parts, one for each index of `groups`. A program takes and returns all parts, laid end to end along the dimension named above; an argument that names none is the same for every part. Nothing has to cross between parts.
Inputs may be any that keep to these rules, and one draw needn't show every extreme that they name: `lengths`: each row holds the used rows of one device's 4 blocks; a row sums to 288 and its largest entry is 96.
All inputs are finite; a program needn't handle non-finite values.
Results may differ from a plain program's by a relative error of at most 0.0055.
Values sent between devices are 32-bit elements; how exact they have to be, the bound alone decides.
No kernel may reach another device: no remote copies, remote signals or barrier semaphores. Data moves between devices by JAX's collectives and lax.ppermute only.
A program may use at most 128 MiB of HBM per device.

v0:
```python
import jax
import jax.numpy as jnp
from jax import lax
from jax.sharding import PartitionSpec as P


def mix_slices(slices, slice_mix, lengths):
    slice_count = slices.shape[0]
    symmetric = (slice_mix + slice_mix.T) * 0.5
    coupling = symmetric * (1.0 - jnp.eye(slice_count, dtype=jnp.float32))
    block_count = lengths.shape[1]
    block_rows = slices.shape[1] // block_count
    position = lax.broadcasted_iota(jnp.int32, (block_count, block_rows), 1)
    row_used = (position < lengths[0][:, None]).reshape(-1).astype(jnp.float32)
    rows_out = []
    for target in range(slice_count):
        total = coupling[target, 0] * slices[0].astype(jnp.float32)
        for source in range(1, slice_count):
            total = total + coupling[target, source] * slices[source].astype(jnp.float32)
        rows_out.append(total)
    stacked = jnp.stack(rows_out) * row_used[None, :, None]
    return stacked.astype(jnp.bfloat16)


def on_device(slices, slice_mix, lengths, search_step):
    width = slices.shape[2]
    mixed = mix_slices(slices, slice_mix, lengths)
    left = slices.reshape(-1, width)
    right = mixed.reshape(-1, width)
    schur_rows = lax.psum_scatter(
        lax.dot_general(left, right, (((0,), (0,)), ((), ())), preferred_element_type=jnp.float32),
        "block",
        scatter_dimension=0,
        tiled=True,
    )
    applied = jnp.dot(right, search_step, preferred_element_type=jnp.float32)
    head_part = applied.astype(jnp.bfloat16)
    tail_part = (applied - head_part.astype(jnp.float32)).astype(jnp.bfloat16)
    dims = (((0,), (0,)), ((), ()))
    share = lax.dot_general(left, head_part, dims, preferred_element_type=jnp.float32)
    share = share + lax.dot_general(left, tail_part, dims, preferred_element_type=jnp.float32)
    schur_step = lax.psum(share, "block")
    return (schur_rows, schur_step)


def solution(mesh):
    return jax.shard_map(
        on_device,
        mesh=mesh,
        in_specs=(
            P(None, ("groups", "block"), None),
            P(),
            P(("groups", "block"), None),
            P("groups"),
        ),
        out_specs=(P(("groups", "block"), None), P("groups")),
        check_vma=False,
    )
```

profile of v0, /device:TPU:0, one launch (start us, length us, event | category | flops | bytes accessed | tf_op | source)
XLA Modules:
  0.0 238.7 jit_solution(13698805752388967102)
XLA Ops:
  7.2 0.0 reduce-scatter.2.cloned.1.call-start
  7.2 0.7 fusion.16
  7.9 0.1 reshape.28
  8.0 0.8 copy.6
  8.8 0.7 fusion.15
  9.5 0.7 fusion.17
  10.2 0.0 slice-start
  10.2 0.0 slice-start.1
  10.2 9.4 %fusion.4 = (f32[1,384,2048]{2,1,0:T(8,128)S(1)}, f32[1,384,2048]{2,1,0:T(8,128)S(1)}) fusion(f32[]{:T(128)} %bitcast.4, f32[]{:T(128)} %bitcast.3, f32[]{:T(128)} %bitcast.2, f32[]{:T(128)} %bitcast.1, bf16[4,384,2048]{2,1,0:T(8,128)(2,1)} %param.4, f32[]{:T(128)} %bitcast.16, f32[]{:T(128)} %bitcast.15, f32[]{:T(128)} %bitcast.14, f32[]{:T(128)} %bitcast.13), kind=kLoop, calls=%fused_computation.24 | loop fusion | flops 14155776 | bytes 12582944 | tf_op jit(solution)/shard_map/add | solution.py:19
  19.6 0.0 copy-start
  19.6 0.0 slice-done
  19.6 0.0 slice-done.1
  19.6 8.0 %fusion.7 = (f32[1,384,2048]{2,1,0:T(8,128)S(1)}, f32[1,384,2048]{2,1,0:T(8,128)}) fusion(f32[]{:T(128)} %bitcast.8, f32[]{:T(128)} %bitcast.7, f32[]{:T(128)} %bitcast.6, f32[]{:T(128)} %bitcast.5, bf16[4,384,2048]{2,1,0:T(8,128)(2,1)S(1)} %bitcast.44, f32[]{:T(128)} %bitcast.12, f32[]{:T(128)} %bitcast.11, f32[]{:T(128)} %bitcast.10, f32[]{:T(128)} %bitcast.9), kind=kLoop, calls=%fused_computation.27 | loop fusion | flops 14155776 | bytes 12582944 | tf_op jit(solution)/shard_map/add | solution.py:19
  27.7 0.0 copy-start.1
  27.7 0.0 copy-done
  27.7 1.7 copy-done.1
  29.4 18.2 %convolution_bitcast_fusion = f32[2048,2048]{0,1:T(8,128)} fusion(bf16[4,384,2048]{2,1,0:T(8,128)(2,1)S(1)} %bitcast.44, f32[384]{0:T(512)S(1)} %reshape.28, f32[1,384,2048]{2,1,0:T(8,128)S(1)} %get-tuple-element.7, f32[1,384,2048]{2,1,0:T(8,128)} %get-tuple-element.9, f32[1,384,2048]{2,1,0:T(8,128)S(1)} %get-tuple-element.8, ...), kind=kOutput, calls=%fused_computation.4 | convolution fusion | flops 12900630528 | bytes 35653120 | tf_op jit(solution)/shard_map/dot_general | solution.py:31
  47.6 0.0 copy-start.2
  47.6 0.0 reduce-scatter.2.cloned.1.call-update
  47.6 0.6 copy-done.2
  48.3 9.0 %pad_maximum_fusion = f32[4,384,2048]{2,1,0:T(8,128)} fusion(f32[1,384,2048]{2,1,0:T(8,128)} %copy-done, f32[1,384,2048]{2,1,0:T(8,128)} %get-tuple-element.9, f32[1,384,2048]{2,1,0:T(8,128)} %copy-done.1, f32[1,384,2048]{2,1,0:T(8,128)S(1)} %get-tuple-element.6), kind=kLoop, calls=%fused_computation | loop fusion | flops 9437184 | bytes 25165824 | tf_op jit(solution)/shard_map/stack | solution.py:21
  57.3 11.0 %fusion = bf16[1536,2048]{1,0:T(8,128)(2,1)} fusion(f32[4,384,2048]{2,1,0:T(8,128)} %pad_maximum_fusion, f32[1536]{0:T(1024)S(1)} %mul.172), kind=kLoop, calls=%fused_computation.2 | loop fusion | flops 6291456 | bytes 18880512 | tf_op jit(solution)/shard_map/convert_element_type | solution.py:22
  68.3 5.7 %convolution_reduce_fusion = f32[1536]{0:T(1024)S(1)} fusion(bf16[1536,2048]{1,0:T(8,128)(2,1)} %fusion, bf16[2048,1]{0,1:T(2,128)(2,1)S(1)} %reshape.30), kind=kOutput, calls=%fused_computation.34 | convolution fusion | flops 6291456 | bytes 6301696 | tf_op jit(solution)/shard_map/dot_general | solution.py:36
  74.1 4.6 %fusion.18 = f32[1,2048]{1,0:T(1,128)S(1)} fusion(bf16[1536,1]{0,1:T(2,128)(2,1)S(1)} %reshape.32, bf16[1536,2048]{1,0:T(8,128)(2,1)} %bitcast.41), kind=kOutput, calls=%fused_computation.43 | convolution fusion | flops 6291456 | bytes 6302720 | tf_op jit(solution)/shard_map/dot_general | solution.py:40
  78.7 3.7 %fusion.19 = f32[1,2048]{1,0:T(1,128)S(1)} fusion(bf16[1536,1]{0,1:T(2,128)(2,1)S(1)} %reshape.34, bf16[1536,2048]{1,0:T(8,128)(2,1)} %bitcast.42), kind=kOutput, calls=%fused_computation.44 | convolution fusion | flops 6291456 | bytes 6302720 | tf_op jit(solution)/shard_map/dot_general | solution.py:41
  82.4 38.2 %psum.7 = f32[2048]{0:T(1024)} all-reduce(f32[2048]{0:T(1024)S(1)} %add.71), channel_id=1, replica_groups=mesh['groups'=2,'block'=16] {'block'}, use_global_device_ids=true, to_apply=%region_1.0 | all-reduce | flops 2048 | bytes 16384 | tf_op jit(solution)/shard_map/psum | solution.py:42
  120.6 108.7 %reduce-scatter.2.cloned.1.call-done = f32[128,2048]{0,1:T(8,128)} async-done(((f32[2048,2048]{0,1:T(8,128)}), f32[128,2048]{0,1:T(8,128)}) %reduce-scatter.2.cloned.1.call-update) | async-done | bytes 1048592 | tf_op jit(solution)/shard_map/reduce_scatter | solution.py:30
  229.3 2.5 %copy.8 = f32[128,2048]{1,0:T(8,128)} copy(f32[128,2048]{0,1:T(8,128)} %reduce-scatter.2.cloned.1.call-done) | data formatting | bytes 2097152
  (8 shorter events, 0.0 us)
Async XLA Ops:
  7.2 222.2 %reduce-scatter.2.cloned.1.call-start = ((), (), s32[]{:S(2)}) async-start(), calls=%async_computation.1 | async-start | bytes 17825792 | tf_op jit(solution)/shard_map/reduce_scatter | solution.py:30
  10.2 9.4 %slice-start = ((s8[6291456]{0:T(1024)(128)(4,1)}), s8[4194304]{0:T(1024)(128)(4,1)S(1)}, s32[]{:S(2)}) async-start(s8[6291456]{0:T(1024)(128)(4,1)} %bitcast.43), calls=%async_computation.2 | async-start | bytes 8388608
  10.2 9.4 %slice-start.1 = ((s8[6291456]{0:T(1024)(128)(4,1)}), s8[2097152]{0:T(1024)(128)(4,1)S(1)}, s32[]{:S(2)}) async-start(s8[6291456]{0:T(1024)(128)(4,1)} %bitcast.43), calls=%async_computation.3 | async-start | bytes 4194304
  19.6 8.1 %copy-start = (f32[1,384,2048]{2,1,0:T(8,128)}, f32[1,384,2048]{2,1,0:T(8,128)S(1)}, u32[]{:S(2)}) copy-start(f32[1,384,2048]{2,1,0:T(8,128)S(1)} %get-tuple-element.7) | copy-start | bytes 9437188
  27.7 1.7 copy-start.1
  47.6 0.7 copy-start.2
Sparse Core Ops, SparseCore 0:
  47.7 181.5 reduce-scatter.1
where the time goes:
time: 239 us
  waiting for transfers between devices  109 us (46%)
  other arithmetic  38.9 us (16%)
  blocking collectives  38.2 us (16%)
  matrix products  32.3 us (14%)
  between operations  14.1 us (6%)
  local copies, waits for them, and re-layouts  6.48 us (3%)
    reduce_scatter x1, waiting for transfers between devices, on_device(): lax.psum_scatter(lax.dot_general(left, right, (((0,), (0,)), ((), ())), p...  109 us
    psum x1, blocking collectives, on_device(): schur_step = lax.psum(share, 'block')  38.2 us
    dot_general x1, matrix products, on_device(): lax.dot_general(left, right, (((0,), (0,)), ((), ())), preferred_element_...  18.2 us
    add x2, other arithmetic, mix_slices(): total + coupling[target, source] * slices[source].astype(jnp.float32)  17.4 us
    convert_element_type x1, other arithmetic, mix_slices(): return stacked.astype(jnp.bfloat16)  11 us
    another operation x1, other arithmetic, mix_slices(): stacked = jnp.stack(rows_out) * row_used[None, :, None]  9 us
    dot_general x1, matrix products, on_device(): applied = jnp.dot(right, search_step, preferred_element_type=jnp.float32)  5.73 us
    unnamed x13, local copies, waits for them, and re-layouts  5.66 us
  transfers between devices with their start and end apart: 1, of which 1 were waited for; matrix products, arithmetic and copies ran while one was open for 14% of the time, Pallas kernels for 0%

commit v1 on v0

v1 whole, which is shorter than its diff:
```python
import functools

import jax
import jax.numpy as jnp
from jax import lax
from jax.experimental import pallas as pl
from jax.experimental.pallas import tpu as pltpu
from jax.sharding import PartitionSpec as P

AXIS = "block"
CORES = 2
COLS = 2
DIMS0 = (((0,), (0,)), ((), ()))
DIMS1 = (((1,), (1,)), ((), ()))
VMEM = pl.BlockSpec(memory_space=pltpu.VMEM)
SMEM = pl.BlockSpec(memory_space=pltpu.SMEM)


def row_mask(lengths_ref, rows, width):
    blocks = lengths_ref.shape[1]
    step = rows // blocks
    row = lax.broadcasted_iota(jnp.int32, (rows, width), 0)
    limit = jnp.zeros((rows, width), jnp.int32)
    for j in range(blocks):
        limit = jnp.where(row >= j * step, j * step + lengths_ref[0, j], limit)
    return row < limit


def mix_kernel(mix_ref, lengths_ref, slices_ref, left_ref, right_ref):
    count, rows, width = slices_ref.shape
    used = row_mask(lengths_ref, rows, width)
    s = [slices_ref[k] for k in range(count)]
    f = [a.astype(jnp.float32) for a in s]
    for k in range(count):
        total = None
        for l in range(count):
            if l != k:
                term = ((mix_ref[k, l] + mix_ref[l, k]) * 0.5) * f[l]
                total = term if total is None else total + term
        right_ref[k * rows : (k + 1) * rows, :] = jnp.where(used, total, 0.0).astype(jnp.bfloat16)
        left_ref[:, k * rows : (k + 1) * rows] = s[k].T


def mix(slices, slice_mix, lengths, tile):
    count, rows, width = slices.shape
    depth = count * rows
    return pl.pallas_call(
        mix_kernel,
        grid=(width // tile,),
        in_specs=[SMEM, SMEM, pl.BlockSpec((count, rows, tile), lambda i: (0, 0, i))],
        out_specs=[
            pl.BlockSpec((tile, depth), lambda i: (i, 0)),
            pl.BlockSpec((depth, tile), lambda i: (0, i)),
        ],
        out_shape=[
            jax.ShapeDtypeStruct((width, depth), jnp.bfloat16),
            jax.ShapeDtypeStruct((depth, width), jnp.bfloat16),
        ],
        compiler_params=pltpu.CompilerParams(vmem_limit_bytes=24 << 20),
        name="mix",
    )(slice_mix, lengths, slices)


def place():
    me = lax.axis_index(AXIS)
    core = lax.rem(me, CORES)
    y = lax.rem(me // CORES, COLS)
    z = me // (CORES * COLS)
    return z, y, core


def tiles_kernel(lines, unit, jobs, left_ref, right_ref, *refs):
    outs, acc = refs[:-1], refs[-1]
    chips = lines * COLS
    z, y, core = place()
    for n, (shift, sy) in enumerate(jobs):
        own_ref, other_ref = outs[2 * n], outs[2 * n + 1]
        half = 2 * shift == chips

        def step(sz, carry):
            row = lax.rem(z + sz, lines) * COLS + (y ^ sy)
            col = lax.rem(row + shift, chips)
            acc[...] = jnp.dot(
                left_ref[pl.ds(pl.multiple_of(row * 2 * unit, 2 * unit), 2 * unit), :],
                right_ref[:, pl.ds(pl.multiple_of(col * 2 * unit, 2 * unit), 2 * unit)],
                preferred_element_type=jnp.float32,
            )
            flip = (row >= shift).astype(jnp.int32) if half else 0
            for ref, owner in ((own_ref, core), (other_ref, 1 - core)):
                for j in range(ref.shape[1]):
                    first = pl.multiple_of((owner ^ j ^ flip) * unit, unit)
                    ref[sz, j] = acc[pl.ds(pl.multiple_of(owner * unit, unit), unit), pl.ds(first, unit)]
            return carry

        lax.fori_loop(0, lines, step, 0)


def tiles(left, right, jobs, lines, unit):
    shapes = []
    for shift, _ in jobs:
        blocks = 1 if 2 * shift == lines * COLS else CORES
        shapes += [jax.ShapeDtypeStruct((lines, blocks, unit, unit), jnp.float32)] * 2
    flops = 2 * len(jobs) * lines * (2 * unit) ** 2 * left.shape[1]
    out = pl.pallas_call(
        functools.partial(tiles_kernel, lines, unit, jobs),
        in_specs=[VMEM, VMEM],
        out_specs=[VMEM] * len(shapes),
        out_shape=shapes,
        scratch_shapes=[pltpu.VMEM((2 * unit, 2 * unit), jnp.float32)],
        cost_estimate=pl.CostEstimate(flops=flops, bytes_accessed=0, transcendentals=0),
        compiler_params=pltpu.CompilerParams(vmem_limit_bytes=24 << 20),
        name="tiles",
    )(left, right)
    return [(out[2 * n], out[2 * n + 1]) for n in range(len(jobs))]


def vector_kernel(left_ref, right_ref, step_ref, out_ref):
    x = jnp.broadcast_to(step_ref[...], (8, step_ref.shape[1]))
    applied = lax.dot_general(x, right_ref[...], DIMS1, preferred_element_type=jnp.float32)
    head = applied.astype(jnp.bfloat16)
    tail = (applied - head.astype(jnp.float32)).astype(jnp.bfloat16)
    row = lax.broadcasted_iota(jnp.int32, applied.shape, 0)
    both = jnp.where(row == 0, head.astype(jnp.float32), jnp.where(row == 1, tail.astype(jnp.float32), 0.0))
    share = lax.dot_general(both.astype(jnp.bfloat16), left_ref[...], DIMS1, preferred_element_type=jnp.float32)
    out_ref[...] = share[0:1, :] + share[1:2, :]


def vector(left, right, step):
    return pl.pallas_call(
        vector_kernel,
        in_specs=[VMEM] * 3,
        out_specs=VMEM,
        out_shape=jax.ShapeDtypeStruct((1, step.shape[0]), jnp.float32),
        compiler_params=pltpu.CompilerParams(vmem_limit_bytes=24 << 20),
        name="vector",
    )(left, right, step.reshape(1, -1))


def join_kernel(lines, unit, plan, *refs):
    chips = lines * COLS
    out_ref = refs[-1]
    z, y, core = place()
    chip = z * COLS + y
    for ref, index, shift, sign, j, mirrored in plan:
        col = lax.rem(chip + sign * shift + chips, chips)
        if 2 * shift == chips:
            low = (chip >= shift).astype(jnp.int32)
            other = core ^ (1 - low) if mirrored else core ^ low
        else:
            other = core ^ j
        value = refs[ref][...] if index is None else refs[ref][index]
        out_ref[:, pl.ds(pl.multiple_of((col * CORES + other) * unit, unit), unit)] = value.T if mirrored else value


def join(arrays, plan, lines, unit, width):
    return pl.pallas_call(
        functools.partial(join_kernel, lines, unit, plan),
        in_specs=[VMEM] * len(arrays),
        out_specs=VMEM,
        out_shape=jax.ShapeDtypeStruct((unit, width), jnp.float32),
        compiler_params=pltpu.CompilerParams(vmem_limit_bytes=24 << 20),
        name="join",
    )(*arrays)


def flat(z, y, core):
    return (z * COLS + y) * CORES + core


def send(x, lines, to):
    pairs = []
    for z in range(lines):
        for y in range(COLS):
            for core in range(CORES):
                target = to(z, y, core)
                if target is not None:
                    pairs.append((flat(z, y, core), flat(*target)))
    return lax.ppermute(x, AXIS, pairs)


def to_core(z, y, core):
    return z, y, 1 - core


def to_col(z, y, core):
    return z, 1 - y, core


def along_line(parts, lines):
    parts = list(parts)
    for r in range(1, lines):
        up = send(parts[lines - r], lines, lambda z, y, c: (z + 1, y, c) if z < r else None)
        down = send(parts[r], lines, lambda z, y, c: (z - 1, y, c) if z >= lines - r else None)
        to_up, to_down = lines - r - 1, (r + 1) % lines
        if to_up == to_down:
            parts[to_up] = parts[to_up] + up + down
        else:
            parts[to_up] = parts[to_up] + up
            parts[to_down] = parts[to_down] + down
    return parts[0]


def mirrored(block, lines, shift, j):
    chips = lines * COLS

    def to(z, y, core):
        chip = z * COLS + y
        flip = int(chip >= shift) if 2 * shift == chips else j
        other = (chip + shift) % chips
        return other // COLS, other % COLS, core ^ flip

    return send(block, lines, to)


def total_of(share, lines):
    share = share + send(share, lines, to_core)
    share = share + send(share, lines, to_col)
    hop = 1
    while hop < lines:
        share = share + send(share, lines, lambda z, y, c: (z ^ hop, y, c))
        hop *= 2
    return share


def halved(slices, slice_mix, lengths, search_step, lines, unit):
    width = slices.shape[2]
    chips = lines * COLS
    left, right = mix(slices, slice_mix, lengths, 2 * unit)
    order = [2, 4, 1, 3, 0]
    parts = {}
    jobs = [(order[0], 1)]
    parts[jobs[0]] = tiles(left, right, jobs, lines, unit)[0]
    jobs = [(k, sy) for k in order for sy in (1, 0)][1:]
    for job, out in zip(jobs, tiles(left, right, jobs, lines, unit)):
        parts[job] = out
    step = total_of(vector(left, right, search_step), lines)
    arrays, plan = [], []
    for k in order:
        q = {}
        for sy in (1, 0):
            own, other = parts[k, sy]
            q[sy] = own + send(other, lines, to_core)
        if k == 4:
            both = [jnp.concatenate([q[1][s : s + 1], q[0][s : s + 1]]) for s in range(lines)]
            done = along_line(both, lines)
            done = done[1] + send(done[0], lines, to_col)
        else:
            came = send(q[1], lines, to_col)
            done = along_line([q[0][s] + came[s] for s in range(lines)], lines)
        for j in range(done.shape[0]):
            plan.append((len(arrays), j, k, 1, j, False))
        arrays.append(done)
        if k:
            for j in range(done.shape[0]):
                plan.append((len(arrays), None, k, -1, j, True))
                arrays.append(mirrored(done[j], lines, k, j))
    return join(arrays, plan, lines, unit, width), step.reshape(-1)


def coupled(slices, slice_mix, lengths):
    count = slices.shape[0]
    coupling = (slice_mix + slice_mix.T) * 0.5 * (1.0 - jnp.eye(count, dtype=jnp.float32))
    blocks = lengths.shape[1]
    position = lax.broadcasted_iota(jnp.int32, (blocks, slices.shape[1] // blocks), 1)
    used = (position < lengths[0][:, None]).reshape(-1).astype(jnp.float32)
    out = []
    for k in range(count):
        total = coupling[k, 0] * slices[0].astype(jnp.float32)
        for l in range(1, count):
            total = total + coupling[k, l] * slices[l].astype(jnp.float32)
        out.append(total)
    return (jnp.stack(out) * used[None, :, None]).astype(jnp.bfloat16)


def whole(slices, slice_mix, lengths, search_step):
    width = slices.shape[2]
    left = slices.reshape(-1, width)
    right = coupled(slices, slice_mix, lengths).reshape(-1, width)
    rows = lax.psum_scatter(
        lax.dot_general(left, right, DIMS0, preferred_element_type=jnp.float32), AXIS, scatter_dimension=0, tiled=True
    )
    applied = jnp.dot(right, search_step, preferred_element_type=jnp.float32)
    head = applied.astype(jnp.bfloat16)
    tail = (applied - head.astype(jnp.float32)).astype(jnp.bfloat16)
    share = lax.dot_general(left, head, DIMS0, preferred_element_type=jnp.float32)
    share = share + lax.dot_general(left, tail, DIMS0, preferred_element_type=jnp.float32)
    return rows, lax.psum(share, AXIS)


def solution(mesh):
    devices = mesh.shape[AXIS]

    def on_device(slices, slice_mix, lengths, search_step):
        unit = slices.shape[2] // devices
        if devices == 16 and unit % 128 == 0:
            return halved(slices, slice_mix, lengths, search_step, devices // (COLS * CORES), unit)
        return whole(slices, slice_mix, lengths, search_step)

    return jax.shard_map(
        on_device,
        mesh=mesh,
        in_specs=(
            P(None, ("groups", AXIS), None),
            P(),
            P(("groups", AXIS), None),
            P("groups"),
        ),
        out_specs=(P(("groups", AXIS), None), P("groups")),
        check_vma=False,
    )
```

time: 239 us -> 186 us (0.78)
  starting transfers between devices: 0.04 us -> 102 us
  waiting for transfers between devices: 109 us -> 48.2 us
  blocking collectives: 38.2 us -> 0 us
  other arithmetic: 38.9 us -> 1.92 us
  matrix products: 32.3 us -> 0 us
  Pallas kernels: 0 us -> 27.7 us
  between operations: 14.1 us -> 1.41 us
    reduce_scatter x1 -> x0, waiting for transfers between devices: 109 us -> none  [on_device(): lax.psum_scatter(lax.dot_general(left, right, (((0,), (0,)), ((), ())), p...]
    ppermute x0 -> x56, starting transfers between devices: none -> 102 us  [send(): return lax.ppermute(x, AXIS, pairs)]
    ppermute x0 -> x56, waiting for transfers between devices: none -> 48.2 us  [send(): return lax.ppermute(x, AXIS, pairs)]
    psum x1 -> x0, blocking collectives: 38.2 us -> none  [on_device(): schur_step = lax.psum(share, 'block')]
    dot_general x4 -> x0, matrix products: 32.3 us -> none  [the longest x1 18.2 us: on_device(): lax.dot_general(left, right, (((0,), (0,)), ((), ())), preferred_element_...]
    pallas_call x0 -> x5, Pallas kernels: none -> 27.7 us  [the longest x2 16.5 us: tiles(): pl.pallas_call(functools.partial(tiles_kernel, lines, unit, jobs), in_spe...]
    add x3 -> x39, other arithmetic: 17.4 us -> 1.89 us  [the longest x2 0.62 us: total_of(): share = share + send(share, lines, lambda z, y, c: (z ^ hop, y, c))]
    convert_element_type x3 -> x0, other arithmetic: 11.8 us -> none  [the longest x1 11 us: mix_slices(): return stacked.astype(jnp.bfloat16)]
  transfers between devices with their start and end apart: 1 -> 56, of which waited for: 1 -> 17; matrix products, arithmetic and copies ran while one was open for 14% -> 1% of each run, Pallas kernels for 0% -> 3%
where the time goes in v1:
time: 186 us
  starting transfers between devices  102 us (55%)
  waiting for transfers between devices  48.2 us (26%)
  Pallas kernels  27.7 us (15%)
  local copies, waits for them, and re-layouts  4.2 us (2%)
  other arithmetic  1.92 us (1%)
    ppermute x56, starting transfers between devices, send(): return lax.ppermute(x, AXIS, pairs)  102 us
    ppermute x56, waiting for transfers between devices, send(): return lax.ppermute(x, AXIS, pairs)  48.2 us
    pallas_call x2, Pallas kernels, tiles(): pl.pallas_call(functools.partial(tiles_kernel, lines, unit, jobs), in_spe...  16.5 us
    pallas_call x1, Pallas kernels, mix(): pl.pallas_call(mix_kernel, grid=(width // tile,), in_specs=[SMEM, SMEM, p...  6.65 us
    unnamed x8, local copies, waits for them, and re-layouts  4.12 us
  transfers between devices with their start and end apart: 56, of which 17 were waited for; matrix products, arithmetic and copies ran while one was open for 1% of the time, Pallas kernels for 3%

profile of v1, /device:TPU:0, one launch (start us, length us, event | category | flops | bytes accessed | tf_op | source)
XLA Modules:
  0.0 185.7 jit_solution(9976927608591254932)
XLA Ops:
  0.6 2.8 %copy-done = bf16[4,384,2048]{2,1,0:T(8,128)(2,1)S(1)} copy-done((bf16[4,384,2048]{2,1,0:T(8,128)(2,1)S(1)}, bf16[4,384,2048]{2,1,0:T(8,128)(2,1)}, u32[]{:S(2)}) %copy-start) | copy-done | bytes 6291480
  4.8 6.7 %mix.1 = (bf16[2048,1536]{1,0:T(8,128)(2,1)S(1)}, bf16[1536,2048]{1,0:T(8,128)(2,1)S(1)}) custom-call(f32[4,4]{1,0:T(4,128)S(1)} %copy-done.1, s32[1,4]{1,0:T(1,128)S(1)} %copy-done.2, bf16[4,384,2048]{2,1,0:T(8,128)(2,1)S(1)} %copy-done), custom_call_target="tpu_custom_call" | custom-call | tf_op jit(solution)/shard_map/mix/pallas_call | solution.py:47
  11.4 14.8 %tiles.2 = (f32[4,2,128,128]{3,2,1,0:T(8,128)S(1)}, f32[4,2,128,128]{3,2,1,0:T(8,128)S(1)}, f32[4,1,128,128]{3,2,1,0:T(8,128)S(1)}, f32[4,1,128,128]{3,2,1,0:T(8...) custom-call(bf16[2048,1536]{1,0:T(8,128)(2,1)S(1)} %get-tuple-elemen, ...), custom_call_target="tpu_custom_call" | custom-call | flops 7247757312 | tf_op jit(solution)/shard_map/tiles/pallas_call | solution.py:104
  26.9 3.4 %vector.1 = f32[1,2048]{1,0:T(1,128)S(1)} custom-call(bf16[2048,1536]{1,0:T(8,128)(2,1)S(1)} %get-tuple-element.24.left_ref, bf16[1536,2048]{1,0:T(8,128)(2,1)S(1)} %get-tuple-element.25.right_ref, bf16[1,2048]{1,0:T(2,128)(2,1)S(1)} %reshape.26.step_ref), custom_call_target="tpu_custom_call" | custom-call | tf_op jit(solution)/shard_map/vector/pallas_call | solution.py:129
  31.5 3.0 %collective-permute-start.53 = (f32[1,2048]{1,0:T(1,128)S(1)}, f32[1,2048]{1,0:T(1,128)S(1)}, u32[]{:S(2)}, u32[]{:S(2)}) collective-permute-start(f32[1,2048]{1,0:T(1,128)S(1)} %add.304), channel_id=1, source_target_pairs={{0,2},{1,3},{2,0},{3,1},{4,6},{5,7},{6,4},{7,5},{8,10},{9,11},{10,... | collective-permute-start | bytes 24584 | tf_op jit(solution)/shard_map/ppermute | solution.py:178
  36.1 2.1 %collective-permute-start.54 = (f32[1,2048]{1,0:T(1,128)S(1)}, f32[1,2048]{1,0:T(1,128)S(1)}, u32[]{:S(2)}, u32[]{:S(2)}) collective-permute-start(f32[1,2048]{1,0:T(1,128)S(1)} %add.305), channel_id=1, source_target_pairs={{0,4},{1,5},{2,6},{3,7},{4,0},{5,1},{6,2},{7,3},{8,12},{9,13},{10,... | collective-permute-start | bytes 24584 | tf_op jit(solution)/shard_map/ppermute | solution.py:178
  38.3 2.0 %collective-permute-start.13 = (f32[2,1,128,128]{3,2,1,0:T(8,128)S(1)}, f32[2,1,128,128]{3,2,1,0:T(8,128)S(1)}, u32[]{:S(2)}, u32[]{:S(2)}) collective-permute-start(f32[2,1,128,128]{3,2,1,0:T(8,128)S(1)} %pad_maximum_fusion.1), channel_id=1, source_target_pairs={{0,4},{1,5},{2,6},{3,7},{16,20},{17,21},{18,22},{19,23}} | collective-permute-start | bytes 393224 | tf_op jit(solution)/shard_map/ppermute | solution.py:178
  41.0 2.7 %collective-permute-done.13 = f32[2,1,128,128]{3,2,1,0:T(8,128)S(1)} collective-permute-done((f32[2,1,128,128]{3,2,1,0:T(8,128)S(1)}, f32[2,1,128,128]{3,2,1,0:T(8,128)S(1)}, u32[]{:S(2)}, u32[]{:S(2)}) %collective-permute-start.13) | collective-permute-done | bytes 131104 | tf_op jit(solution)/shard_map/ppermute | solution.py:178
  44.3 4.6 %collective-permute-start.15 = (f32[2,1,128,128]{3,2,1,0:T(8,128)S(1)}, f32[2,1,128,128]{3,2,1,0:T(8,128)S(1)}, u32[]{:S(2)}, u32[]{:S(2)}) collective-permute-start(f32[2,1,128,128]{3,2,1,0:T(8,128)S(1)} %fusion.33), channel_id=1, source_target_pairs={{0,4},{1,5},{2,6},{3,7},{4,8},{5,9},{6,10},{7,11},{16,20},{17,21},... | collective-permute-start | bytes 393224 | tf_op jit(solution)/shard_map/ppermute | solution.py:178
  52.5 8.6 %collective-permute-start.16 = (f32[2,1,128,128]{3,2,1,0:T(8,128)S(1)}, f32[2,1,128,128]{3,2,1,0:T(8,128)S(1)}, u32[]{:S(2)}, u32[]{:S(2)}) collective-permute-start(f32[2,1,128,128]{3,2,1,0:T(8,128)S(1)} %fusion.36), channel_id=1, source_target_pairs={{0,4},{1,5},{2,6},{3,7},{4,8},{5,9},{6,10},{7,11},{8,12},{9,13},{1... | collective-permute-start | bytes 393224 | tf_op jit(solution)/shard_map/ppermute | solution.py:178
  62.5 1.7 collective-permute-start.45
  70.4 7.0 %collective-permute-done.45 = f32[4,2,128,128]{3,2,1,0:T(8,128)S(1)} collective-permute-done((f32[4,2,128,128]{3,2,1,0:T(8,128)S(1)}, f32[4,2,128,128]{3,2,1,0:T(8,128)S(1)}, u32[]{:S(2)}, u32[]{:S(2)}) %collective-permute-start.45) | collective-permute-done | bytes 524320 | tf_op jit(solution)/shard_map/ppermute | solution.py:178
  77.4 4.6 %collective-permute-start.46 = (f32[2,128,128]{2,1,0:T(8,128)S(1)}, f32[2,128,128]{2,1,0:T(8,128)S(1)}, u32[]{:S(2)}, u32[]{:S(2)}) collective-permute-start(f32[2,128,128]{2,1,0:T(8,128)S(1)} %get-tuple-element.47), channel_id=1, source_target_pairs={{0,4},{1,5},{2,6},{3,7},{16,20},{17,21},{18,22},{19,23}} | collective-permute-start | bytes 393224 | tf_op jit(solution)/shard_map/ppermute | solution.py:178
  82.0 6.6 %collective-permute-done.34 = f32[4,2,128,128]{3,2,1,0:T(8,128)S(1)} collective-permute-done((f32[4,2,128,128]{3,2,1,0:T(8,128)S(1)}, f32[4,2,128,128]{3,2,1,0:T(8,128)S(1)}, u32[]{:S(2)}, u32[]{:S(2)}) %collective-permute-start.34) | collective-permute-done | bytes 524320 | tf_op jit(solution)/shard_map/ppermute | solution.py:178
  89.3 10.5 %collective-permute-done.23 = f32[4,2,128,128]{3,2,1,0:T(8,128)S(1)} collective-permute-done((f32[4,2,128,128]{3,2,1,0:T(8,128)S(1)}, f32[4,2,128,128]{3,2,1,0:T(8,128)S(1)}, u32[]{:S(2)}, u32[]{:S(2)}) %collective-permute-start.23) | collective-permute-done | bytes 524320 | tf_op jit(solution)/shard_map/ppermute | solution.py:178
  99.8 4.6 %collective-permute-start.35 = (f32[2,128,128]{2,1,0:T(8,128)S(1)}, f32[2,128,128]{2,1,0:T(8,128)S(1)}, u32[]{:S(2)}, u32[]{:S(2)}) collective-permute-start(f32[2,128,128]{2,1,0:T(8,128)S(1)} %get-tuple-element.49), channel_id=1, source_target_pairs={{0,4},{1,5},{2,6},{3,7},{16,20},{17,21},{18,22},{19,23}} | collective-permute-start | bytes 393224 | tf_op jit(solution)/shard_map/ppermute | solution.py:178
  104.5 6.6 %collective-permute-done.2 = f32[4,2,128,128]{3,2,1,0:T(8,128)S(1)} collective-permute-done((f32[4,2,128,128]{3,2,1,0:T(8,128)S(1)}, f32[4,2,128,128]{3,2,1,0:T(8,128)S(1)}, u32[]{:S(2)}, u32[]{:S(2)}) %collective-permute-start.2) | collective-permute-done | bytes 524320 | tf_op jit(solution)/shard_map/ppermute | solution.py:178
  111.8 4.3 %collective-permute-start.24 = (f32[2,128,128]{2,1,0:T(8,128)S(1)}, f32[2,128,128]{2,1,0:T(8,128)S(1)}, u32[]{:S(2)}, u32[]{:S(2)}) collective-permute-start(f32[2,128,128]{2,1,0:T(8,128)S(1)} %get-tuple-element.51), channel_id=1, source_target_pairs={{0,4},{1,5},{2,6},{3,7},{16,20},{17,21},{18,22},{19,23}} | collective-permute-start | bytes 393224 | tf_op jit(solution)/shard_map/ppermute | solution.py:178
  119.4 4.4 %collective-permute-start.48 = (f32[2,128,128]{2,1,0:T(8,128)S(1)}, f32[2,128,128]{2,1,0:T(8,128)S(1)}, u32[]{:S(2)}, u32[]{:S(2)}) collective-permute-start(f32[2,128,128]{2,1,0:T(8,128)S(1)} %fusion.3), channel_id=1, source_target_pairs={{0,4},{1,5},{2,6},{3,7},{4,8},{5,9},{6,10},{7,11},{16,20},{17,21},... | collective-permute-start | bytes 393224 | tf_op jit(solution)/shard_map/ppermute | solution.py:178
  123.8 3.1 %collective-permute-start.37 = (f32[2,128,128]{2,1,0:T(8,128)S(1)}, f32[2,128,128]{2,1,0:T(8,128)S(1)}, u32[]{:S(2)}, u32[]{:S(2)}) collective-permute-start(f32[2,128,128]{2,1,0:T(8,128)S(1)} %fusion.11), channel_id=1, source_target_pairs={{0,4},{1,5},{2,6},{3,7},{4,8},{5,9},{6,10},{7,11},{16,20},{17,21},... | collective-permute-start | bytes 393224 | tf_op jit(solution)/shard_map/ppermute | solution.py:178
  130.0 4.4 %collective-permute-start.26 = (f32[2,128,128]{2,1,0:T(8,128)S(1)}, f32[2,128,128]{2,1,0:T(8,128)S(1)}, u32[]{:S(2)}, u32[]{:S(2)}) collective-permute-start(f32[2,128,128]{2,1,0:T(8,128)S(1)} %fusion.19), channel_id=1, source_target_pairs={{0,4},{1,5},{2,6},{3,7},{4,8},{5,9},{6,10},{7,11},{16,20},{17,21},... | collective-permute-start | bytes 393224 | tf_op jit(solution)/shard_map/ppermute | solution.py:178
  135.2 3.9 %collective-permute-start.5 = (f32[2,128,128]{2,1,0:T(8,128)S(1)}, f32[2,128,128]{2,1,0:T(8,128)S(1)}, u32[]{:S(2)}, u32[]{:S(2)}) collective-permute-start(f32[2,128,128]{2,1,0:T(8,128)S(1)} %fusion.27), channel_id=1, source_target_pairs={{0,4},{1,5},{2,6},{3,7},{4,8},{5,9},{6,10},{7,11},{16,20},{17,21},... | collective-permute-start | bytes 393224 | tf_op jit(solution)/shard_map/ppermute | solution.py:178
  139.7 5.2 %collective-permute-start.38 = (f32[2,128,128]{2,1,0:T(8,128)S(1)}, f32[2,128,128]{2,1,0:T(8,128)S(1)}, u32[]{:S(2)}, u32[]{:S(2)}) collective-permute-start(f32[2,128,128]{2,1,0:T(8,128)S(1)} %add.284), channel_id=1, source_target_pairs={{0,4},{1,5},{2,6},{3,7},{4,8},{5,9},{6,10},{7,11},{8,12},{9,13},{1... | collective-permute-start | bytes 393224 | tf_op jit(solution)/shard_map/ppermute | solution.py:178
  146.3 4.8 %collective-permute-start.20 = (f32[128,128]{1,0:T(8,128)S(1)}, f32[128,128]{1,0:T(8,128)S(1)}, u32[]{:S(2)}, u32[]{:S(2)}) collective-permute-start(f32[128,128]{1,0:T(8,128)S(1)} %bitcast.84), channel_id=1, source_target_pairs={{0,8},{1,9},{2,10},{3,11},{4,12},{5,13},{6,14},{7,15},{8,1},{9,0},... | collective-permute-start | bytes 196616 | tf_op jit(solution)/shard_map/ppermute | solution.py:178
  151.1 1.9 %collective-permute-start.49 = (f32[2,128,128]{2,1,0:T(8,128)S(1)}, f32[2,128,128]{2,1,0:T(8,128)S(1)}, u32[]{:S(2)}, u32[]{:S(2)}) collective-permute-start(f32[2,128,128]{2,1,0:T(8,128)S(1)} %add.300), channel_id=1, source_target_pairs={{0,4},{1,5},{2,6},{3,7},{4,8},{5,9},{6,10},{7,11},{8,12},{9,13},{1... | collective-permute-start | bytes 393224 | tf_op jit(solution)/shard_map/ppermute | solution.py:178
  154.4 4.6 %collective-permute-start.27 = (f32[2,128,128]{2,1,0:T(8,128)S(1)}, f32[2,128,128]{2,1,0:T(8,128)S(1)}, u32[]{:S(2)}, u32[]{:S(2)}) collective-permute-start(f32[2,128,128]{2,1,0:T(8,128)S(1)} %add.268), channel_id=1, source_target_pairs={{0,4},{1,5},{2,6},{3,7},{4,8},{5,9},{6,10},{7,11},{8,12},{9,13},{1... | collective-permute-start | bytes 393224 | tf_op jit(solution)/shard_map/ppermute | solution.py:178
  161.5 4.3 %collective-permute-start.6 = (f32[2,128,128]{2,1,0:T(8,128)S(1)}, f32[2,128,128]{2,1,0:T(8,128)S(1)}, u32[]{:S(2)}, u32[]{:S(2)}) collective-permute-start(f32[2,128,128]{2,1,0:T(8,128)S(1)} %add.243), channel_id=1, source_target_pairs={{0,4},{1,5},{2,6},{3,7},{4,8},{5,9},{6,10},{7,11},{8,12},{9,13},{1... | collective-permute-start | bytes 393224 | tf_op jit(solution)/shard_map/ppermute | solution.py:178
  168.3 3.5 %collective-permute-start.41 = (f32[128,128]{1,0:T(8,128)S(1)}, f32[128,128]{1,0:T(8,128)S(1)}, u32[]{:S(2)}, u32[]{:S(2)}) collective-permute-start(f32[128,128]{1,0:T(8,128)S(1)} %get-tuple-element.63), channel_id=1, source_target_pairs={{0,6},{1,7},{2,8},{3,9},{4,10},{5,11},{6,12},{7,13},{8,14},{9,15},... | collective-permute-start | bytes 196616 | tf_op jit(solution)/shard_map/ppermute | solution.py:178
  172.8 2.3 %collective-permute-start.30 = (f32[128,128]{1,0:T(8,128)S(1)}, f32[128,128]{1,0:T(8,128)S(1)}, u32[]{:S(2)}, u32[]{:S(2)}) collective-permute-start(f32[128,128]{1,0:T(8,128)S(1)} %get-tuple-element.65), channel_id=1, source_target_pairs={{0,2},{1,3},{2,4},{3,5},{4,6},{5,7},{6,8},{7,9},{8,10},{9,11},{10,... | collective-permute-start | bytes 196616 | tf_op jit(solution)/shard_map/ppermute | solution.py:178
  175.1 2.6 %collective-permute-start.31 = (f32[128,128]{1,0:T(8,128)S(1)}, f32[128,128]{1,0:T(8,128)S(1)}, u32[]{:S(2)}, u32[]{:S(2)}) collective-permute-start(f32[128,128]{1,0:T(8,128)S(1)} %get-tuple-element.64), channel_id=1, source_target_pairs={{0,3},{1,2},{2,5},{3,4},{4,7},{5,6},{6,9},{7,8},{8,11},{9,10},{10,... | collective-permute-start | bytes 196616 | tf_op jit(solution)/shard_map/ppermute | solution.py:178
  177.8 2.5 %collective-permute-done.42.refs_10_ = f32[128,128]{1,0:T(8,128)S(1)} collective-permute-done((f32[128,128]{1,0:T(8,128)S(1)}, f32[128,128]{1,0:T(8,128)S(1)}, u32[]{:S(2)}, u32[]{:S(2)}) %collective-permute-start.42) | collective-permute-done | bytes 65568 | tf_op jit(solution)/shard_map/ppermute | solution.py:178
  180.3 2.4 %collective-permute-done.31.refs_7_ = f32[128,128]{1,0:T(8,128)S(1)} collective-permute-done((f32[128,128]{1,0:T(8,128)S(1)}, f32[128,128]{1,0:T(8,128)S(1)}, u32[]{:S(2)}, u32[]{:S(2)}) %collective-permute-start.31) | collective-permute-done | bytes 65568 | tf_op jit(solution)/shard_map/ppermute | solution.py:178
  (141 shorter events, 38.3 us)
Async XLA Ops:
  26.2 9.9 %collective-permute-start.11 = (f32[4,1,128,128]{3,2,1,0:T(8,128)S(1)}, f32[4,1,128,128]{3,2,1,0:T(8,128)S(1)}, u32[]{:S(2)}, u32[]{:S(2)}) collective-permute-start(f32[4,1,128,128]{3,2,1,0:T(8,128)S(1)} %get-tuple-element.31), channel_id=1, source_target_pairs={{0,1},{1,0},{2,3},{3,2},{4,5},{5,4},{6,7},{7,6},{8,9},{9,8},{10,11... | collective-permute-start | bytes 786440 | tf_op jit(solution)/shard_map/ppermute | solution.py:178
  26.8 11.5 %collective-permute-start.12 = (f32[4,1,128,128]{3,2,1,0:T(8,128)S(1)}, f32[4,1,128,128]{3,2,1,0:T(8,128)S(1)}, u32[]{:S(2)}, u32[]{:S(2)}) collective-permute-start(f32[4,1,128,128]{3,2,1,0:T(8,128)S(1)} %get-tuple-element.33), channel_id=1, source_target_pairs={{0,1},{1,0},{2,3},{3,2},{4,5},{5,4},{6,7},{7,6},{8,9},{9,8},{10,11... | collective-permute-start | bytes 786440 | tf_op jit(solution)/shard_map/ppermute | solution.py:178
  34.5 15.0 %collective-permute-start.43 = (f32[4,2,128,128]{3,2,1,0:T(8,128)S(1)}, f32[4,2,128,128]{3,2,1,0:T(8,128)S(1)}, u32[]{:S(2)}, u32[]{:S(2)}) collective-permute-start(f32[4,2,128,128]{3,2,1,0:T(8,128)S(1)} %get-tuple-element.43), channel_id=1, source_target_pairs={{0,1},{1,0},{2,3},{3,2},{4,5},{5,4},{6,7},{7,6},{8,9},{9,8},{10,11... | collective-permute-start | bytes 1572872 | tf_op jit(solution)/shard_map/ppermute | solution.py:178
  34.5 15.1 %collective-permute-start.44 = (f32[4,2,128,128]{3,2,1,0:T(8,128)S(1)}, f32[4,2,128,128]{3,2,1,0:T(8,128)S(1)}, u32[]{:S(2)}, u32[]{:S(2)}) collective-permute-start(f32[4,2,128,128]{3,2,1,0:T(8,128)S(1)} %get-tuple-element.45), channel_id=1, source_target_pairs={{0,1},{1,0},{2,3},{3,2},{4,5},{5,4},{6,7},{7,6},{8,9},{9,8},{10,11... | collective-permute-start | bytes 1572872 | tf_op jit(solution)/shard_map/ppermute | solution.py:178
  36.1 15.7 %collective-permute-start.32 = (f32[4,2,128,128]{3,2,1,0:T(8,128)S(1)}, f32[4,2,128,128]{3,2,1,0:T(8,128)S(1)}, u32[]{:S(2)}, u32[]{:S(2)}) collective-permute-start(f32[4,2,128,128]{3,2,1,0:T(8,128)S(1)} %get-tuple-element.39), channel_id=1, source_target_pairs={{0,1},{1,0},{2,3},{3,2},{4,5},{5,4},{6,7},{7,6},{8,9},{9,8},{10,11... | collective-permute-start | bytes 1572872 | tf_op jit(solution)/shard_map/ppermute | solution.py:178
  49.6 11.5 %collective-permute-start.21 = (f32[4,2,128,128]{3,2,1,0:T(8,128)S(1)}, f32[4,2,128,128]{3,2,1,0:T(8,128)S(1)}, u32[]{:S(2)}, u32[]{:S(2)}) collective-permute-start(f32[4,2,128,128]{3,2,1,0:T(8,128)S(1)} %get-tuple-element.35), channel_id=1, source_target_pairs={{0,1},{1,0},{2,3},{3,2},{4,5},{5,4},{6,7},{7,6},{8,9},{9,8},{10,11... | collective-permute-start | bytes 1572872 | tf_op jit(solution)/shard_map/ppermute | solution.py:178
  51.8 10.7 %collective-permute-start.22 = (f32[4,2,128,128]{3,2,1,0:T(8,128)S(1)}, f32[4,2,128,128]{3,2,1,0:T(8,128)S(1)}, u32[]{:S(2)}, u32[]{:S(2)}) collective-permute-start(f32[4,2,128,128]{3,2,1,0:T(8,128)S(1)} %get-tuple-element.37), channel_id=1, source_target_pairs={{0,1},{1,0},{2,3},{3,2},{4,5},{5,4},{6,7},{7,6},{8,9},{9,8},{10,11... | collective-permute-start | bytes 1572872 | tf_op jit(solution)/shard_map/ppermute | solution.py:178
  52.0 13.2 %collective-permute-start = (f32[4,2,128,128]{3,2,1,0:T(8,128)S(1)}, f32[4,2,128,128]{3,2,1,0:T(8,128)S(1)}, u32[]{:S(2)}, u32[]{:S(2)}) collective-permute-start(f32[4,2,128,128]{3,2,1,0:T(8,128)S(1)} %get-tuple-element.27), channel_id=1, source_target_pairs={{0,1},{1,0},{2,3},{3,2},{4,5},{5,4},{6,7},{7,6},{8,9},{9,8},{10,11... | collective-permute-start | bytes 1572872 | tf_op jit(solution)/shard_map/ppermute | solution.py:178
  52.4 13.3 %collective-permute-start.1 = (f32[4,2,128,128]{3,2,1,0:T(8,128)S(1)}, f32[4,2,128,128]{3,2,1,0:T(8,128)S(1)}, u32[]{:S(2)}, u32[]{:S(2)}) collective-permute-start(f32[4,2,128,128]{3,2,1,0:T(8,128)S(1)} %get-tuple-element.29), channel_id=1, source_target_pairs={{0,1},{1,0},{2,3},{3,2},{4,5},{5,4},{6,7},{7,6},{8,9},{9,8},{10,11... | collective-permute-start | bytes 1572872 | tf_op jit(solution)/shard_map/ppermute | solution.py:178
  52.5 14.9 %collective-permute-start.16 = (f32[2,1,128,128]{3,2,1,0:T(8,128)S(1)}, f32[2,1,128,128]{3,2,1,0:T(8,128)S(1)}, u32[]{:S(2)}, u32[]{:S(2)}) collective-permute-start(f32[2,1,128,128]{3,2,1,0:T(8,128)S(1)} %fusion.36), channel_id=1, source_target_pairs={{0,4},{1,5},{2,6},{3,7},{4,8},{5,9},{6,10},{7,11},{8,12},{9,13},{1... | collective-permute-start | bytes 393224 | tf_op jit(solution)/shard_map/ppermute | solution.py:178
  62.5 14.8 %collective-permute-start.45 = (f32[4,2,128,128]{3,2,1,0:T(8,128)S(1)}, f32[4,2,128,128]{3,2,1,0:T(8,128)S(1)}, u32[]{:S(2)}, u32[]{:S(2)}) collective-permute-start(f32[4,2,128,128]{3,2,1,0:T(8,128)S(1)} %add.289), channel_id=1, source_target_pairs={{0,2},{1,3},{2,0},{3,1},{4,6},{5,7},{6,4},{7,5},{8,10},{9,11},{10,... | collective-permute-start | bytes 1572872 | tf_op jit(solution)/shard_map/ppermute | solution.py:178
  65.2 23.4 %collective-permute-start.34 = (f32[4,2,128,128]{3,2,1,0:T(8,128)S(1)}, f32[4,2,128,128]{3,2,1,0:T(8,128)S(1)}, u32[]{:S(2)}, u32[]{:S(2)}) collective-permute-start(f32[4,2,128,128]{3,2,1,0:T(8,128)S(1)} %add.273), channel_id=1, source_target_pairs={{0,2},{1,3},{2,0},{3,1},{4,6},{5,7},{6,4},{7,5},{8,10},{9,11},{10,... | collective-permute-start | bytes 1572872 | tf_op jit(solution)/shard_map/ppermute | solution.py:178
  65.7 34.1 %collective-permute-start.23 = (f32[4,2,128,128]{3,2,1,0:T(8,128)S(1)}, f32[4,2,128,128]{3,2,1,0:T(8,128)S(1)}, u32[]{:S(2)}, u32[]{:S(2)}) collective-permute-start(f32[4,2,128,128]{3,2,1,0:T(8,128)S(1)} %add.257), channel_id=1, source_target_pairs={{0,2},{1,3},{2,0},{3,1},{4,6},{5,7},{6,4},{7,5},{8,10},{9,11},{10,... | collective-permute-start | bytes 1572872 | tf_op jit(solution)/shard_map/ppermute | solution.py:178
  67.4 43.6 %collective-permute-start.2 = (f32[4,2,128,128]{3,2,1,0:T(8,128)S(1)}, f32[4,2,128,128]{3,2,1,0:T(8,128)S(1)}, u32[]{:S(2)}, u32[]{:S(2)}) collective-permute-start(f32[4,2,128,128]{3,2,1,0:T(8,128)S(1)} %add.232), channel_id=1, source_target_pairs={{0,2},{1,3},{2,0},{3,1},{4,6},{5,7},{6,4},{7,5},{8,10},{9,11},{10,... | collective-permute-start | bytes 1572872 | tf_op jit(solution)/shard_map/ppermute | solution.py:178
  68.7 66.4 %collective-permute-start.19 = (f32[1,128,128]{2,1,0:T(8,128)S(1)}, f32[1,128,128]{2,1,0:T(8,128)S(1)}, u32[]{:S(2)}, u32[]{:S(2)}) collective-permute-start(f32[1,128,128]{2,1,0:T(8,128)S(1)} %slice_bitcast_fusion.4), channel_id=1, source_target_pairs={{0,2},{1,3},{2,0},{3,1},{4,6},{5,7},{6,4},{7,5},{8,10},{9,11},{10,... | collective-permute-start | bytes 196616 | tf_op jit(solution)/shard_map/ppermute | solution.py:178
  77.4 34.4 %collective-permute-start.46 = (f32[2,128,128]{2,1,0:T(8,128)S(1)}, f32[2,128,128]{2,1,0:T(8,128)S(1)}, u32[]{:S(2)}, u32[]{:S(2)}) collective-permute-start(f32[2,128,128]{2,1,0:T(8,128)S(1)} %get-tuple-element.47), channel_id=1, source_target_pairs={{0,4},{1,5},{2,6},{3,7},{16,20},{17,21},{18,22},{19,23}} | collective-permute-start | bytes 393224 | tf_op jit(solution)/shard_map/ppermute | solution.py:178
  88.6 27.5 %collective-permute-start.47 = (f32[2,128,128]{2,1,0:T(8,128)S(1)}, f32[2,128,128]{2,1,0:T(8,128)S(1)}, u32[]{:S(2)}, u32[]{:S(2)}) collective-permute-start(f32[2,128,128]{2,1,0:T(8,128)S(1)} %get-tuple-element.46), channel_id=1, source_target_pairs={{12,8},{13,9},{14,10},{15,11},{28,24},{29,25},{30,26},{31,27}} | collective-permute-start | bytes 393224 | tf_op jit(solution)/shard_map/ppermute | solution.py:178
  99.8 17.0 %collective-permute-start.35 = (f32[2,128,128]{2,1,0:T(8,128)S(1)}, f32[2,128,128]{2,1,0:T(8,128)S(1)}, u32[]{:S(2)}, u32[]{:S(2)}) collective-permute-start(f32[2,128,128]{2,1,0:T(8,128)S(1)} %get-tuple-element.49), channel_id=1, source_target_pairs={{0,4},{1,5},{2,6},{3,7},{16,20},{17,21},{18,22},{19,23}} | collective-permute-start | bytes 393224 | tf_op jit(solution)/shard_map/ppermute | solution.py:178
  116.8 10.2 %collective-permute-start.3 = (f32[2,128,128]{2,1,0:T(8,128)S(1)}, f32[2,128,128]{2,1,0:T(8,128)S(1)}, u32[]{:S(2)}, u32[]{:S(2)}) collective-permute-start(f32[2,128,128]{2,1,0:T(8,128)S(1)} %get-tuple-element.53), channel_id=1, source_target_pairs={{0,4},{1,5},{2,6},{3,7},{16,20},{17,21},{18,22},{19,23}} | collective-permute-start | bytes 393224 | tf_op jit(solution)/shard_map/ppermute | solution.py:178
  118.1 9.5 %collective-permute-start.4 = (f32[2,128,128]{2,1,0:T(8,128)S(1)}, f32[2,128,128]{2,1,0:T(8,128)S(1)}, u32[]{:S(2)}, u32[]{:S(2)}) collective-permute-start(f32[2,128,128]{2,1,0:T(8,128)S(1)} %get-tuple-element.52), channel_id=1, source_target_pairs={{12,8},{13,9},{14,10},{15,11},{28,24},{29,25},{30,26},{31,27}} | collective-permute-start | bytes 393224 | tf_op jit(solution)/shard_map/ppermute | solution.py:178
  119.4 19.6 %collective-permute-start.48 = (f32[2,128,128]{2,1,0:T(8,128)S(1)}, f32[2,128,128]{2,1,0:T(8,128)S(1)}, u32[]{:S(2)}, u32[]{:S(2)}) collective-permute-start(f32[2,128,128]{2,1,0:T(8,128)S(1)} %fusion.3), channel_id=1, source_target_pairs={{0,4},{1,5},{2,6},{3,7},{4,8},{5,9},{6,10},{7,11},{16,20},{17,21},... | collective-permute-start | bytes 393224 | tf_op jit(solution)/shard_map/ppermute | solution.py:178
  127.0 12.7 %collective-permute-start.50 = (f32[2,128,128]{2,1,0:T(8,128)S(1)}, f32[2,128,128]{2,1,0:T(8,128)S(1)}, u32[]{:S(2)}, u32[]{:S(2)}) collective-permute-start(f32[2,128,128]{2,1,0:T(8,128)S(1)} %fusion.3), channel_id=1, source_target_pairs={{8,4},{9,5},{10,6},{11,7},{12,8},{13,9},{14,10},{15,11},{24,20},{2... | collective-permute-start | bytes 393224 | tf_op jit(solution)/shard_map/ppermute | solution.py:178
  130.0 14.9 %collective-permute-start.26 = (f32[2,128,128]{2,1,0:T(8,128)S(1)}, f32[2,128,128]{2,1,0:T(8,128)S(1)}, u32[]{:S(2)}, u32[]{:S(2)}) collective-permute-start(f32[2,128,128]{2,1,0:T(8,128)S(1)} %fusion.19), channel_id=1, source_target_pairs={{0,4},{1,5},{2,6},{3,7},{4,8},{5,9},{6,10},{7,11},{16,20},{17,21},... | collective-permute-start | bytes 393224 | tf_op jit(solution)/shard_map/ppermute | solution.py:178
  134.4 11.9 %collective-permute-start.28 = (f32[2,128,128]{2,1,0:T(8,128)S(1)}, f32[2,128,128]{2,1,0:T(8,128)S(1)}, u32[]{:S(2)}, u32[]{:S(2)}) collective-permute-start(f32[2,128,128]{2,1,0:T(8,128)S(1)} %fusion.19), channel_id=1, source_target_pairs={{8,4},{9,5},{10,6},{11,7},{12,8},{13,9},{14,10},{15,11},{24,20},{2... | collective-permute-start | bytes 393224 | tf_op jit(solution)/shard_map/ppermute | solution.py:178
  135.2 15.9 %collective-permute-start.5 = (f32[2,128,128]{2,1,0:T(8,128)S(1)}, f32[2,128,128]{2,1,0:T(8,128)S(1)}, u32[]{:S(2)}, u32[]{:S(2)}) collective-permute-start(f32[2,128,128]{2,1,0:T(8,128)S(1)} %fusion.27), channel_id=1, source_target_pairs={{0,4},{1,5},{2,6},{3,7},{4,8},{5,9},{6,10},{7,11},{16,20},{17,21},... | collective-permute-start | bytes 393224 | tf_op jit(solution)/shard_map/ppermute | solution.py:178
  139.0 14.0 %collective-permute-start.7 = (f32[2,128,128]{2,1,0:T(8,128)S(1)}, f32[2,128,128]{2,1,0:T(8,128)S(1)}, u32[]{:S(2)}, u32[]{:S(2)}) collective-permute-start(f32[2,128,128]{2,1,0:T(8,128)S(1)} %fusion.27), channel_id=1, source_target_pairs={{8,4},{9,5},{10,6},{11,7},{12,8},{13,9},{14,10},{15,11},{24,20},{2... | collective-permute-start | bytes 393224 | tf_op jit(solution)/shard_map/ppermute | solution.py:178
  139.7 14.7 %collective-permute-start.38 = (f32[2,128,128]{2,1,0:T(8,128)S(1)}, f32[2,128,128]{2,1,0:T(8,128)S(1)}, u32[]{:S(2)}, u32[]{:S(2)}) collective-permute-start(f32[2,128,128]{2,1,0:T(8,128)S(1)} %add.284), channel_id=1, source_target_pairs={{0,4},{1,5},{2,6},{3,7},{4,8},{5,9},{6,10},{7,11},{8,12},{9,13},{1... | collective-permute-start | bytes 393224 | tf_op jit(solution)/shard_map/ppermute | solution.py:178
  144.9 14.1 %collective-permute-start.40 = (f32[2,128,128]{2,1,0:T(8,128)S(1)}, f32[2,128,128]{2,1,0:T(8,128)S(1)}, u32[]{:S(2)}, u32[]{:S(2)}) collective-permute-start(f32[2,128,128]{2,1,0:T(8,128)S(1)} %add.286), channel_id=1, source_target_pairs={{4,0},{5,1},{6,2},{7,3},{8,4},{9,5},{10,6},{11,7},{12,8},{13,9},{1... | collective-permute-start | bytes 393224 | tf_op jit(solution)/shard_map/ppermute | solution.py:178
  146.3 26.5 %collective-permute-start.20 = (f32[128,128]{1,0:T(8,128)S(1)}, f32[128,128]{1,0:T(8,128)S(1)}, u32[]{:S(2)}, u32[]{:S(2)}) collective-permute-start(f32[128,128]{1,0:T(8,128)S(1)} %bitcast.84), channel_id=1, source_target_pairs={{0,8},{1,9},{2,10},{3,11},{4,12},{5,13},{6,14},{7,15},{8,1},{9,0},... | collective-permute-start | bytes 196616 | tf_op jit(solution)/shard_map/ppermute | solution.py:178
  151.1 24.0 %collective-permute-start.49 = (f32[2,128,128]{2,1,0:T(8,128)S(1)}, f32[2,128,128]{2,1,0:T(8,128)S(1)}, u32[]{:S(2)}, u32[]{:S(2)}) collective-permute-start(f32[2,128,128]{2,1,0:T(8,128)S(1)} %add.300), channel_id=1, source_target_pairs={{0,4},{1,5},{2,6},{3,7},{4,8},{5,9},{6,10},{7,11},{8,12},{9,13},{1... | collective-permute-start | bytes 393224 | tf_op jit(solution)/shard_map/ppermute | solution.py:178
  153.1 24.7 %collective-permute-start.51 = (f32[2,128,128]{2,1,0:T(8,128)S(1)}, f32[2,128,128]{2,1,0:T(8,128)S(1)}, u32[]{:S(2)}, u32[]{:S(2)}) collective-permute-start(f32[2,128,128]{2,1,0:T(8,128)S(1)} %add.302), channel_id=1, source_target_pairs={{4,0},{5,1},{6,2},{7,3},{8,4},{9,5},{10,6},{11,7},{12,8},{13,9},{1... | collective-permute-start | bytes 393224 | tf_op jit(solution)/shard_map/ppermute | solution.py:178
  168.3 9.4 %collective-permute-start.41 = (f32[128,128]{1,0:T(8,128)S(1)}, f32[128,128]{1,0:T(8,128)S(1)}, u32[]{:S(2)}, u32[]{:S(2)}) collective-permute-start(f32[128,128]{1,0:T(8,128)S(1)} %get-tuple-element.63), channel_id=1, source_target_pairs={{0,6},{1,7},{2,8},{3,9},{4,10},{5,11},{6,12},{7,13},{8,14},{9,15},... | collective-permute-start | bytes 196616 | tf_op jit(solution)/shard_map/ppermute | solution.py:178
  (28 other events, 164.4 us)

commit v2 on v0

v2 whole, which is shorter than its diff:
```python
import functools

import jax
import jax.numpy as jnp
from jax import lax
from jax.experimental import pallas as pl
from jax.experimental.pallas import tpu as pltpu
from jax.sharding import PartitionSpec as P

AXIS = "block"
CORES = 2
TILE = 16
LANES = 128
DIMS0 = (((0,), (0,)), ((), ()))
DIMS1 = (((1,), (1,)), ((), ()))
VMEM = pl.BlockSpec(memory_space=pltpu.VMEM)
HBM = pl.BlockSpec(memory_space=pltpu.HBM)
ANY = pl.BlockSpec(memory_space=pl.ANY)

PIECES = {
    "a": ((1, 2), (1, 2, 4)),
    "b": ((3, 4), (2, 1, 4)),
    "c": ((0,), (1, 2, 4)),
}
FIRST, CARRIER = "a", "b"
ORDER = "Ka Kb a1 Kc b1 c1 a2 b2 a3 b3 c2 a4 c3 b4"


class Sizes:
    def __init__(self, devices, slices, lengths):
        self.devices = devices
        self.chips = devices // CORES
        self.count, self.rows, self.width = slices.shape
        self.blocks = lengths.shape[1]
        self.unit = self.width // devices
        self.step = self.rows // self.blocks
        most = self.step // TILE + ((self.blocks - 2) * self.step + (self.blocks - 1) * (TILE - 1)) // TILE
        self.chunk = 256 // self.count
        self.chunks = -(-most * TILE // self.chunk)
        self.tiles = self.chunks * self.chunk // TILE
        self.depth = self.count * self.chunks * self.chunk
        self.extended = self.width + 2 * CORES * self.unit

    def parts(self, shift):
        return 1 if 2 * shift == self.chips else CORES

    def piece_blocks(self, shifts):
        return sum(self.parts(k) for k in shifts)


def fits(devices, slices, lengths):
    unit, step = slices.shape[2] // devices, slices.shape[1] // lengths.shape[1]
    return devices == 16 and unit == LANES and slices.shape[0] == 4 and step % TILE == 0


def place():
    me = lax.axis_index(AXIS)
    return me // CORES, lax.rem(me, CORES)


def load_and_mix(sz, mix_hbm, lengths_hbm, slices_hbm, left_ref, right_ref, raw, mix_ref, lengths_ref, table, sems):
    first = pltpu.make_async_copy(lengths_hbm, lengths_ref, sems.at[sz.chunks])
    second = pltpu.make_async_copy(mix_hbm, mix_ref, sems.at[sz.chunks + 1])
    first.start()
    second.start()
    first.wait()
    for p in range(sz.tiles + 1):
        table[0, p] = 0
        table[1, p] = 0
    at = jnp.int32(0)
    for j in range(sz.blocks):
        for i in range(sz.step // TILE):
            inside = lengths_ref[0, j] - i * TILE
            at_safe = jnp.minimum(at, sz.tiles)
            table[0, at_safe] = jnp.where(inside > 0, j * sz.step + i * TILE, 0)
            table[1, at_safe] = jnp.clip(inside, 0, TILE)
            at = at + (inside > 0).astype(jnp.int32)
    per = sz.chunk // TILE
    for p in range(sz.tiles):
        source = pl.multiple_of(table[0, p], TILE)
        pltpu.make_async_copy(
            slices_hbm.at[:, pl.ds(source, TILE), :], raw.at[:, pl.ds(p * TILE, TILE), :], sems.at[p // per]
        ).start()
    second.wait()
    weight = {}
    for k in range(sz.count):
        for l in range(sz.count):
            if l != k:
                weight[k, l] = (mix_ref[k, l] + mix_ref[l, k]) * 0.5
    span = 4 * LANES
    wide = 2 * LANES

    def one_chunk(g, carry):
        here = pl.ds(pl.multiple_of(g * sz.chunk, sz.chunk), sz.chunk)
        pltpu.make_async_copy(slices_hbm.at[:, pl.ds(0, sz.chunk), :], raw.at[:, here, :], sems.at[g]).wait()
        base = g * sz.count * sz.chunk
        for p in range(per):
            row = lax.broadcasted_iota(jnp.int32, (TILE, LANES), 0)
            used = jnp.tile(row < table[1, g * per + p], (1, span // LANES))

            def columns(i, carry):
                cols = pl.ds(pl.multiple_of(i * span, span), span)
                rows = pl.ds(pl.multiple_of(g * sz.chunk + p * TILE, TILE), TILE)
                f = [raw[k, rows, cols].astype(jnp.float32) for k in range(sz.count)]
                for k in range(sz.count):
                    total = None
                    for l in range(sz.count):
                        if l != k:
                            term = weight[k, l] * f[l]
                            total = term if total is None else total + term
                    value = jnp.where(used, total, 0.0).astype(jnp.bfloat16)
                    to = pl.ds(pl.multiple_of(base + k * sz.chunk + p * TILE, TILE), TILE)
                    right_ref[to, cols] = value
                return carry

            lax.fori_loop(0, sz.width // span, columns, 0, unroll=2)

        def turn(i, carry):
            cols = pl.ds(pl.multiple_of(i * wide, wide), wide)
            block = raw[:, here, cols].reshape(sz.count * sz.chunk, wide)
            left_ref[cols, pl.ds(pl.multiple_of(base, LANES), sz.count * sz.chunk)] = block.T
            return carry

        lax.fori_loop(0, sz.width // wide, turn, 0, unroll=2)
        rows = pl.ds(pl.multiple_of(base, LANES), sz.count * sz.chunk)
        right_ref[rows, sz.width :] = right_ref[rows, : sz.extended - sz.width]
        return carry

    lax.fori_loop(0, sz.chunks, one_chunk, 0)


def runs(shifts):
    out = []
    for k in shifts:
        if out and out[-1][-1] + 1 == k:
            out[-1].append(k)
        else:
            out.append([k])
    return out


def multiply(sz, piece, left_ref, right_ref, outs, acc):
    shifts, order = piece
    unit, chips = sz.unit, sz.chips
    blocks = sz.piece_blocks(shifts)
    wide = CORES * unit
    chip, core = place()
    half = chips // 2
    for bit in (1, 0):
        other_ref, own_ref = outs[2 * (1 - bit)], outs[2 * (1 - bit) + 1]

        def one(index, carry):
            slot = bit * order[0]
            for n, mask in enumerate(order[1:]):
                slot = slot + mask * ((index >> (len(order) - 2 - n)) & 1)
            row = chip ^ slot
            lhs = left_ref[pl.ds(pl.multiple_of(row * wide, wide), wide), :]
            at = 0
            for run in runs(shifts):
                col = lax.rem(row + run[0], chips)
                size = wide * len(run)
                acc[:, :size] = jnp.dot(
                    lhs, right_ref[:, pl.ds(pl.multiple_of(col * wide, wide), size)], preferred_element_type=jnp.float32
                )
                for n, k in enumerate(run):
                    for h in range(sz.parts(k)):
                        for ref, owner in ((other_ref, 1 - core), (own_ref, core)):
                            if 2 * k == chips:
                                rows, cols = owner, owner ^ (row >= half).astype(jnp.int32)
                            else:
                                rows, cols = owner ^ h, owner
                            ref[pl.ds(pl.multiple_of((index * blocks + at + h) * unit, unit), unit), :] = acc[
                                pl.ds(pl.multiple_of(rows * unit, unit), unit),
                                pl.ds(pl.multiple_of(n * wide + cols * unit, unit), unit),
                            ]
                    at += sz.parts(k)
            return carry

        lax.fori_loop(0, chips // 2, one, 0)


def vector(sz, left_ref, right_ref, step_ref, outs):
    x = jnp.broadcast_to(step_ref[...], (8, sz.width))
    applied = lax.dot_general(x, right_ref[:, : sz.width], DIMS1, preferred_element_type=jnp.float32)
    head = applied.astype(jnp.bfloat16).astype(jnp.float32)
    row = lax.broadcasted_iota(jnp.int32, applied.shape, 0)
    both = jnp.where(row == 0, head, jnp.where(row == 1, applied - head, 0.0)).astype(jnp.bfloat16)
    share = lax.dot_general(both, left_ref[...], DIMS1, preferred_element_type=jnp.float32)
    share = share[0:1, :] + share[1:2, :]
    extra = sz.width // LANES
    for ref in outs:
        first = ref.shape[0] - extra
        for r in range(extra):
            ref[first + r : first + r + 1, :] = share[:, r * LANES : (r + 1) * LANES]


def add_rows(to, at, size, *terms):
    block = LANES if size % LANES == 0 else size

    def one(i, carry):
        total = None
        for ref, first in terms:
            value = ref[pl.ds(pl.multiple_of(first + i * block, 8), block), :]
            total = value if total is None else total + value
        to[pl.ds(pl.multiple_of(at + i * block, 8), block), :] = total
        return carry

    lax.fori_loop(0, size // block, one, 0)


class Chain:
    def __init__(self):
        self.token = None

    def call(self, name, body, inputs, shapes, scratch=(), specs=None, flops=0, vmem=24):
        specs = list(specs or [VMEM] * len(inputs))
        inputs = list(inputs)
        count = len(inputs)
        if self.token is not None:
            inputs.append(self.token)
            specs.append(ANY)

        def kernel(*refs):
            body(*refs[:count], *refs[len(inputs) :])

        out = pl.pallas_call(
            kernel,
            in_specs=specs,
            out_specs=[VMEM] * len(shapes),
            out_shape=[jax.ShapeDtypeStruct(s, d) for s, d in shapes],
            scratch_shapes=list(scratch),
            cost_estimate=pl.CostEstimate(flops=flops, bytes_accessed=0, transcendentals=0),
            compiler_params=pltpu.CompilerParams(vmem_limit_bytes=vmem << 20),
            name=name,
        )(*inputs)
        self.token = out[-1]
        return out


def send(x, chips, to):
    pairs = []
    for chip in range(chips):
        for core in range(CORES):
            other, its_core = to(chip, core)
            pairs.append((chip * CORES + core, other * CORES + its_core))
    return lax.ppermute(x, AXIS, pairs)


def to_core(x, chips):
    return send(x, chips, lambda m, c: (m, 1 - c))


def across(x, chips, mask):
    return send(x, chips, lambda m, c: (m ^ mask, c))


def mirror(x, chips, shift):
    def to(m, c):
        flip = int(m >= shift) if 2 * shift == chips else 0
        return (m + shift) % chips, c ^ flip

    return send(x, chips, to)


def halved(sz, slices, slice_mix, lengths, search_step):
    chips, unit, f32 = sz.chips, sz.unit, jnp.float32
    chain = Chain()
    extra = sz.width // LANES
    state = {}
    step_row = search_step.reshape(1, -1)

    def tail(name):
        return extra if name == CARRIER else 0

    def start(name):
        piece = PIECES[name]
        shifts, order = piece
        rows = chips // 2 * sz.piece_blocks(shifts) * unit
        shapes = [((rows + tail(name), LANES), f32)] * 2 + [((rows, LANES), f32)] * 2
        wide = CORES * unit
        acc = pltpu.VMEM((wide, wide * max(len(r) for r in runs(shifts))), f32)
        flops = 2 * chips * wide * wide * len(shifts) * sz.depth
        if name == FIRST:

            def body(mix_hbm, lengths_hbm, slices_hbm, *refs):
                left_ref, right_ref = refs[:2]
                raw, mix_ref, lengths_ref, table, sems, acc_ref = refs[6:]
                load_and_mix(
                    sz, mix_hbm, lengths_hbm, slices_hbm, left_ref, right_ref, raw, mix_ref, lengths_ref, table, sems
                )
                multiply(sz, piece, left_ref, right_ref, refs[2:6], acc_ref)

            out = chain.call(
                "first",
                body,
                [slice_mix, lengths, slices],
                [((sz.width, sz.depth), jnp.bfloat16), ((sz.depth, sz.extended), jnp.bfloat16)] + shapes,
                scratch=[
                    pltpu.VMEM((sz.count, sz.chunks * sz.chunk, sz.width), jnp.bfloat16),
                    pltpu.SMEM(slice_mix.shape, f32),
                    pltpu.SMEM(lengths.shape, jnp.int32),
                    pltpu.SMEM((2, sz.tiles + 1), jnp.int32),
                    pltpu.SemaphoreType.DMA((sz.chunks + 2,)),
                    acc,
                ],
                specs=[HBM] * 3,
                flops=flops,
                vmem=40,
            )
            state["left"], state["right"] = out[:2]
            out = out[2:]
        else:

            def body(left_ref, right_ref, step_ref, *refs):
                if tail(name):
                    vector(sz, left_ref, right_ref, step_ref, refs[:2])
                multiply(sz, piece, left_ref, right_ref, refs[:4], refs[4])

            out = chain.call(
                "multiply_" + name,
                body,
                [state["left"], state["right"], step_row],
                shapes,
                scratch=[acc],
                flops=flops,
                vmem=40,
            )
        other1, own1, other0, own0 = out
        state[name] = dict(own1=own1, own0=own0, came1=to_core(other1, chips), came0=to_core(other0, chips))

    def first_sum(name):
        s = state[name]
        rows = s["own1"].shape[0]

        def body(own, came, out):
            add_rows(out, 0, rows - tail(name), (own, 0), (came, 0))
            if tail(name):
                add_rows(out, rows - extra, extra, (own, rows - extra), (came, rows - extra))

        s["sent"] = chain.call("sum1_" + name, body, [s["own1"], s["came1"]], [((rows, LANES), f32)])[0]
        s["came"] = across(s["sent"], chips, PIECES[name][1][0])

    def next_sum(name, n):
        s = state[name]
        held = [s["own0"], s["came0"]] if n == 1 else [s["kept"]]
        full = held[0].shape[0]
        rows = full // 2
        more = tail(name)

        def body(*refs):
            own, (sent, came), (send_ref, keep_ref) = refs[:-4], refs[-4:-2], refs[-2:]
            terms = [*own, came]
            add_rows(send_ref, 0, rows, *[(r, rows) for r in terms])
            add_rows(keep_ref, 0, rows, *[(r, 0) for r in terms])
            if more:
                add_rows(send_ref, rows, more, (sent, full), (came, full))

        out = chain.call(
            f"sum{n + 1}_" + name,
            body,
            [*held, s["sent"], s["came"]],
            [((rows + more, LANES), f32), ((rows, LANES), f32)],
        )
        s["sent"], s["kept"] = out
        s["came"] = across(s["sent"], chips, PIECES[name][1][n])

    def finish(name):
        s = state[name]
        shifts = PIECES[name][0]
        rows = s["kept"].shape[0]
        more = tail(name)
        swapped = [k for k in shifts if k and 2 * k != chips]
        shapes = [((sz.parts(k) * unit, LANES), f32) for k in shifts]
        if swapped:
            shapes.append(((len(swapped) * unit, LANES), f32))
        if more:
            shapes.append(((extra, LANES), f32))

        def body(kept, sent, came, *outs):
            at = 0
            for n, k in enumerate(shifts):
                add_rows(outs[n], 0, sz.parts(k) * unit, (kept, at), (came, at))
                if k in swapped:
                    add_rows(outs[len(shifts)], swapped.index(k) * unit, unit, (kept, at + unit), (came, at + unit))
                at += sz.parts(k) * unit
            if more:
                add_rows(outs[-1], 0, extra, (sent, rows), (came, rows))

        out = chain.call("done_" + name, body, [s["kept"], s["sent"], s["came"]], shapes)
        if swapped:
            got = to_core(out[len(shifts)], chips)
        for n, k in enumerate(shifts):
            arrays.append(out[n])
            plan.append(("own" if k else "self", k, 0, len(arrays) - 1, 0))
            if k:
                arrays.append(mirror(out[n], chips, k))
                plan.append(("mirrored", k, 0, len(arrays) - 1, 0))
        if swapped:
            arrays.append(got)
            for n, k in enumerate(swapped):
                plan.append(("swapped", k, n * unit, len(arrays) - 1, 0))
        if more:
            state["step"] = out[-1]

    def join(inputs):
        def body(*refs):
            out_ref = refs[-1]
            chip, core = place()

            def put(device, value):
                out_ref[:, pl.ds(pl.multiple_of(device * unit, unit), unit)] = value

            for kind, k, first, n, _ in plan:
                here = refs[n]
                after, before = lax.rem(chip + k, chips), lax.rem(chip + chips - k, chips)
                top = slice(first, first + unit)
                low = (chip >= k).astype(jnp.int32)
                if kind == "self":
                    for h in range(CORES):
                        put(chip * CORES + (core ^ h), here[h * unit : (h + 1) * unit, :].T)
                elif 2 * k == chips:
                    flip = low if kind == "own" else 1 - low
                    value = here[top, :]
                    put(after * CORES + (core ^ flip), value if kind == "own" else value.T)
                elif kind == "own":
                    put(after * CORES + core, here[top, :])
                elif kind == "swapped":
                    put(after * CORES + 1 - core, here[top, :])
                else:
                    for h in range(CORES):
                        put(before * CORES + (core ^ h), here[h * unit : (h + 1) * unit, :].T)

        return chain.call("join", body, inputs, [((unit, sz.width), f32)])[0]

    arrays, plan = [], []
    for what in ORDER.split():
        if what[0] == "K":
            start(what[1])
        elif what[1] == "1":
            first_sum(what[0])
        elif what[1] == "4":
            finish(what[0])
        else:
            next_sum(what[0], int(what[1]) - 1)
    for name in PIECES:
        if name + "4" not in ORDER:
            finish(name)
    out = join(arrays)
    return out, state["step"].reshape(-1)


def coupled(slices, slice_mix, lengths):
    count = slices.shape[0]
    coupling = (slice_mix + slice_mix.T) * 0.5 * (1.0 - jnp.eye(count, dtype=jnp.float32))
    blocks = lengths.shape[1]
    position = lax.broadcasted_iota(jnp.int32, (blocks, slices.shape[1] // blocks), 1)
    used = (position < lengths[0][:, None]).reshape(-1).astype(jnp.float32)
    out = []
    for k in range(count):
        total = coupling[k, 0] * slices[0].astype(jnp.float32)
        for l in range(1, count):
            total = total + coupling[k, l] * slices[l].astype(jnp.float32)
        out.append(total)
    return (jnp.stack(out) * used[None, :, None]).astype(jnp.bfloat16)


def whole(slices, slice_mix, lengths, search_step):
    width = slices.shape[2]
    left = slices.reshape(-1, width)
    right = coupled(slices, slice_mix, lengths).reshape(-1, width)
    rows = lax.psum_scatter(
        lax.dot_general(left, right, DIMS0, preferred_element_type=jnp.float32), AXIS, scatter_dimension=0, tiled=True
    )
    applied = jnp.dot(right, search_step, preferred_element_type=jnp.float32)
    head = applied.astype(jnp.bfloat16)
    tail = (applied - head.astype(jnp.float32)).astype(jnp.bfloat16)
    share = lax.dot_general(left, head, DIMS0, preferred_element_type=jnp.float32)
    share = share + lax.dot_general(left, tail, DIMS0, preferred_element_type=jnp.float32)
    return rows, lax.psum(share, AXIS)


def solution(mesh):
    devices = mesh.shape[AXIS]

    def on_device(slices, slice_mix, lengths, search_step):
        if fits(devices, slices, lengths):
            return halved(Sizes(devices, slices, lengths), slices, slice_mix, lengths, search_step)
        return whole(slices, slice_mix, lengths, search_step)

    return jax.shard_map(
        on_device,
        mesh=mesh,
        in_specs=(
            P(None, ("groups", AXIS), None),
            P(),
            P(("groups", AXIS), None),
            P("groups"),
        ),
        out_specs=(P(("groups", AXIS), None), P("groups")),
        check_vma=False,
    )
```

time: 239 us -> 116 us (0.49)
  waiting for transfers between devices: 109 us -> 57.8 us
  other arithmetic: 38.9 us -> 0 us
  blocking collectives: 38.2 us -> 0 us
  Pallas kernels: 0 us -> 33.5 us
  matrix products: 32.3 us -> 0 us
  starting transfers between devices: 0.04 us -> 21 us
  between operations: 14.1 us -> 0.79 us
  local copies, waits for them, and re-layouts: 6.48 us -> 2.04 us
    reduce_scatter x1 -> x0, waiting for transfers between devices: 109 us -> none  [on_device(): lax.psum_scatter(lax.dot_general(left, right, (((0,), (0,)), ((), ())), p...]
    ppermute x0 -> x21, waiting for transfers between devices: none -> 57.8 us  [send(): return lax.ppermute(x, AXIS, pairs)]
    psum x1 -> x0, blocking collectives: 38.2 us -> none  [on_device(): schur_step = lax.psum(share, 'block')]
    pallas_call x0 -> x16, Pallas kernels: none -> 33.5 us  [call(): pl.pallas_call(kernel, in_specs=specs, out_specs=[VMEM] * len(shapes), ou...]
    dot_general x4 -> x0, matrix products: 32.3 us -> none  [the longest x1 18.2 us: on_device(): lax.dot_general(left, right, (((0,), (0,)), ((), ())), preferred_element_...]
    ppermute x0 -> x21, starting transfers between devices: none -> 21 us  [send(): return lax.ppermute(x, AXIS, pairs)]
    add x3 -> x0, other arithmetic: 17.4 us -> none  [the longest x2 17.4 us: mix_slices(): total + coupling[target, source] * slices[source].astype(jnp.float32)]
    convert_element_type x3 -> x0, other arithmetic: 11.8 us -> none  [the longest x1 11 us: mix_slices(): return stacked.astype(jnp.bfloat16)]
  transfers between devices with their start and end apart: 1 -> 21, of which waited for: 1 -> 8; matrix products, arithmetic and copies ran while one was open for 14% -> 0% of each run, Pallas kernels for 0% -> 16%
where the time goes in v2:
time: 116 us; the launch traced here: 115 us
  waiting for transfers between devices  57.8 us (50%)
  Pallas kernels  33.5 us (29%)
  starting transfers between devices  21 us (18%)
  local copies, waits for them, and re-layouts  2.04 us (2%)
    ppermute x21, waiting for transfers between devices, send(): return lax.ppermute(x, AXIS, pairs)  57.8 us
    pallas_call x16, Pallas kernels, call(): pl.pallas_call(kernel, in_specs=specs, out_specs=[VMEM] * len(shapes), ou...  33.5 us
    ppermute x21, starting transfers between devices, send(): return lax.ppermute(x, AXIS, pairs)  21 us
  transfers between devices with their start and end apart: 21, of which 8 were waited for; matrix products, arithmetic and copies ran while one was open for 0% of the time, Pallas kernels for 16%

profile of v2, /device:TPU:0, one launch (start us, length us, event | category | flops | bytes accessed | tf_op | source)
XLA Modules:
  0.0 115.1 jit_solution(3738467928632974511)
XLA Ops:
  0.6 0.7 copy-done.1
  1.3 0.7 copy-done.2
  2.0 14.2 %first.1 = (bf16[2048,1280]{1,0:T(8,128)(2,1)S(1)}, bf16[1280,2560]{1,0:T(8,128)(2,1)}, f32[2048,128]{1,0:T(8,128)S(1)}, f32[2048,128]{1,0:T(8,128)S(1)}, f32[20...) custom-call(f32[4,4]{1,0:T(4,128)S(1)} %copy-done.1, s32[1,4]{1,0:T(1,128)S(1)} %copy-done.2, bf16[4,384,2048]{2,1,0:T(8,128)(2,1)} %refs_2_.1), custom_call_target="tpu_custom_call" | custom-call | flops 2684354560 | tf_op jit(solution)/shard_map/first/pallas_call | solution.py:226
  16.1 0.5 collective-permute-start.1
  16.7 10.6 %multiply_b.1 = (f32[1552,128]{1,0:T(8,128)S(1)}, f32[1552,128]{1,0:T(8,128)S(1)}, f32[1536,128]{1,0:T(8,128)S(1)}, f32[1536,128]{1,0:T(8,128)S(1)}) custom-call(bf16[2048,1280]{1,0:T(8,128)(2,1)S(1)} %get-tuple-element.39.refs_0_, bf16[1280,2560]{1,0:T(8,128)(2,1)} %get-tuple-element.40.refs_1_, bf16[1,2048]{1,0:T(2,128)(2,1)S(1)} %reshape.10.refs_2_, ...), custom_call_target="tpu_custom_call" | custom-call | flops 2684354560 | tf_op jit(solution)/shard_map/multiply_b/pallas_call | solution.py:226
  27.4 0.5 collective-permute-start
  28.0 2.7 %collective-permute-start.2 = (f32[2048,128]{1,0:T(8,128)S(1)}, f32[2048,128]{1,0:T(8,128)S(1)}, u32[]{:S(2)}, u32[]{:S(2)}) collective-permute-start(f32[2048,128]{1,0:T(8,128)S(1)} %sum1_a.1.refs_3_.refs_2_), channel_id=1, source_target_pairs={{0,2},{1,3},{2,0},{3,1},{4,6},{5,7},{6,4},{7,5},{8,10},{9,11},{10,... | collective-permute-start | bytes 3145736 | tf_op jit(solution)/shard_map/ppermute | solution.py:246
  30.7 5.8 %multiply_c.1 = (f32[1024,128]{1,0:T(8,128)S(1)}, f32[1024,128]{1,0:T(8,128)S(1)}, f32[1024,128]{1,0:T(8,128)S(1)}, f32[1024,128]{1,0:T(8,128)S(1)}) custom-call(bf16[2048,1280]{1,0:T(8,128)(2,1)S(1)} %get-tuple-element.39.refs_0_, bf16[1280,2560]{1,0:T(8,128)(2,1)} %get-tuple-element.40.refs_1_, bf16[1,2048]{1,0:T(2,128)(2,1)S(1)} %reshape.10.refs_2_, ...), custom_call_target="tpu_custom_call" | custom-call | flops 1342177280 | tf_op jit(solution)/shard_map/multiply_c/pallas_call | solution.py:226
  36.6 1.6 %collective-permute-start.7 = (f32[1552,128]{1,0:T(8,128)S(1)}, f32[1552,128]{1,0:T(8,128)S(1)}, u32[]{:S(2)}, u32[]{:S(2)}) collective-permute-start(f32[1552,128]{1,0:T(8,128)S(1)} %sum1_b.1.refs_2_), channel_id=1, source_target_pairs={{0,4},{1,5},{2,6},{3,7},{4,0},{5,1},{6,2},{7,3},{8,12},{9,13},{10,... | collective-permute-start | bytes 2383880 | tf_op jit(solution)/shard_map/ppermute | solution.py:246
  38.2 0.5 collective-permute-start.3
  38.8 2.5 %collective-permute-done.3.refs_1_ = f32[1024,128]{1,0:T(8,128)S(1)} collective-permute-done((f32[1024,128]{1,0:T(8,128)S(1)}, f32[1024,128]{1,0:T(8,128)S(1)}, u32[]{:S(2)}, u32[]{:S(2)}) %collective-permute-start.3) | collective-permute-done | bytes 524320 | tf_op jit(solution)/shard_map/ppermute | solution.py:246
  41.4 13.1 %collective-permute-done.2.refs_3_ = f32[2048,128]{1,0:T(8,128)S(1)} collective-permute-done((f32[2048,128]{1,0:T(8,128)S(1)}, f32[2048,128]{1,0:T(8,128)S(1)}, u32[]{:S(2)}, u32[]{:S(2)}) %collective-permute-start.2) | collective-permute-done | bytes 1048608 | tf_op jit(solution)/shard_map/ppermute | solution.py:246
  54.4 0.2 sum2_a.1
  54.6 1.9 %collective-permute-start.5 = (f32[1024,128]{1,0:T(8,128)S(1)}, f32[1024,128]{1,0:T(8,128)S(1)}, u32[]{:S(2)}, u32[]{:S(2)}) collective-permute-start(f32[1024,128]{1,0:T(8,128)S(1)} %get-tuple-element.48.refs_1_), channel_id=1, source_target_pairs={{0,4},{1,5},{2,6},{3,7},{4,0},{5,1},{6,2},{7,3},{8,12},{9,13},{10,... | collective-permute-start | bytes 1572872 | tf_op jit(solution)/shard_map/ppermute | solution.py:246
  56.5 1.5 %collective-permute-start.10 = (f32[1024,128]{1,0:T(8,128)S(1)}, f32[1024,128]{1,0:T(8,128)S(1)}, u32[]{:S(2)}, u32[]{:S(2)}) collective-permute-start(f32[1024,128]{1,0:T(8,128)S(1)} %sum1_c.1.refs_4_.refs_2_), channel_id=1, source_target_pairs={{0,2},{1,3},{2,0},{3,1},{4,6},{5,7},{6,4},{7,5},{8,10},{9,11},{10,... | collective-permute-start | bytes 1572872 | tf_op jit(solution)/shard_map/ppermute | solution.py:246
  58.2 0.6 collective-permute-start.11
  58.8 9.6 %collective-permute-done.5.refs_2_ = f32[1024,128]{1,0:T(8,128)S(1)} collective-permute-done((f32[1024,128]{1,0:T(8,128)S(1)}, f32[1024,128]{1,0:T(8,128)S(1)}, u32[]{:S(2)}, u32[]{:S(2)}) %collective-permute-start.5) | collective-permute-done | bytes 524320 | tf_op jit(solution)/shard_map/ppermute | solution.py:246
  68.5 2.7 %collective-permute-start.8 = (f32[512,128]{1,0:T(8,128)S(1)}, f32[512,128]{1,0:T(8,128)S(1)}, u32[]{:S(2)}, u32[]{:S(2)}) collective-permute-start(f32[512,128]{1,0:T(8,128)S(1)} %get-tuple-element.52.refs_1_), channel_id=1, source_target_pairs={{0,8},{1,9},{2,10},{3,11},{4,12},{5,13},{6,14},{7,15},{8,0},{9,1},... | collective-permute-start | bytes 786440 | tf_op jit(solution)/shard_map/ppermute | solution.py:246
  71.2 8.3 %collective-permute-done.11.refs_2_ = f32[784,128]{1,0:T(8,128)S(1)} collective-permute-done((f32[784,128]{1,0:T(8,128)S(1)}, f32[784,128]{1,0:T(8,128)S(1)}, u32[]{:S(2)}, u32[]{:S(2)}) %collective-permute-start.11) | collective-permute-done | bytes 401440 | tf_op jit(solution)/shard_map/ppermute | solution.py:246
  79.7 0.3 collective-permute-start.16
  80.0 2.8 %collective-permute-start.15 = (f32[400,128]{1,0:T(8,128)S(1)}, f32[400,128]{1,0:T(8,128)S(1)}, u32[]{:S(2)}, u32[]{:S(2)}) collective-permute-start(f32[400,128]{1,0:T(8,128)S(1)} %get-tuple-element.60.refs_1_), channel_id=1, source_target_pairs={{0,8},{1,9},{2,10},{3,11},{4,12},{5,13},{6,14},{7,15},{8,0},{9,1},... | collective-permute-start | bytes 614408 | tf_op jit(solution)/shard_map/ppermute | solution.py:246
  82.8 9.4 %collective-permute-done.16.refs_2_ = f32[512,128]{1,0:T(8,128)S(1)} collective-permute-done((f32[512,128]{1,0:T(8,128)S(1)}, f32[512,128]{1,0:T(8,128)S(1)}, u32[]{:S(2)}, u32[]{:S(2)}) %collective-permute-start.16) | collective-permute-done | bytes 262176 | tf_op jit(solution)/shard_map/ppermute | solution.py:246
  92.3 0.2 collective-permute-start.20
  92.5 0.6 done_b.1
  93.1 1.7 %collective-permute-start.12 = (f32[256,128]{1,0:T(8,128)S(1)}, f32[256,128]{1,0:T(8,128)S(1)}, u32[]{:S(2)}, u32[]{:S(2)}) collective-permute-start(f32[256,128]{1,0:T(8,128)S(1)} %get-tuple-element.57.refs_0_), channel_id=1, source_target_pairs={{0,2},{1,3},{2,4},{3,5},{4,6},{5,7},{6,8},{7,9},{8,10},{9,11},{10,... | collective-permute-start | bytes 393224 | tf_op jit(solution)/shard_map/ppermute | solution.py:246
  94.8 2.5 %collective-permute-start.13 = (f32[256,128]{1,0:T(8,128)S(1)}, f32[256,128]{1,0:T(8,128)S(1)}, u32[]{:S(2)}, u32[]{:S(2)}) collective-permute-start(f32[256,128]{1,0:T(8,128)S(1)} %get-tuple-element.58.refs_2_), channel_id=1, source_target_pairs={{0,4},{1,5},{2,6},{3,7},{4,8},{5,9},{6,10},{7,11},{8,12},{9,13},{1... | collective-permute-start | bytes 393224 | tf_op jit(solution)/shard_map/ppermute | solution.py:246
  97.3 1.0 collective-permute-start.17
  98.2 9.4 %collective-permute-done.20.refs_2_ = f32[256,128]{1,0:T(8,128)S(1)} collective-permute-done((f32[256,128]{1,0:T(8,128)S(1)}, f32[256,128]{1,0:T(8,128)S(1)}, u32[]{:S(2)}, u32[]{:S(2)}) %collective-permute-start.20) | collective-permute-done | bytes 131104 | tf_op jit(solution)/shard_map/ppermute | solution.py:246
  107.7 0.7 copy-done
  108.4 4.5 %collective-permute-done.18.refs_8_ = f32[128,128]{1,0:T(8,128)S(1)} collective-permute-done((f32[128,128]{1,0:T(8,128)S(1)}, f32[128,128]{1,0:T(8,128)S(1)}, u32[]{:S(2)}, u32[]{:S(2)}) %collective-permute-start.18) | collective-permute-done | bytes 65568 | tf_op jit(solution)/shard_map/ppermute | solution.py:246
  112.9 0.9 collective-permute-done.17.refs_6_
  113.8 1.2 %join.1 = f32[128,2048]{1,0:T(8,128)} custom-call(f32[256,128]{1,0:T(8,128)S(1)} %get-tuple-element.57.refs_0_, f32[256,128]{1,0:T(8,128)S(1)} %collective-permute-done.12.refs_1_, f32[256,128]{1,0:T(8,128)S(1)} %get-tuple-element.58.refs_2_, f32[256,128]{1,0:T(8,128)S(1)} %collective-permute-done.13.refs_3_, ...), custom_call_target="tpu_custom_call" | custom-call | tf_op jit(solution)/shard_map/join/pallas_call | solution.py:226
  (35 shorter events, 1.0 us)
Async XLA Ops:
  0.6 0.7 copy-start.1
  1.3 0.7 copy-start.2
  2.0 14.7 %copy-start.3 = (bf16[2048]{0:T(1024)(128)(2,1)S(1)}, bf16[2048]{0:T(1024)(128)(2,1)}, u32[]{:S(2)}) copy-start(bf16[2048]{0:T(1024)(128)(2,1)} %param.7) | copy-start | bytes 12292
  16.1 11.7 %collective-permute-start.1 = (f32[2048,128]{1,0:T(8,128)S(1)}, f32[2048,128]{1,0:T(8,128)S(1)}, u32[]{:S(2)}, u32[]{:S(2)}) collective-permute-start(f32[2048,128]{1,0:T(8,128)S(1)} %get-tuple-element.38), channel_id=1, source_target_pairs={{0,1},{1,0},{2,3},{3,2},{4,5},{5,4},{6,7},{7,6},{8,9},{9,8},{10,11... | collective-permute-start | bytes 3145736 | tf_op jit(solution)/shard_map/ppermute | solution.py:246
  27.3 9.2 %collective-permute-start.4 = (f32[1552,128]{1,0:T(8,128)S(1)}, f32[1552,128]{1,0:T(8,128)S(1)}, u32[]{:S(2)}, u32[]{:S(2)}) collective-permute-start(f32[1552,128]{1,0:T(8,128)S(1)} %get-tuple-element.45), channel_id=1, source_target_pairs={{0,1},{1,0},{2,3},{3,2},{4,5},{5,4},{6,7},{7,6},{8,9},{9,8},{10,11... | collective-permute-start | bytes 2383880 | tf_op jit(solution)/shard_map/ppermute | solution.py:246
  27.4 14.0 %collective-permute-start = (f32[2048,128]{1,0:T(8,128)S(1)}, f32[2048,128]{1,0:T(8,128)S(1)}, u32[]{:S(2)}, u32[]{:S(2)}) collective-permute-start(f32[2048,128]{1,0:T(8,128)S(1)} %get-tuple-element.36), channel_id=1, source_target_pairs={{0,1},{1,0},{2,3},{3,2},{4,5},{5,4},{6,7},{7,6},{8,9},{9,8},{10,11... | collective-permute-start | bytes 3145736 | tf_op jit(solution)/shard_map/ppermute | solution.py:246
  28.0 26.4 %collective-permute-start.2 = (f32[2048,128]{1,0:T(8,128)S(1)}, f32[2048,128]{1,0:T(8,128)S(1)}, u32[]{:S(2)}, u32[]{:S(2)}) collective-permute-start(f32[2048,128]{1,0:T(8,128)S(1)} %sum1_a.1.refs_3_.refs_2_), channel_id=1, source_target_pairs={{0,2},{1,3},{2,0},{3,1},{4,6},{5,7},{6,4},{7,5},{8,10},{9,11},{10,... | collective-permute-start | bytes 3145736 | tf_op jit(solution)/shard_map/ppermute | solution.py:246
  36.6 21.4 %collective-permute-start.7 = (f32[1552,128]{1,0:T(8,128)S(1)}, f32[1552,128]{1,0:T(8,128)S(1)}, u32[]{:S(2)}, u32[]{:S(2)}) collective-permute-start(f32[1552,128]{1,0:T(8,128)S(1)} %sum1_b.1.refs_2_), channel_id=1, source_target_pairs={{0,4},{1,5},{2,6},{3,7},{4,0},{5,1},{6,2},{7,3},{8,12},{9,13},{10,... | collective-permute-start | bytes 2383880 | tf_op jit(solution)/shard_map/ppermute | solution.py:246
  38.2 19.8 %collective-permute-start.6 = (f32[1536,128]{1,0:T(8,128)S(1)}, f32[1536,128]{1,0:T(8,128)S(1)}, u32[]{:S(2)}, u32[]{:S(2)}) collective-permute-start(f32[1536,128]{1,0:T(8,128)S(1)} %get-tuple-element.49), channel_id=1, source_target_pairs={{0,1},{1,0},{2,3},{3,2},{4,5},{5,4},{6,7},{7,6},{8,9},{9,8},{10,11... | collective-permute-start | bytes 2359304 | tf_op jit(solution)/shard_map/ppermute | solution.py:246
  38.2 3.0 %collective-permute-start.3 = (f32[1024,128]{1,0:T(8,128)S(1)}, f32[1024,128]{1,0:T(8,128)S(1)}, u32[]{:S(2)}, u32[]{:S(2)}) collective-permute-start(f32[1024,128]{1,0:T(8,128)S(1)} %get-tuple-element.43), channel_id=1, source_target_pairs={{0,1},{1,0},{2,3},{3,2},{4,5},{5,4},{6,7},{7,6},{8,9},{9,8},{10,11... | collective-permute-start | bytes 1572872 | tf_op jit(solution)/shard_map/ppermute | solution.py:246
  54.6 13.7 %collective-permute-start.5 = (f32[1024,128]{1,0:T(8,128)S(1)}, f32[1024,128]{1,0:T(8,128)S(1)}, u32[]{:S(2)}, u32[]{:S(2)}) collective-permute-start(f32[1024,128]{1,0:T(8,128)S(1)} %get-tuple-element.48.refs_1_), channel_id=1, source_target_pairs={{0,4},{1,5},{2,6},{3,7},{4,0},{5,1},{6,2},{7,3},{8,12},{9,13},{10,... | collective-permute-start | bytes 1572872 | tf_op jit(solution)/shard_map/ppermute | solution.py:246
  56.5 23.0 %collective-permute-start.9 = (f32[1024,128]{1,0:T(8,128)S(1)}, f32[1024,128]{1,0:T(8,128)S(1)}, u32[]{:S(2)}, u32[]{:S(2)}) collective-permute-start(f32[1024,128]{1,0:T(8,128)S(1)} %get-tuple-element.53), channel_id=1, source_target_pairs={{0,1},{1,0},{2,3},{3,2},{4,5},{5,4},{6,7},{7,6},{8,9},{9,8},{10,11... | collective-permute-start | bytes 1572872 | tf_op jit(solution)/shard_map/ppermute | solution.py:246
  56.5 23.0 %collective-permute-start.10 = (f32[1024,128]{1,0:T(8,128)S(1)}, f32[1024,128]{1,0:T(8,128)S(1)}, u32[]{:S(2)}, u32[]{:S(2)}) collective-permute-start(f32[1024,128]{1,0:T(8,128)S(1)} %sum1_c.1.refs_4_.refs_2_), channel_id=1, source_target_pairs={{0,2},{1,3},{2,0},{3,1},{4,6},{5,7},{6,4},{7,5},{8,10},{9,11},{10,... | collective-permute-start | bytes 1572872 | tf_op jit(solution)/shard_map/ppermute | solution.py:246
  58.2 21.2 %collective-permute-start.11 = (f32[784,128]{1,0:T(8,128)S(1)}, f32[784,128]{1,0:T(8,128)S(1)}, u32[]{:S(2)}, u32[]{:S(2)}) collective-permute-start(f32[784,128]{1,0:T(8,128)S(1)} %get-tuple-element.54.refs_1_), channel_id=1, source_target_pairs={{0,2},{1,3},{2,0},{3,1},{4,6},{5,7},{6,4},{7,5},{8,10},{9,11},{10,... | collective-permute-start | bytes 1204232 | tf_op jit(solution)/shard_map/ppermute | solution.py:246
  68.5 14.3 %collective-permute-start.8 = (f32[512,128]{1,0:T(8,128)S(1)}, f32[512,128]{1,0:T(8,128)S(1)}, u32[]{:S(2)}, u32[]{:S(2)}) collective-permute-start(f32[512,128]{1,0:T(8,128)S(1)} %get-tuple-element.52.refs_1_), channel_id=1, source_target_pairs={{0,8},{1,9},{2,10},{3,11},{4,12},{5,13},{6,14},{7,15},{8,0},{9,1},... | collective-permute-start | bytes 786440 | tf_op jit(solution)/shard_map/ppermute | solution.py:246
  79.7 12.6 %collective-permute-start.16 = (f32[512,128]{1,0:T(8,128)S(1)}, f32[512,128]{1,0:T(8,128)S(1)}, u32[]{:S(2)}, u32[]{:S(2)}) collective-permute-start(f32[512,128]{1,0:T(8,128)S(1)} %get-tuple-element.61.refs_1_), channel_id=1, source_target_pairs={{0,4},{1,5},{2,6},{3,7},{4,0},{5,1},{6,2},{7,3},{8,12},{9,13},{10,... | collective-permute-start | bytes 786440 | tf_op jit(solution)/shard_map/ppermute | solution.py:246
  80.0 12.5 %collective-permute-start.15 = (f32[400,128]{1,0:T(8,128)S(1)}, f32[400,128]{1,0:T(8,128)S(1)}, u32[]{:S(2)}, u32[]{:S(2)}) collective-permute-start(f32[400,128]{1,0:T(8,128)S(1)} %get-tuple-element.60.refs_1_), channel_id=1, source_target_pairs={{0,8},{1,9},{2,10},{3,11},{4,12},{5,13},{6,14},{7,15},{8,0},{9,1},... | collective-permute-start | bytes 614408 | tf_op jit(solution)/shard_map/ppermute | solution.py:246
  92.3 15.4 %collective-permute-start.20 = (f32[256,128]{1,0:T(8,128)S(1)}, f32[256,128]{1,0:T(8,128)S(1)}, u32[]{:S(2)}, u32[]{:S(2)}) collective-permute-start(f32[256,128]{1,0:T(8,128)S(1)} %get-tuple-element.66.refs_1_), channel_id=1, source_target_pairs={{0,8},{1,9},{2,10},{3,11},{4,12},{5,13},{6,14},{7,15},{8,0},{9,1},... | collective-permute-start | bytes 393224 | tf_op jit(solution)/shard_map/ppermute | solution.py:246
  93.1 5.1 %collective-permute-start.19 = (f32[128,128]{1,0:T(8,128)S(1)}, f32[128,128]{1,0:T(8,128)S(1)}, u32[]{:S(2)}, u32[]{:S(2)}) collective-permute-start(f32[128,128]{1,0:T(8,128)S(1)} %get-tuple-element.65), channel_id=1, source_target_pairs={{0,1},{1,0},{2,3},{3,2},{4,5},{5,4},{6,7},{7,6},{8,9},{9,8},{10,11... | collective-permute-start | bytes 196616 | tf_op jit(solution)/shard_map/ppermute | solution.py:246
  93.1 19.8 %collective-permute-start.12 = (f32[256,128]{1,0:T(8,128)S(1)}, f32[256,128]{1,0:T(8,128)S(1)}, u32[]{:S(2)}, u32[]{:S(2)}) collective-permute-start(f32[256,128]{1,0:T(8,128)S(1)} %get-tuple-element.57.refs_0_), channel_id=1, source_target_pairs={{0,2},{1,3},{2,4},{3,5},{4,6},{5,7},{6,8},{7,9},{8,10},{9,11},{10,... | collective-permute-start | bytes 393224 | tf_op jit(solution)/shard_map/ppermute | solution.py:246
  94.8 18.1 %collective-permute-start.13 = (f32[256,128]{1,0:T(8,128)S(1)}, f32[256,128]{1,0:T(8,128)S(1)}, u32[]{:S(2)}, u32[]{:S(2)}) collective-permute-start(f32[256,128]{1,0:T(8,128)S(1)} %get-tuple-element.58.refs_2_), channel_id=1, source_target_pairs={{0,4},{1,5},{2,6},{3,7},{4,8},{5,9},{6,10},{7,11},{8,12},{9,13},{1... | collective-permute-start | bytes 393224 | tf_op jit(solution)/shard_map/ppermute | solution.py:246
  97.3 16.6 %collective-permute-start.17 = (f32[256,128]{1,0:T(8,128)S(1)}, f32[256,128]{1,0:T(8,128)S(1)}, u32[]{:S(2)}, u32[]{:S(2)}) collective-permute-start(f32[256,128]{1,0:T(8,128)S(1)} %get-tuple-element.63.refs_5_), channel_id=1, source_target_pairs={{0,6},{1,7},{2,8},{3,9},{4,10},{5,11},{6,12},{7,13},{8,14},{9,15},... | collective-permute-start | bytes 393224 | tf_op jit(solution)/shard_map/ppermute | solution.py:246
  98.2 15.6 %collective-permute-start.14 = (f32[256,128]{1,0:T(8,128)S(1)}, f32[256,128]{1,0:T(8,128)S(1)}, u32[]{:S(2)}, u32[]{:S(2)}) collective-permute-start(f32[256,128]{1,0:T(8,128)S(1)} %get-tuple-element.59.refs_3_), channel_id=1, source_target_pairs={{0,1},{1,0},{2,3},{3,2},{4,5},{5,4},{6,7},{7,6},{8,9},{9,8},{10,11... | collective-permute-start | bytes 393224 | tf_op jit(solution)/shard_map/ppermute | solution.py:246
  107.6 5.2 %collective-permute-start.18 = (f32[128,128]{1,0:T(8,128)S(1)}, f32[128,128]{1,0:T(8,128)S(1)}, u32[]{:S(2)}, u32[]{:S(2)}) collective-permute-start(f32[128,128]{1,0:T(8,128)S(1)} %get-tuple-element.64.refs_7_), channel_id=1, source_target_pairs={{0,8},{1,9},{2,10},{3,11},{4,12},{5,13},{6,14},{7,15},{8,1},{9,0},... | collective-permute-start | bytes 196616 | tf_op jit(solution)/shard_map/ppermute | solution.py:246
  107.7 0.7 copy-start

commit v3 on v2

v3 whole, which is shorter than its diff:
```python
import functools

import jax
import jax.numpy as jnp
from jax import lax
from jax.experimental import pallas as pl
from jax.experimental.pallas import tpu as pltpu
from jax.sharding import PartitionSpec as P

AXIS = "block"
CORES = 2
TILE = 16
LANES = 128
DIMS0 = (((0,), (0,)), ((), ()))
DIMS1 = (((1,), (1,)), ((), ()))
VMEM = pl.BlockSpec(memory_space=pltpu.VMEM)
HBM = pl.BlockSpec(memory_space=pltpu.HBM)
ANY = pl.BlockSpec(memory_space=pl.ANY)

PIECES = {
    "a": ((0,), (1, 2, 4)),
    "b": ((1,), (1, 2, 4)),
    "c": ((3,), (2, 4, 1)),
    "d": ((2, 4), (1, 2, 4)),
}
SPLIT = "a"
SWAPPERS = "bcd"
LAST = "a"
CARRIER = "c"
ORDER = (
    *("Ka1", "Kd", "Kb", "Kc", "d1", "Ka0", "V", "c1", "fa", "a1", "b1", "d2", "c2", "b2"),
    *("d3", "a2", "c3", "b3", "d4", "c4", "b4", "a3", "c5", "d5", "b5", "a4", "a5"),
)


class Sizes:
    def __init__(self, devices, slices, lengths):
        self.devices = devices
        self.chips = devices // CORES
        self.count, self.rows, self.width = slices.shape
        self.blocks = lengths.shape[1]
        self.unit = self.width // devices
        self.step = self.rows // self.blocks
        most = self.step // TILE + ((self.blocks - 2) * self.step + (self.blocks - 1) * (TILE - 1)) // TILE
        self.chunk = 256 // self.count
        self.chunks = -(-most * TILE // self.chunk)
        self.tiles = self.chunks * self.chunk // TILE
        self.depth = self.count * self.chunks * self.chunk
        self.extended = self.width + 2 * CORES * self.unit

    def parts(self, shift):
        return 1 if 2 * shift == self.chips else CORES

    def piece_blocks(self, shifts):
        return sum(self.parts(k) for k in shifts)


def fits(devices, slices, lengths):
    unit, step = slices.shape[2] // devices, slices.shape[1] // lengths.shape[1]
    return devices == 16 and unit == LANES and slices.shape[0] == 4 and step % TILE == 0


def place():
    me = lax.axis_index(AXIS)
    return me // CORES, lax.rem(me, CORES)


def load_and_mix(sz, mix_hbm, lengths_hbm, slices_hbm, left_ref, right_ref, raw, mix_ref, lengths_ref, table, sems):
    first = pltpu.make_async_copy(lengths_hbm, lengths_ref, sems.at[sz.chunks])
    second = pltpu.make_async_copy(mix_hbm, mix_ref, sems.at[sz.chunks + 1])
    first.start()
    second.start()
    first.wait()
    for p in range(sz.tiles + 1):
        table[0, p] = 0
        table[1, p] = 0
    at = jnp.int32(0)
    for j in range(sz.blocks):
        for i in range(sz.step // TILE):
            inside = lengths_ref[0, j] - i * TILE
            at_safe = jnp.minimum(at, sz.tiles)
            table[0, at_safe] = jnp.where(inside > 0, j * sz.step + i * TILE, 0)
            table[1, at_safe] = jnp.clip(inside, 0, TILE)
            at = at + (inside > 0).astype(jnp.int32)
    per = sz.chunk // TILE
    for p in range(sz.tiles):
        source = pl.multiple_of(table[0, p], TILE)
        pltpu.make_async_copy(
            slices_hbm.at[:, pl.ds(source, TILE), :], raw.at[:, pl.ds(p * TILE, TILE), :], sems.at[p // per]
        ).start()
    second.wait()
    weight = {}
    for k in range(sz.count):
        for l in range(sz.count):
            if l != k:
                weight[k, l] = (mix_ref[k, l] + mix_ref[l, k]) * 0.5
    unit, wide = sz.unit, CORES * sz.unit
    _, core = place()

    def one_chunk(g, carry):
        here = pl.ds(pl.multiple_of(g * sz.chunk, sz.chunk), sz.chunk)
        pltpu.make_async_copy(slices_hbm.at[:, pl.ds(0, sz.chunk), :], raw.at[:, here, :], sems.at[g]).wait()
        base = g * sz.count * sz.chunk
        row = lax.broadcasted_iota(jnp.int32, (TILE, unit), 0)
        used = [row < table[1, g * per + p] for p in range(per)]

        def one_chip(i, carry):
            for c in range(CORES):
                cols = pl.ds(pl.multiple_of(i * wide + c * unit, unit), unit)
                mine = pl.ds(pl.multiple_of(i * wide + (c ^ core) * unit, unit), unit)
                for p in range(per):
                    rows = pl.ds(pl.multiple_of(g * sz.chunk + p * TILE, TILE), TILE)
                    f = [raw[k, rows, cols].astype(jnp.float32) for k in range(sz.count)]
                    for k in range(sz.count):
                        total = None
                        for l in range(sz.count):
                            if l != k:
                                term = weight[k, l] * f[l]
                                total = term if total is None else total + term
                        to = pl.ds(pl.multiple_of(base + k * sz.chunk + p * TILE, TILE), TILE)
                        right_ref[to, mine] = jnp.where(used[p], total, 0.0).astype(jnp.bfloat16)
                block = raw[:, here, cols].reshape(sz.count * sz.chunk, unit)
                left_ref[mine, pl.ds(pl.multiple_of(base, LANES), sz.count * sz.chunk)] = block.T
            return carry

        lax.fori_loop(0, sz.chips, one_chip, 0)
        rows = pl.ds(pl.multiple_of(base, LANES), sz.count * sz.chunk)
        right_ref[rows, sz.width :] = right_ref[rows, : sz.extended - sz.width]
        return carry

    lax.fori_loop(0, sz.chunks, one_chunk, 0)


def runs(shifts):
    out = []
    for k in shifts:
        if out and out[-1][-1] + 1 == k:
            out[-1].append(k)
        else:
            out.append([k])
    return out


def multiply(sz, piece, bit, left_ref, right_ref, other_ref, own_ref, first=0):
    shifts, order = piece
    unit, chips = sz.unit, sz.chips
    blocks = sz.piece_blocks(shifts)
    wide = CORES * unit
    chip, _ = place()
    half = chips // 2
    for index in range(half):
        slot = bit * order[0]
        for n, mask in enumerate(order[1:]):
            slot += mask * ((index >> (len(order) - 2 - n)) & 1)
        row = chip ^ slot
        at = first // unit + index * blocks
        for run in runs(shifts):
            col = lax.rem(row + run[0], chips)
            tile = jnp.dot(
                left_ref[pl.ds(pl.multiple_of(row * wide, wide), wide), :],
                right_ref[:, pl.ds(pl.multiple_of(col * wide, wide), wide * len(run))],
                preferred_element_type=jnp.float32,
            )
            for n, k in enumerate(run):
                for ref, owner in ((own_ref, 0), (other_ref, 1)):
                    if 2 * k == chips:
                        rows = tile[owner * unit : (owner + 1) * unit, n * wide : (n + 1) * wide]
                        same, cross = (rows[:, (owner ^ f) * unit : ((owner ^ f) + 1) * unit] for f in (0, 1))
                        ref[at * unit : (at + 1) * unit, :] = jnp.where(row >= half, cross, same)
                    else:
                        left = n * wide + owner * unit
                        for h in range(CORES):
                            rows = owner ^ h
                            ref[(at + h) * unit : (at + h + 1) * unit, :] = tile[
                                rows * unit : (rows + 1) * unit, left : left + unit
                            ]
                at += sz.parts(k)


def vector(sz, left_ref, right_ref, step_ref, outs):
    unit = sz.unit
    _, core = place()
    turned = []
    for d in range(sz.devices):
        turned.append(step_ref[:, pl.ds(pl.multiple_of((d ^ core) * unit, unit), unit)])
    x = jnp.broadcast_to(jnp.concatenate(turned, axis=1), (8, sz.width))
    applied = lax.dot_general(x, right_ref[:, : sz.width], DIMS1, preferred_element_type=jnp.float32)
    head = applied.astype(jnp.bfloat16).astype(jnp.float32)
    row = lax.broadcasted_iota(jnp.int32, applied.shape, 0)
    both = jnp.where(row == 0, head, jnp.where(row == 1, applied - head, 0.0)).astype(jnp.bfloat16)
    share = lax.dot_general(both, left_ref[...], DIMS1, preferred_element_type=jnp.float32)
    share = share[0:1, :] + share[1:2, :]
    for ref in outs:
        first = ref.shape[0] - sz.devices
        for d in range(sz.devices):
            ref[pl.ds(first + (d ^ core), 1), :] = share[:, d * unit : (d + 1) * unit]


def add_rows(to, at, size, *terms):
    block = LANES if size % LANES == 0 else size

    def one(i, carry):
        total = None
        for ref, first in terms:
            value = ref[pl.ds(pl.multiple_of(first + i * block, 8), block), :]
            total = value if total is None else total + value
        to[pl.ds(pl.multiple_of(at + i * block, 8), block), :] = total
        return carry

    lax.fori_loop(0, size // block, one, 0)


class Chain:
    def __init__(self):
        self.token = None

    def call(self, name, body, inputs, shapes, scratch=(), specs=None, outs=None, alias=None, flops=0, vmem=4):
        specs = list(specs or [VMEM] * len(inputs))
        inputs = list(inputs)
        count = len(inputs)
        if self.token is not None:
            inputs.append(self.token)
            specs.append(ANY)

        def kernel(*refs):
            body(*refs[:count], *refs[len(inputs) :])

        out = pl.pallas_call(
            kernel,
            in_specs=specs,
            out_specs=outs or [VMEM] * len(shapes),
            input_output_aliases=alias or {},
            out_shape=[jax.ShapeDtypeStruct(s, d) for s, d in shapes],
            scratch_shapes=list(scratch),
            cost_estimate=pl.CostEstimate(flops=flops, bytes_accessed=0, transcendentals=0),
            compiler_params=pltpu.CompilerParams(vmem_limit_bytes=vmem << 20),
            name=name,
        )(*inputs)
        self.token = out[-1]
        return out


def send(x, chips, to):
    pairs = []
    for chip in range(chips):
        for core in range(CORES):
            other, its_core = to(chip, core)
            pairs.append((chip * CORES + core, other * CORES + its_core))
    return lax.ppermute(x, AXIS, pairs)


def to_core(x, chips):
    return send(x, chips, lambda m, c: (m, 1 - c))


def across(x, chips, mask):
    return send(x, chips, lambda m, c: (m ^ mask, c))


def mirror(x, chips, shift):
    def to(m, c):
        flip = int(m >= shift) if 2 * shift == chips else 0
        return (m + shift) % chips, c ^ flip

    return send(x, chips, to)


def halved(sz, slices, slice_mix, lengths, search_step):
    chips, unit, f32 = sz.chips, sz.unit, jnp.float32
    chain = Chain()
    extra = sz.width // LANES
    state = {"swaps": []}
    step_row = search_step.reshape(1, -1)

    def tail(name):
        return extra if name == CARRIER else 0

    def start(name, bits):
        piece = PIECES[name]
        shifts = piece[0]
        half = chips // 2 * sz.piece_blocks(shifts) * unit
        rows = half * len(bits)
        shapes = [((rows, LANES), f32)] * 2
        flops = chips * (CORES * unit) ** 2 * len(shifts) * sz.depth * len(bits)
        if "left" not in state:

            def body(mix_hbm, lengths_hbm, slices_hbm, left_ref, right_ref, other_ref, own_ref, *scratch):
                load_and_mix(sz, mix_hbm, lengths_hbm, slices_hbm, left_ref, right_ref, *scratch)
                multiply(sz, piece, bits[0], left_ref, right_ref, other_ref, own_ref)

            out = chain.call(
                "first",
                body,
                [pltpu.with_memory_space_constraint(a, pltpu.HBM) for a in (slice_mix, lengths, slices)],
                [((sz.width, sz.depth), jnp.bfloat16), ((sz.depth, sz.extended), jnp.bfloat16)] + shapes,
                scratch=[
                    pltpu.VMEM((sz.count, sz.chunks * sz.chunk, sz.width), jnp.bfloat16),
                    pltpu.SMEM(slice_mix.shape, f32),
                    pltpu.SMEM(lengths.shape, jnp.int32),
                    pltpu.SMEM((2, sz.tiles + 1), jnp.int32),
                    pltpu.SemaphoreType.DMA((sz.chunks + 2,)),
                ],
                specs=[HBM] * 3,
                flops=flops,
                vmem=12,
            )
            state["left"], state["right"] = out[:2]
            other, own = out[2:]
        else:

            def body(left_ref, right_ref, other_ref, own_ref):
                for n, bit in enumerate(bits):
                    multiply(sz, piece, bit, left_ref, right_ref, other_ref, own_ref, n * half)

            other, own = chain.call(
                "multiply_" + name,
                body,
                [state["left"], state["right"]],
                shapes,
                flops=flops,
                vmem=8,
            )
        s = state.setdefault(name, {})
        n = bits[0] if len(bits) == 1 else ""
        s[f"own{n}"], s[f"came{n}"] = own, to_core(other, chips)

    def start_vector():
        def body(left_ref, right_ref, step_ref, out_ref):
            vector(sz, left_ref, right_ref, step_ref, [out_ref])

        share = chain.call(
            "vector", body, [state["left"], state["right"], step_row], [((extra, LANES), f32)], vmem=8
        )[0]
        state["vector"] = [share, to_core(share, chips)]

    def first_sum(name):
        s = state[name]
        half = chips // 2 * sz.piece_blocks(PIECES[name][0]) * unit
        more = tail(name)
        if name in SPLIT:

            def body(own, came, out):
                add_rows(out, 0, half, (own, 0), (came, 0))

            s["sent"] = chain.call("sum1_" + name, body, [s["own1"], s["came1"]], [((half, LANES), f32)])[0]
        else:

            def body(own, came, *refs):
                send_ref, keep_ref = refs[-2:]
                add_rows(send_ref, 0, half, (own, 0), (came, 0))
                add_rows(keep_ref, 0, half, (own, half), (came, half))
                if more:
                    add_rows(send_ref, half, more, (refs[0], 0), (refs[1], 0))

            s["sent"], s["kept"] = chain.call(
                "sum1_" + name,
                body,
                [s["own"], s["came"], *(state["vector"] if more else [])],
                [((half + more, LANES), f32), ((half, LANES), f32)],
            )
        s["came"] = across(s["sent"], chips, PIECES[name][1][0])

    def fold(name):
        s = state[name]
        rows = s["own0"].shape[0]

        def body(own, came, out):
            add_rows(out, 0, rows, (own, 0), (came, 0))

        s["kept"] = chain.call("fold_" + name, body, [s["own0"], s["came0"]], [((rows, LANES), f32)])[0]

    def next_sum(name, n):
        s = state[name]
        shifts, order = PIECES[name]
        full = s["kept"].shape[0]
        rows = full // 2
        more = tail(name)
        half = first_row(shifts, chips // 2) if n == len(order) - 1 and chips // 2 in shifts else None
        both = 0 if half is None else unit

        def body(kept, sent, came, send_ref, keep_ref):
            add_rows(send_ref, 0, rows, (kept, rows), (came, rows))
            add_rows(keep_ref, 0, rows, (kept, 0), (came, 0))
            if both:
                add_rows(send_ref, rows, both, (kept, half), (came, half))
            if more:
                add_rows(send_ref, rows + both, more, (sent, full), (came, full))

        s["sent"], s["kept"] = chain.call(
            f"sum{n + 1}_" + name,
            body,
            [s["kept"], s["sent"], s["came"]],
            [((rows + both + more, LANES), f32), ((rows, LANES), f32)],
        )
        s["came"] = across(s["sent"], chips, order[n])

    def first_row(shifts, shift):
        return unit * sz.piece_blocks([k for k in shifts if k < shift])

    def finish(name):
        s = state[name]
        shifts = PIECES[name][0]
        rows = s["kept"].shape[0]
        more = tail(name)
        swapped = [k for k in shifts if k]
        last = name in SWAPPERS
        before = list(state["swaps"]) if last else []
        shapes = [((CORES * unit, LANES), f32) for k in shifts]
        if last:
            shapes.append((((len(swapped) + len(before)) * unit, LANES), f32))
        if more:
            shapes.append(((extra, LANES), f32))

        def body(kept, sent, came, *refs):
            outs = refs[len(before) :]
            for n, k in enumerate(shifts):
                at = first_row(shifts, k)
                terms = [((kept, at + h * unit), (came, at + h * unit)) for h in range(sz.parts(k))]
                if 2 * k == chips:
                    terms.append(((sent, at), (came, rows)))
                for h, pair in enumerate(terms):
                    add_rows(outs[n], h * unit, unit, *pair)
                if last and k in swapped:
                    add_rows(outs[len(shifts)], (len(before) + swapped.index(k)) * unit, unit, *terms[1])
            for n, (_, _, row, _) in enumerate(before):
                add_rows(outs[len(shifts)], n * unit, unit, (refs[n], row))
            if more:
                add_rows(outs[-1], 0, extra, (sent, rows), (came, rows))

        out = chain.call("done_" + name, body, [s["kept"], s["sent"], s["came"], *(b[0] for b in before)], shapes)
        s["done"] = list(out[: len(shifts)])
        s["plan"] = [(k, "own", n, 0) for n, k in enumerate(shifts)]
        for k in swapped:
            if 2 * k != chips:
                s["plan"].append((k, "mirrored", len(s["done"]), 0))
                s["done"].append(mirror(out[shifts.index(k)], chips, k))
        for n, k in enumerate(swapped):
            state["swaps"].append((out[shifts.index(k)], k, unit, name))
        if last:
            for n, (_, k, _, _) in enumerate(state["swaps"]):
                s["plan"].append((k, "swapped", len(s["done"]), n * unit))
            s["done"].append(to_core(out[len(shifts)], chips))
            state["swaps"] = []
        if more:
            state["step"] = out[-1]

    def place_blocks(name):
        s = state[name]
        inputs, plan = s["done"], s["plan"]
        old = [state["out"]] if "out" in state else []
        final = name == LAST

        def body(*refs):
            chip, core = place()
            to = refs[len(inputs)]

            def put(device, value):
                to[:, pl.ds(pl.multiple_of(device * unit, unit), unit)] = value

            for k, kind, n, first in plan:
                here = refs[n]
                after, before = lax.rem(chip + k, chips), lax.rem(chip + chips - k, chips)
                one, two = (slice(first + h * unit, first + (h + 1) * unit) for h in range(2))
                low = (chip >= k).astype(jnp.int32)
                if k == 0:
                    put(chip * CORES + core, here[one, :].T)
                    put(chip * CORES + 1 - core, here[two, :].T)
                elif 2 * k == chips and kind == "own":
                    put(after * CORES + (core ^ low), here[one, :])
                    mine = (here, two)
                elif 2 * k == chips:
                    value = jnp.where(low > 0, mine[0][mine[1], :], here[one, :])
                    put(after * CORES + (core ^ (1 - low)), value.T)
                elif kind == "own":
                    put(after * CORES + core, here[one, :])
                elif kind == "swapped":
                    put(after * CORES + 1 - core, here[one, :])
                else:
                    put(before * CORES + core, here[one, :].T)
                    put(before * CORES + 1 - core, here[two, :].T)
            if final:
                pltpu.sync_copy(to, refs[len(inputs) + 1])

        state["out"] = chain.call(
            "place_" + name,
            body,
            [*inputs, *old],
            [((unit, sz.width), f32)],
            outs=[HBM] if final else [VMEM],
            alias={len(inputs): 0} if old and not final else None,
        )[0]

    for what in ORDER:
        if what == "V":
            start_vector()
        elif what[0] == "K":
            start(what[1], (int(what[2]),) if what[2:] else (1, 0))
        elif what[0] == "f":
            fold(what[1])
        elif what[1] == "1":
            first_sum(what[0])
        elif what[1] == "4":
            finish(what[0])
        elif what[1] == "5":
            place_blocks(what[0])
        else:
            next_sum(what[0], int(what[1]) - 1)
    return state["out"], state["step"].reshape(-1)


def coupled(slices, slice_mix, lengths):
    count = slices.shape[0]
    coupling = (slice_mix + slice_mix.T) * 0.5 * (1.0 - jnp.eye(count, dtype=jnp.float32))
    blocks = lengths.shape[1]
    position = lax.broadcasted_iota(jnp.int32, (blocks, slices.shape[1] // blocks), 1)
    used = (position < lengths[0][:, None]).reshape(-1).astype(jnp.float32)
    out = []
    for k in range(count):
        total = coupling[k, 0] * slices[0].astype(jnp.float32)
        for l in range(1, count):
            total = total + coupling[k, l] * slices[l].astype(jnp.float32)
        out.append(total)
    return (jnp.stack(out) * used[None, :, None]).astype(jnp.bfloat16)


def whole(slices, slice_mix, lengths, search_step):
    width = slices.shape[2]
    left = slices.reshape(-1, width)
    right = coupled(slices, slice_mix, lengths).reshape(-1, width)
    rows = lax.psum_scatter(
        lax.dot_general(left, right, DIMS0, preferred_element_type=jnp.float32), AXIS, scatter_dimension=0, tiled=True
    )
    applied = jnp.dot(right, search_step, preferred_element_type=jnp.float32)
    head = applied.astype(jnp.bfloat16)
    tail = (applied - head.astype(jnp.float32)).astype(jnp.bfloat16)
    share = lax.dot_general(left, head, DIMS0, preferred_element_type=jnp.float32)
    share = share + lax.dot_general(left, tail, DIMS0, preferred_element_type=jnp.float32)
    return rows, lax.psum(share, AXIS)


def solution(mesh):
    devices = mesh.shape[AXIS]

    def on_device(slices, slice_mix, lengths, search_step):
        if fits(devices, slices, lengths):
            return halved(Sizes(devices, slices, lengths), slices, slice_mix, lengths, search_step)
        return whole(slices, slice_mix, lengths, search_step)

    return jax.shard_map(
        on_device,
        mesh=mesh,
        in_specs=(
            P(None, ("groups", AXIS), None),
            P(),
            P(("groups", AXIS), None),
            P("groups"),
        ),
        out_specs=(P(("groups", AXIS), None), P("groups")),
        check_vma=False,
    )
```

time: 116 us -> 92.6 us (0.80)
  waiting for transfers between devices: 57.8 us -> 37.6 us
  Pallas kernels: 33.5 us -> 21.3 us
  starting transfers between devices: 21 us -> 31.8 us
    ppermute x21 -> x24, waiting for transfers between devices: 57.8 us -> 37.6 us  [send(): return lax.ppermute(x, AXIS, pairs)]
    pallas_call x16 -> x27, Pallas kernels: 33.5 us -> 21.3 us  [call(): pl.pallas_call(kernel, in_specs=specs, out_specs=outs or [VMEM] * len(sha...]
    ppermute x21 -> x24, starting transfers between devices: 21 us -> 31.8 us  [send(): return lax.ppermute(x, AXIS, pairs)]
  transfers between devices with their start and end apart: 21 -> 24, of which waited for: 8 -> 10; matrix products, arithmetic and copies ran while one was open for 0% -> 0% of each run, Pallas kernels for 16% -> 10%
where the time goes in v3:
time: 92.6 us; the launch traced here: 92.4 us
  waiting for transfers between devices  37.6 us (41%)
  starting transfers between devices  31.8 us (34%)
  Pallas kernels  21.3 us (23%)
    ppermute x24, waiting for transfers between devices, send(): return lax.ppermute(x, AXIS, pairs)  37.6 us
    ppermute x24, starting transfers between devices, send(): return lax.ppermute(x, AXIS, pairs)  31.8 us
    pallas_call x27, Pallas kernels, call(): pl.pallas_call(kernel, in_specs=specs, out_specs=outs or [VMEM] * len(sha...  21.3 us
  transfers between devices with their start and end apart: 24, of which 10 were waited for; matrix products, arithmetic and copies ran while one was open for 0% of the time, Pallas kernels for 10%

profile of v3, /device:TPU:0, one launch (start us, length us, event | category | flops | bytes accessed | tf_op | source)
XLA Modules:
  0.0 92.4 jit_solution(15413181474824001952)
XLA Ops:
  0.6 7.9 %first.1 = (bf16[2048,1280]{1,0:T(8,128)(2,1)S(1)}, bf16[1280,2560]{1,0:T(8,128)(2,1)S(1)}, f32[1024,128]{1,0:T(8,128)S(1)}, f32[1024,128]{1,0:T(8,128)S(1)}) custom-call(f32[4,4]{1,0:T(4,128)} %refs_0_.1, s32[1,4]{1,0:T(1,128)} %refs_1_.1, bf16[4,384,2048]{2,1,0:T(8,128)(2,1)} %refs_2_.1), custom_call_target="tpu_custom_call" | custom-call | flops 671088640 | tf_op jit(solution)/shard_map/first/pallas_call | solution.py:228
  8.6 2.9 %multiply_d.1 = (f32[3072,128]{1,0:T(8,128)S(1)}, f32[3072,128]{1,0:T(8,128)S(1)}) custom-call(bf16[2048,1280]{1,0:T(8,128)(2,1)S(1)} %get-tuple-element.44.refs_0_, bf16[1280,2560]{1,0:T(8,128)(2,1)S(1)} %get-tuple-element.45.refs_1_, f32[1024,128]{1,0:T(8,128)S(1)} %get-tuple-element.46.refs_2_.refs_0_), custom_call_target="tpu_custom_call" | custom-call | flops 2684354560 | tf_op jit(solution)/shard_map/multiply_d/pallas_call | solution.py:228
  12.0 1.5 %multiply_b.1 = (f32[2048,128]{1,0:T(8,128)S(1)}, f32[2048,128]{1,0:T(8,128)S(1)}) custom-call(bf16[2048,1280]{1,0:T(8,128)(2,1)S(1)} %get-tuple-element.44.refs_0_, bf16[1280,2560]{1,0:T(8,128)(2,1)S(1)} %get-tuple-element.45.refs_1_, f32[3072,128]{1,0:T(8,128)S(1)} %get-tuple-element.47.refs_2_.refs_0_), custom_call_target="tpu_custom_call" | custom-call | flops 1342177280 | tf_op jit(solution)/shard_map/multiply_b/pallas_call | solution.py:228
  13.5 1.5 %multiply_c.1 = (f32[2048,128]{1,0:T(8,128)S(1)}, f32[2048,128]{1,0:T(8,128)S(1)}) custom-call(bf16[2048,1280]{1,0:T(8,128)(2,1)S(1)} %get-tuple-element.44.refs_0_, bf16[1280,2560]{1,0:T(8,128)(2,1)S(1)} %get-tuple-element.45.refs_1_, f32[2048,128]{1,0:T(8,128)S(1)} %get-tuple-element.49.refs_2_.refs_0_), custom_call_target="tpu_custom_call" | custom-call | flops 1342177280 | tf_op jit(solution)/shard_map/multiply_c/pallas_call | solution.py:228
  15.8 2.7 %collective-permute-start.6 = (f32[1536,128]{1,0:T(8,128)S(1)}, f32[1536,128]{1,0:T(8,128)S(1)}, u32[]{:S(2)}, u32[]{:S(2)}) collective-permute-start(f32[1536,128]{1,0:T(8,128)S(1)} %get-tuple-element.57.refs_1_), channel_id=1, source_target_pairs={{0,2},{1,3},{2,0},{3,1},{4,6},{5,7},{6,4},{7,5},{8,10},{9,11},{10,... | collective-permute-start | bytes 2359304 | tf_op jit(solution)/shard_map/ppermute | solution.py:249
  18.5 0.8 multiply_a.1
  19.9 3.2 %vector.1.refs_2_.refs_4_ = f32[16,128]{1,0:T(8,128)S(1)} custom-call(bf16[2048,1280]{1,0:T(8,128)(2,1)S(1)} %get-tuple-element.44.refs_0_, bf16[1280,2560]{1,0:T(8,128)(2,1)S(1)} %get-tuple-element.45.refs_1_, bf16[1,2048]{1,0:T(2,128)(2,1)S(1)} %reshape.10.refs_2_, f32[1024,128]{1,0:T(8,128)S(1)} %get-tuple-element.52.refs_3_.refs_0_), custom_call_target="tpu_custom_call" | custom-call | tf_op jit(solution)/shard_map/vector/pallas_call | solution.py:228
  23.4 1.0 %collective-permute-done.3.refs_3_ = f32[16,128]{1,0:T(8,128)S(1)} collective-permute-done((f32[16,128]{1,0:T(8,128)S(1)}, f32[16,128]{1,0:T(8,128)S(1)}, u32[]{:S(2)}, u32[]{:S(2)}) %collective-permute-start.3) | collective-permute-done | bytes 8224 | tf_op jit(solution)/shard_map/ppermute | solution.py:249
  24.6 1.6 %collective-permute-start.10 = (f32[1040,128]{1,0:T(8,128)S(1)}, f32[1040,128]{1,0:T(8,128)S(1)}, u32[]{:S(2)}, u32[]{:S(2)}) collective-permute-start(f32[1040,128]{1,0:T(8,128)S(1)} %get-tuple-element.63.refs_1_), channel_id=1, source_target_pairs={{0,4},{1,5},{2,6},{3,7},{4,0},{5,1},{6,2},{7,3},{8,12},{9,13},{10,... | collective-permute-start | bytes 1597448 | tf_op jit(solution)/shard_map/ppermute | solution.py:249
  27.1 1.5 %collective-permute-start.5 = (f32[1024,128]{1,0:T(8,128)S(1)}, f32[1024,128]{1,0:T(8,128)S(1)}, u32[]{:S(2)}, u32[]{:S(2)}) collective-permute-start(f32[1024,128]{1,0:T(8,128)S(1)} %sum1_a.1.refs_2_.refs_1_), channel_id=1, source_target_pairs={{0,2},{1,3},{2,0},{3,1},{4,6},{5,7},{6,4},{7,5},{8,10},{9,11},{10,... | collective-permute-start | bytes 1572872 | tf_op jit(solution)/shard_map/ppermute | solution.py:249
  28.7 8.2 %collective-permute-done.6.refs_2_ = f32[1536,128]{1,0:T(8,128)S(1)} collective-permute-done((f32[1536,128]{1,0:T(8,128)S(1)}, f32[1536,128]{1,0:T(8,128)S(1)}, u32[]{:S(2)}, u32[]{:S(2)}) %collective-permute-start.6) | collective-permute-done | bytes 786464 | tf_op jit(solution)/shard_map/ppermute | solution.py:249
  37.0 2.1 %collective-permute-start.8 = (f32[768,128]{1,0:T(8,128)S(1)}, f32[768,128]{1,0:T(8,128)S(1)}, u32[]{:S(2)}, u32[]{:S(2)}) collective-permute-start(f32[768,128]{1,0:T(8,128)S(1)} %get-tuple-element.61.refs_1_), channel_id=1, source_target_pairs={{0,4},{1,5},{2,6},{3,7},{4,0},{5,1},{6,2},{7,3},{8,12},{9,13},{10,... | collective-permute-start | bytes 1179656 | tf_op jit(solution)/shard_map/ppermute | solution.py:249
  39.2 2.7 %collective-permute-start.13 = (f32[528,128]{1,0:T(8,128)S(1)}, f32[528,128]{1,0:T(8,128)S(1)}, u32[]{:S(2)}, u32[]{:S(2)}) collective-permute-start(f32[528,128]{1,0:T(8,128)S(1)} %get-tuple-element.70.refs_1_), channel_id=1, source_target_pairs={{0,8},{1,9},{2,10},{3,11},{4,12},{5,13},{6,14},{7,15},{8,0},{9,1},... | collective-permute-start | bytes 811016 | tf_op jit(solution)/shard_map/ppermute | solution.py:249
  41.8 6.3 %collective-permute-done.9.refs_2_ = f32[1024,128]{1,0:T(8,128)S(1)} collective-permute-done((f32[1024,128]{1,0:T(8,128)S(1)}, f32[1024,128]{1,0:T(8,128)S(1)}, u32[]{:S(2)}, u32[]{:S(2)}) %collective-permute-start.9) | collective-permute-done | bytes 524320 | tf_op jit(solution)/shard_map/ppermute | solution.py:249
  48.2 2.1 %collective-permute-start.12 = (f32[512,128]{1,0:T(8,128)S(1)}, f32[512,128]{1,0:T(8,128)S(1)}, u32[]{:S(2)}, u32[]{:S(2)}) collective-permute-start(f32[512,128]{1,0:T(8,128)S(1)} %get-tuple-element.69.refs_1_), channel_id=1, source_target_pairs={{0,4},{1,5},{2,6},{3,7},{4,0},{5,1},{6,2},{7,3},{8,12},{9,13},{10,... | collective-permute-start | bytes 786440 | tf_op jit(solution)/shard_map/ppermute | solution.py:249
  50.3 4.6 %collective-permute-done.8.refs_2_ = f32[768,128]{1,0:T(8,128)S(1)} collective-permute-done((f32[768,128]{1,0:T(8,128)S(1)}, f32[768,128]{1,0:T(8,128)S(1)}, u32[]{:S(2)}, u32[]{:S(2)}) %collective-permute-start.8) | collective-permute-done | bytes 393248 | tf_op jit(solution)/shard_map/ppermute | solution.py:249
  55.0 2.2 %collective-permute-start.16 = (f32[512,128]{1,0:T(8,128)S(1)}, f32[512,128]{1,0:T(8,128)S(1)}, u32[]{:S(2)}, u32[]{:S(2)}) collective-permute-start(f32[512,128]{1,0:T(8,128)S(1)} %get-tuple-element.75.refs_1_), channel_id=1, source_target_pairs={{0,8},{1,9},{2,10},{3,11},{4,12},{5,13},{6,14},{7,15},{8,0},{9,1},... | collective-permute-start | bytes 786440 | tf_op jit(solution)/shard_map/ppermute | solution.py:249
  57.2 1.9 %collective-permute-done.5.refs_2_ = f32[1024,128]{1,0:T(8,128)S(1)} collective-permute-done((f32[1024,128]{1,0:T(8,128)S(1)}, f32[1024,128]{1,0:T(8,128)S(1)}, u32[]{:S(2)}, u32[]{:S(2)}) %collective-permute-start.5) | collective-permute-done | bytes 524320 | tf_op jit(solution)/shard_map/ppermute | solution.py:249
  59.2 1.9 %collective-permute-start.11 = (f32[512,128]{1,0:T(8,128)S(1)}, f32[512,128]{1,0:T(8,128)S(1)}, u32[]{:S(2)}, u32[]{:S(2)}) collective-permute-start(f32[512,128]{1,0:T(8,128)S(1)} %get-tuple-element.68.refs_1_), channel_id=1, source_target_pairs={{0,4},{1,5},{2,6},{3,7},{4,0},{5,1},{6,2},{7,3},{8,12},{9,13},{10,... | collective-permute-start | bytes 786440 | tf_op jit(solution)/shard_map/ppermute | solution.py:249
  61.1 1.6 %collective-permute-start.15 = (f32[272,128]{1,0:T(8,128)S(1)}, f32[272,128]{1,0:T(8,128)S(1)}, u32[]{:S(2)}, u32[]{:S(2)}) collective-permute-start(f32[272,128]{1,0:T(8,128)S(1)} %get-tuple-element.74.refs_1_), channel_id=1, source_target_pairs={{0,2},{1,3},{2,0},{3,1},{4,6},{5,7},{6,4},{7,5},{8,10},{9,11},{10,... | collective-permute-start | bytes 417800 | tf_op jit(solution)/shard_map/ppermute | solution.py:249
  62.7 2.3 %collective-permute-done.12.refs_2_ = f32[512,128]{1,0:T(8,128)S(1)} collective-permute-done((f32[512,128]{1,0:T(8,128)S(1)}, f32[512,128]{1,0:T(8,128)S(1)}, u32[]{:S(2)}, u32[]{:S(2)}) %collective-permute-start.12) | collective-permute-done | bytes 262176 | tf_op jit(solution)/shard_map/ppermute | solution.py:249
  65.4 3.2 %collective-permute-done.16.refs_2_ = f32[512,128]{1,0:T(8,128)S(1)} collective-permute-done((f32[512,128]{1,0:T(8,128)S(1)}, f32[512,128]{1,0:T(8,128)S(1)}, u32[]{:S(2)}, u32[]{:S(2)}) %collective-permute-start.16) | collective-permute-done | bytes 262176 | tf_op jit(solution)/shard_map/ppermute | solution.py:249
  68.7 0.6 done_c.1
  69.3 1.5 %collective-permute-start.22 = (f32[256,128]{1,0:T(8,128)S(1)}, f32[256,128]{1,0:T(8,128)S(1)}, u32[]{:S(2)}, u32[]{:S(2)}) collective-permute-start(f32[256,128]{1,0:T(8,128)S(1)} %get-tuple-element.84.refs_0_), channel_id=1, source_target_pairs={{0,6},{1,7},{2,8},{3,9},{4,10},{5,11},{6,12},{7,13},{8,14},{9,15},... | collective-permute-start | bytes 393224 | tf_op jit(solution)/shard_map/ppermute | solution.py:249
  71.4 2.4 %collective-permute-done.14.refs_2_ = f32[256,128]{1,0:T(8,128)S(1)} collective-permute-done((f32[256,128]{1,0:T(8,128)S(1)}, f32[256,128]{1,0:T(8,128)S(1)}, u32[]{:S(2)}, u32[]{:S(2)}) %collective-permute-start.14) | collective-permute-done | bytes 131104 | tf_op jit(solution)/shard_map/ppermute | solution.py:249
  73.8 3.9 %collective-permute-start.20 = (f32[256,128]{1,0:T(8,128)S(1)}, f32[256,128]{1,0:T(8,128)S(1)}, u32[]{:S(2)}, u32[]{:S(2)}) collective-permute-start(f32[256,128]{1,0:T(8,128)S(1)} %get-tuple-element.82.refs_0_), channel_id=1, source_target_pairs={{0,4},{1,5},{2,6},{3,7},{4,8},{5,9},{6,10},{7,11},{8,12},{9,13},{1... | collective-permute-start | bytes 393224 | tf_op jit(solution)/shard_map/ppermute | solution.py:249
  77.7 0.7 copy-done
  78.4 1.7 %collective-permute-start.18 = (f32[256,128]{1,0:T(8,128)S(1)}, f32[256,128]{1,0:T(8,128)S(1)}, u32[]{:S(2)}, u32[]{:S(2)}) collective-permute-start(f32[256,128]{1,0:T(8,128)S(1)} %get-tuple-element.81.refs_0_), channel_id=1, source_target_pairs={{0,2},{1,3},{2,4},{3,5},{4,6},{5,7},{6,8},{7,9},{8,10},{9,11},{10,... | collective-permute-start | bytes 393224 | tf_op jit(solution)/shard_map/ppermute | solution.py:249
  80.1 3.1 %collective-permute-start.17 = (f32[256,128]{1,0:T(8,128)S(1)}, f32[256,128]{1,0:T(8,128)S(1)}, u32[]{:S(2)}, u32[]{:S(2)}) collective-permute-start(f32[256,128]{1,0:T(8,128)S(1)} %get-tuple-element.80.refs_1_), channel_id=1, source_target_pairs={{0,8},{1,9},{2,10},{3,11},{4,12},{5,13},{6,14},{7,15},{8,0},{9,1},... | collective-permute-start | bytes 393224 | tf_op jit(solution)/shard_map/ppermute | solution.py:249
  83.2 6.7 %collective-permute-done.22.refs_1_ = f32[256,128]{1,0:T(8,128)S(1)} collective-permute-done((f32[256,128]{1,0:T(8,128)S(1)}, f32[256,128]{1,0:T(8,128)S(1)}, u32[]{:S(2)}, u32[]{:S(2)}) %collective-permute-start.22) | collective-permute-done | bytes 131104 | tf_op jit(solution)/shard_map/ppermute | solution.py:249
  90.4 0.8 collective-permute-done.19.refs_2_
  91.3 1.1 %place_a.1 = f32[128,2048]{1,0:T(8,128)} custom-call(f32[256,128]{1,0:T(8,128)S(1)} %done_a.1.refs_0_.refs_2_, f32[128,2048]{1,0:T(8,128)S(1)} %place_b.1.refs_3_.refs_1_, f32[256,128]{1,0:T(8,128)S(1)} %done_a.1.refs_0_.refs_2_), custom_call_target="tpu_custom_call" | custom-call | tf_op jit(solution)/shard_map/place_a/pallas_call | solution.py:228
  (50 shorter events, 5.2 us)
Async XLA Ops:
  11.4 4.2 %collective-permute-start = (f32[3072,128]{1,0:T(8,128)S(1)}, f32[3072,128]{1,0:T(8,128)S(1)}, u32[]{:S(2)}, u32[]{:S(2)}) collective-permute-start(f32[3072,128]{1,0:T(8,128)S(1)} %get-tuple-element.48), channel_id=1, source_target_pairs={{0,1},{1,0},{2,3},{3,2},{4,5},{5,4},{6,7},{7,6},{8,9},{9,8},{10,11... | collective-permute-start | bytes 4718600 | tf_op jit(solution)/shard_map/ppermute | solution.py:249
  15.0 8.2 %collective-permute-start.2 = (f32[2048,128]{1,0:T(8,128)S(1)}, f32[2048,128]{1,0:T(8,128)S(1)}, u32[]{:S(2)}, u32[]{:S(2)}) collective-permute-start(f32[2048,128]{1,0:T(8,128)S(1)} %get-tuple-element.54), channel_id=1, source_target_pairs={{0,1},{1,0},{2,3},{3,2},{4,5},{5,4},{6,7},{7,6},{8,9},{9,8},{10,11... | collective-permute-start | bytes 3145736 | tf_op jit(solution)/shard_map/ppermute | solution.py:249
  15.2 11.2 %collective-permute-start.7 = (f32[2048,128]{1,0:T(8,128)S(1)}, f32[2048,128]{1,0:T(8,128)S(1)}, u32[]{:S(2)}, u32[]{:S(2)}) collective-permute-start(f32[2048,128]{1,0:T(8,128)S(1)} %get-tuple-element.58), channel_id=1, source_target_pairs={{0,1},{1,0},{2,3},{3,2},{4,5},{5,4},{6,7},{7,6},{8,9},{9,8},{10,11... | collective-permute-start | bytes 3145736 | tf_op jit(solution)/shard_map/ppermute | solution.py:249
  15.8 21.1 %collective-permute-start.6 = (f32[1536,128]{1,0:T(8,128)S(1)}, f32[1536,128]{1,0:T(8,128)S(1)}, u32[]{:S(2)}, u32[]{:S(2)}) collective-permute-start(f32[1536,128]{1,0:T(8,128)S(1)} %get-tuple-element.57.refs_1_), channel_id=1, source_target_pairs={{0,2},{1,3},{2,0},{3,1},{4,6},{5,7},{6,4},{7,5},{8,10},{9,11},{10,... | collective-permute-start | bytes 2359304 | tf_op jit(solution)/shard_map/ppermute | solution.py:249
  18.5 1.4 %copy-start.1 = (bf16[2048]{0:T(1024)(128)(2,1)S(1)}, bf16[2048]{0:T(1024)(128)(2,1)}, u32[]{:S(2)}) copy-start(bf16[2048]{0:T(1024)(128)(2,1)} %param.7) | copy-start | bytes 12292
  19.4 6.8 %collective-permute-start.1 = (f32[1024,128]{1,0:T(8,128)S(1)}, f32[1024,128]{1,0:T(8,128)S(1)}, u32[]{:S(2)}, u32[]{:S(2)}) collective-permute-start(f32[1024,128]{1,0:T(8,128)S(1)} %get-tuple-element.53), channel_id=1, source_target_pairs={{0,1},{1,0},{2,3},{3,2},{4,5},{5,4},{6,7},{7,6},{8,9},{9,8},{10,11... | collective-permute-start | bytes 1572872 | tf_op jit(solution)/shard_map/ppermute | solution.py:249
  19.6 6.7 %collective-permute-start.4 = (f32[1024,128]{1,0:T(8,128)S(1)}, f32[1024,128]{1,0:T(8,128)S(1)}, u32[]{:S(2)}, u32[]{:S(2)}) collective-permute-start(f32[1024,128]{1,0:T(8,128)S(1)} %get-tuple-element.56), channel_id=1, source_target_pairs={{0,1},{1,0},{2,3},{3,2},{4,5},{5,4},{6,7},{7,6},{8,9},{9,8},{10,11... | collective-permute-start | bytes 1572872 | tf_op jit(solution)/shard_map/ppermute | solution.py:249
  23.2 1.2 %collective-permute-start.3 = (f32[16,128]{1,0:T(8,128)S(1)}, f32[16,128]{1,0:T(8,128)S(1)}, u32[]{:S(2)}, u32[]{:S(2)}) collective-permute-start(f32[16,128]{1,0:T(8,128)S(1)} %vector.1.refs_2_.refs_4_), channel_id=1, source_target_pairs={{0,1},{1,0},{2,3},{3,2},{4,5},{5,4},{6,7},{7,6},{8,9},{9,8},{10,11... | collective-permute-start | bytes 24584 | tf_op jit(solution)/shard_map/ppermute | solution.py:249
  24.6 14.5 %collective-permute-start.10 = (f32[1040,128]{1,0:T(8,128)S(1)}, f32[1040,128]{1,0:T(8,128)S(1)}, u32[]{:S(2)}, u32[]{:S(2)}) collective-permute-start(f32[1040,128]{1,0:T(8,128)S(1)} %get-tuple-element.63.refs_1_), channel_id=1, source_target_pairs={{0,4},{1,5},{2,6},{3,7},{4,0},{5,1},{6,2},{7,3},{8,12},{9,13},{10,... | collective-permute-start | bytes 1597448 | tf_op jit(solution)/shard_map/ppermute | solution.py:249
  26.6 21.6 %collective-permute-start.9 = (f32[1024,128]{1,0:T(8,128)S(1)}, f32[1024,128]{1,0:T(8,128)S(1)}, u32[]{:S(2)}, u32[]{:S(2)}) collective-permute-start(f32[1024,128]{1,0:T(8,128)S(1)} %get-tuple-element.62.refs_1_), channel_id=1, source_target_pairs={{0,2},{1,3},{2,0},{3,1},{4,6},{5,7},{6,4},{7,5},{8,10},{9,11},{10,... | collective-permute-start | bytes 1572872 | tf_op jit(solution)/shard_map/ppermute | solution.py:249
  27.1 32.0 %collective-permute-start.5 = (f32[1024,128]{1,0:T(8,128)S(1)}, f32[1024,128]{1,0:T(8,128)S(1)}, u32[]{:S(2)}, u32[]{:S(2)}) collective-permute-start(f32[1024,128]{1,0:T(8,128)S(1)} %sum1_a.1.refs_2_.refs_1_), channel_id=1, source_target_pairs={{0,2},{1,3},{2,0},{3,1},{4,6},{5,7},{6,4},{7,5},{8,10},{9,11},{10,... | collective-permute-start | bytes 1572872 | tf_op jit(solution)/shard_map/ppermute | solution.py:249
  37.0 17.9 %collective-permute-start.8 = (f32[768,128]{1,0:T(8,128)S(1)}, f32[768,128]{1,0:T(8,128)S(1)}, u32[]{:S(2)}, u32[]{:S(2)}) collective-permute-start(f32[768,128]{1,0:T(8,128)S(1)} %get-tuple-element.61.refs_1_), channel_id=1, source_target_pairs={{0,4},{1,5},{2,6},{3,7},{4,0},{5,1},{6,2},{7,3},{8,12},{9,13},{10,... | collective-permute-start | bytes 1179656 | tf_op jit(solution)/shard_map/ppermute | solution.py:249
  39.2 21.9 %collective-permute-start.13 = (f32[528,128]{1,0:T(8,128)S(1)}, f32[528,128]{1,0:T(8,128)S(1)}, u32[]{:S(2)}, u32[]{:S(2)}) collective-permute-start(f32[528,128]{1,0:T(8,128)S(1)} %get-tuple-element.70.refs_1_), channel_id=1, source_target_pairs={{0,8},{1,9},{2,10},{3,11},{4,12},{5,13},{6,14},{7,15},{8,0},{9,1},... | collective-permute-start | bytes 811016 | tf_op jit(solution)/shard_map/ppermute | solution.py:249
  48.2 16.8 %collective-permute-start.12 = (f32[512,128]{1,0:T(8,128)S(1)}, f32[512,128]{1,0:T(8,128)S(1)}, u32[]{:S(2)}, u32[]{:S(2)}) collective-permute-start(f32[512,128]{1,0:T(8,128)S(1)} %get-tuple-element.69.refs_1_), channel_id=1, source_target_pairs={{0,4},{1,5},{2,6},{3,7},{4,0},{5,1},{6,2},{7,3},{8,12},{9,13},{10,... | collective-permute-start | bytes 786440 | tf_op jit(solution)/shard_map/ppermute | solution.py:249
  55.0 13.7 %collective-permute-start.16 = (f32[512,128]{1,0:T(8,128)S(1)}, f32[512,128]{1,0:T(8,128)S(1)}, u32[]{:S(2)}, u32[]{:S(2)}) collective-permute-start(f32[512,128]{1,0:T(8,128)S(1)} %get-tuple-element.75.refs_1_), channel_id=1, source_target_pairs={{0,8},{1,9},{2,10},{3,11},{4,12},{5,13},{6,14},{7,15},{8,0},{9,1},... | collective-permute-start | bytes 786440 | tf_op jit(solution)/shard_map/ppermute | solution.py:249
  59.2 19.2 %collective-permute-start.11 = (f32[512,128]{1,0:T(8,128)S(1)}, f32[512,128]{1,0:T(8,128)S(1)}, u32[]{:S(2)}, u32[]{:S(2)}) collective-permute-start(f32[512,128]{1,0:T(8,128)S(1)} %get-tuple-element.68.refs_1_), channel_id=1, source_target_pairs={{0,4},{1,5},{2,6},{3,7},{4,0},{5,1},{6,2},{7,3},{8,12},{9,13},{10,... | collective-permute-start | bytes 786440 | tf_op jit(solution)/shard_map/ppermute | solution.py:249
  61.1 7.6 %collective-permute-start.15 = (f32[272,128]{1,0:T(8,128)S(1)}, f32[272,128]{1,0:T(8,128)S(1)}, u32[]{:S(2)}, u32[]{:S(2)}) collective-permute-start(f32[272,128]{1,0:T(8,128)S(1)} %get-tuple-element.74.refs_1_), channel_id=1, source_target_pairs={{0,2},{1,3},{2,0},{3,1},{4,6},{5,7},{6,4},{7,5},{8,10},{9,11},{10,... | collective-permute-start | bytes 417800 | tf_op jit(solution)/shard_map/ppermute | solution.py:249
  65.0 8.8 %collective-permute-start.14 = (f32[256,128]{1,0:T(8,128)S(1)}, f32[256,128]{1,0:T(8,128)S(1)}, u32[]{:S(2)}, u32[]{:S(2)}) collective-permute-start(f32[256,128]{1,0:T(8,128)S(1)} %get-tuple-element.73.refs_1_), channel_id=1, source_target_pairs={{0,8},{1,9},{2,10},{3,11},{4,12},{5,13},{6,14},{7,15},{8,0},{9,1},... | collective-permute-start | bytes 393224 | tf_op jit(solution)/shard_map/ppermute | solution.py:249
  69.3 20.6 %collective-permute-start.22 = (f32[256,128]{1,0:T(8,128)S(1)}, f32[256,128]{1,0:T(8,128)S(1)}, u32[]{:S(2)}, u32[]{:S(2)}) collective-permute-start(f32[256,128]{1,0:T(8,128)S(1)} %get-tuple-element.84.refs_0_), channel_id=1, source_target_pairs={{0,6},{1,7},{2,8},{3,9},{4,10},{5,11},{6,12},{7,13},{8,14},{9,15},... | collective-permute-start | bytes 393224 | tf_op jit(solution)/shard_map/ppermute | solution.py:249
  70.8 9.3 %collective-permute-start.23 = (f32[128,128]{1,0:T(8,128)S(1)}, f32[128,128]{1,0:T(8,128)S(1)}, u32[]{:S(2)}, u32[]{:S(2)}) collective-permute-start(f32[128,128]{1,0:T(8,128)S(1)} %get-tuple-element.85), channel_id=1, source_target_pairs={{0,1},{1,0},{2,3},{3,2},{4,5},{5,4},{6,7},{7,6},{8,9},{9,8},{10,11... | collective-permute-start | bytes 196616 | tf_op jit(solution)/shard_map/ppermute | solution.py:249
  70.9 19.3 %collective-permute-start.21 = (f32[256,128]{1,0:T(8,128)S(1)}, f32[256,128]{1,0:T(8,128)S(1)}, u32[]{:S(2)}, u32[]{:S(2)}) collective-permute-start(f32[256,128]{1,0:T(8,128)S(1)} %get-tuple-element.76.refs_3_), channel_id=1, source_target_pairs={{0,1},{1,0},{2,3},{3,2},{4,5},{5,4},{6,7},{7,6},{8,9},{9,8},{10,11... | collective-permute-start | bytes 393224 | tf_op jit(solution)/shard_map/ppermute | solution.py:249
  73.8 16.4 %collective-permute-start.20 = (f32[256,128]{1,0:T(8,128)S(1)}, f32[256,128]{1,0:T(8,128)S(1)}, u32[]{:S(2)}, u32[]{:S(2)}) collective-permute-start(f32[256,128]{1,0:T(8,128)S(1)} %get-tuple-element.82.refs_0_), channel_id=1, source_target_pairs={{0,4},{1,5},{2,6},{3,7},{4,8},{5,9},{6,10},{7,11},{8,12},{9,13},{1... | collective-permute-start | bytes 393224 | tf_op jit(solution)/shard_map/ppermute | solution.py:249
  77.7 0.7 copy-start
  78.4 12.8 %collective-permute-start.18 = (f32[256,128]{1,0:T(8,128)S(1)}, f32[256,128]{1,0:T(8,128)S(1)}, u32[]{:S(2)}, u32[]{:S(2)}) collective-permute-start(f32[256,128]{1,0:T(8,128)S(1)} %get-tuple-element.81.refs_0_), channel_id=1, source_target_pairs={{0,2},{1,3},{2,4},{3,5},{4,6},{5,7},{6,8},{7,9},{8,10},{9,11},{10,... | collective-permute-start | bytes 393224 | tf_op jit(solution)/shard_map/ppermute | solution.py:249
  80.1 11.2 %collective-permute-start.17 = (f32[256,128]{1,0:T(8,128)S(1)}, f32[256,128]{1,0:T(8,128)S(1)}, u32[]{:S(2)}, u32[]{:S(2)}) collective-permute-start(f32[256,128]{1,0:T(8,128)S(1)} %get-tuple-element.80.refs_1_), channel_id=1, source_target_pairs={{0,8},{1,9},{2,10},{3,11},{4,12},{5,13},{6,14},{7,15},{8,0},{9,1},... | collective-permute-start | bytes 393224 | tf_op jit(solution)/shard_map/ppermute | solution.py:249
  89.9 1.3 %collective-permute-start.19 = (f32[128,128]{1,0:T(8,128)S(1)}, f32[128,128]{1,0:T(8,128)S(1)}, u32[]{:S(2)}, u32[]{:S(2)}) collective-permute-start(f32[128,128]{1,0:T(8,128)S(1)} %get-tuple-element.78.refs_3_), channel_id=1, source_target_pairs={{0,1},{1,0},{2,3},{3,2},{4,5},{5,4},{6,7},{7,6},{8,9},{9,8},{10,11... | collective-permute-start | bytes 196616 | tf_op jit(solution)/shard_map/ppermute | solution.py:249

commit v4 on v3

--- a/solution.py
+++ b/solution.py
@@ -19,17 +19,18 @@
 
 PIECES = {
     "a": ((0,), (1, 2, 4)),
-    "b": ((1,), (1, 2, 4)),
-    "c": ((3,), (2, 4, 1)),
-    "d": ((2, 4), (1, 2, 4)),
+    "b": ((2,), (2, 4, 1)),
+    "c": ((3,), (1, 2, 4)),
+    "d": ((1, 4), (1, 2, 4)),
 }
-SPLIT = "a"
+SPLIT = "abcd"
 SWAPPERS = "bcd"
 LAST = "a"
 CARRIER = "c"
 ORDER = (
-    *("Ka1", "Kd", "Kb", "Kc", "d1", "Ka0", "V", "c1", "fa", "a1", "b1", "d2", "c2", "b2"),
-    *("d3", "a2", "c3", "b3", "d4", "c4", "b4", "a3", "c5", "d5", "b5", "a4", "a5"),
+    *("Kd1", "Kb1", "Ka1", "d1", "Kd0", "a1", "b1", "Kb0", "Ka0", "Kc1", "fb", "fa", "V", "fd"),
+    *("Kc0", "c1", "d2", "b2", "fc", "d3", "c2", "b3", "a2", "c3", "d4", "b4", "a3", "c4"),
+    *("d5", "b5", "c5", "a4", "a5"),
 )
 
 
@@ -236,7 +237,7 @@
             compiler_params=pltpu.CompilerParams(vmem_limit_bytes=vmem << 20),
             name=name,
         )(*inputs)
-        self.token = out[-1]
+        self.token = out[0]
         return out
 
 
@@ -339,10 +340,13 @@
         more = tail(name)
         if name in SPLIT:
 
-            def body(own, came, out):
-                add_rows(out, 0, half, (own, 0), (came, 0))
-
-            s["sent"] = chain.call("sum1_" + name, body, [s["own1"], s["came1"]], [((half, LANES), f32)])[0]
+            def body(own, came, *refs):
+                add_rows(refs[-1], 0, half, (own, 0), (came, 0))
+                if more:
+                    add_rows(refs[-1], half, more, (refs[0], 0), (refs[1], 0))
+
+            inputs = [s["own1"], s["came1"], *(state["vector"] if more else [])]
+            s["sent"] = chain.call("sum1_" + name, body, inputs, [((half + more, LANES), f32)])[0]
         else:
 
             def body(own, came, *refs):
@@ -448,11 +452,10 @@
         s = state[name]
         inputs, plan = s["done"], s["plan"]
         old = [state["out"]] if "out" in state else []
-        final = name == LAST
 
         def body(*refs):
             chip, core = place()
-            to = refs[len(inputs)]
+            to = refs[len(inputs) + len(old)]
 
             def put(device, value):
                 to[:, pl.ds(pl.multiple_of(device * unit, unit), unit)] = value
@@ -462,10 +465,7 @@
                 after, before = lax.rem(chip + k, chips), lax.rem(chip + chips - k, chips)
                 one, two = (slice(first + h * unit, first + (h + 1) * unit) for h in range(2))
                 low = (chip >= k).astype(jnp.int32)
-                if k == 0:
-                    put(chip * CORES + core, here[one, :].T)
-                    put(chip * CORES + 1 - core, here[two, :].T)
-                elif 2 * k == chips and kind == "own":
+                if 2 * k == chips and kind == "own":
                     put(after * CORES + (core ^ low), here[one, :])
                     mine = (here, two)
                 elif 2 * k == chips:
@@ -478,17 +478,40 @@
                 else:
                     put(before * CORES + core, here[one, :].T)
                     put(before * CORES + 1 - core, here[two, :].T)
-            if final:
-                pltpu.sync_copy(to, refs[len(inputs) + 1])
-
-        state["out"] = chain.call(
+
+        out = chain.call(
             "place_" + name,
             body,
             [*inputs, *old],
             [((unit, sz.width), f32)],
-            outs=[HBM] if final else [VMEM],
-            alias={len(inputs): 0} if old and not final else None,
-        )[0]
+            alias={len(inputs): 0} if old else None,
+        )
+        state["out"] = out[0]
+
+    def place_last(name):
+        s = state[name]
+
+        def body(done, step, old, rows, out_ref, step_ref, sems):
+            chip, core = place()
+            vector_copy = pltpu.make_async_copy(step, step_ref, sems.at[1])
+            vector_copy.start()
+            for h in range(CORES):
+                cols = pl.ds(pl.multiple_of((chip * CORES + (core ^ h)) * unit, unit), unit)
+                rows[:, cols] = done[h * unit : (h + 1) * unit, :].T
+            rows_copy = pltpu.make_async_copy(rows, out_ref, sems.at[0])
+            rows_copy.start()
+            vector_copy.wait()
+            rows_copy.wait()
+
+        _, state["out"], state["step"] = chain.call(
+            "place_" + name,
+            body,
+            [s["done"][0], state["step"], state["out"]],
+            [((unit, sz.width), f32), ((unit, sz.width), f32), ((extra, LANES), f32)],
+            outs=[VMEM, HBM, HBM],
+            alias={2: 0},
+            scratch=[pltpu.SemaphoreType.DMA((2,))],
+        )
 
     for what in ORDER:
         if what == "V":
@@ -502,7 +525,7 @@
         elif what[1] == "4":
             finish(what[0])
         elif what[1] == "5":
-            place_blocks(what[0])
+            (place_last if what[0] == LAST else place_blocks)(what[0])
         else:
             next_sum(what[0], int(what[1]) - 1)
     return state["out"], state["step"].reshape(-1)

time: 92.6 us -> 91 us (0.983)
    ppermute x24 -> x27, waiting for transfers between devices: 37.6 us -> 37 us  [send(): return lax.ppermute(x, AXIS, pairs)]
    ppermute x24 -> x27, starting transfers between devices: 31.8 us -> 31.2 us  [send(): return lax.ppermute(x, AXIS, pairs)]
    pallas_call x27 -> x33, Pallas kernels: 21.3 us -> 21.2 us  [call(): pl.pallas_call(kernel, in_specs=specs, out_specs=outs or [VMEM] * len(sha...]
  transfers between devices with their start and end apart: 24 -> 27, of which waited for: 10 -> 7; matrix products, arithmetic and copies ran while one was open for 0% -> 0% of each run, Pallas kernels for 10% -> 13%
where the time goes in v4:
time: 91 us; the launch traced here: 90.6 us
  waiting for transfers between devices  37 us (41%)
  starting transfers between devices  31.2 us (34%)
  Pallas kernels  21.2 us (23%)
  between operations  0.98 us (1%)
    ppermute x27, waiting for transfers between devices, send(): return lax.ppermute(x, AXIS, pairs)  37 us
    ppermute x27, starting transfers between devices, send(): return lax.ppermute(x, AXIS, pairs)  31.2 us
    pallas_call x33, Pallas kernels, call(): pl.pallas_call(kernel, in_specs=specs, out_specs=outs or [VMEM] * len(sha...  21.2 us
  transfers between devices with their start and end apart: 27, of which 7 were waited for; matrix products, arithmetic and copies ran while one was open for 0% of the time, Pallas kernels for 13%

profile of v4, /device:TPU:0, one launch (start us, length us, event | category | flops | bytes accessed | tf_op | source)
XLA Modules:
  0.0 90.6 jit_solution(3582751869472177491)
XLA Ops:
  0.6 8.6 %first.1 = (bf16[2048,1280]{1,0:T(8,128)(2,1)S(1)}, bf16[1280,2560]{1,0:T(8,128)(2,1)S(1)}, f32[1536,128]{1,0:T(8,128)S(1)}, f32[1536,128]{1,0:T(8,128)S(1)}) custom-call(f32[4,4]{1,0:T(4,128)} %refs_0_.1, s32[1,4]{1,0:T(1,128)} %refs_1_.1, bf16[4,384,2048]{2,1,0:T(8,128)(2,1)} %refs_2_.1), custom_call_target="tpu_custom_call" | custom-call | flops 1342177280 | tf_op jit(solution)/shard_map/first/pallas_call | solution.py:229
  9.2 0.5 collective-permute-start.2
  9.7 0.8 multiply_b.2
  10.6 0.9 multiply_a.2
  12.2 1.5 %multiply_d.1 = (f32[1536,128]{1,0:T(8,128)S(1)}, f32[1536,128]{1,0:T(8,128)S(1)}) custom-call(bf16[2048,1280]{1,0:T(8,128)(2,1)S(1)} %get-tuple-element.46.refs_0_.refs_2_, bf16[1280,2560]{1,0:T(8,128)(2,1)S(1)} %get-tuple-element.47.refs_1_, f32[1536,128]{1,0:T(8,128)S(1)} %sum1_d.1.refs_2_.refs_1_), custom_call_target="tpu_custom_call" | custom-call | flops 1342177280 | tf_op jit(solution)/shard_map/multiply_d/pallas_call | solution.py:229
  13.8 2.9 %collective-permute-start.8 = (f32[1536,128]{1,0:T(8,128)S(1)}, f32[1536,128]{1,0:T(8,128)S(1)}, u32[]{:S(2)}, u32[]{:S(2)}) collective-permute-start(f32[1536,128]{1,0:T(8,128)S(1)} %sum1_d.1.refs_2_.refs_1_), channel_id=1, source_target_pairs={{0,2},{1,3},{2,0},{3,1},{4,6},{5,7},{6,4},{7,5},{8,10},{9,11},{10,... | collective-permute-start | bytes 2359304 | tf_op jit(solution)/shard_map/ppermute | solution.py:250
  17.0 0.9 multiply_b.3
  17.9 0.9 multiply_a.3
  18.8 0.5 collective-permute-start.3
  19.3 0.8 multiply_c.2
  20.3 1.6 %collective-permute-start.6 = (f32[1024,128]{1,0:T(8,128)S(1)}, f32[1024,128]{1,0:T(8,128)S(1)}, u32[]{:S(2)}, u32[]{:S(2)}) collective-permute-start(f32[1024,128]{1,0:T(8,128)S(1)} %sum1_b.1.refs_2_.refs_1_), channel_id=1, source_target_pairs={{0,4},{1,5},{2,6},{3,7},{4,0},{5,1},{6,2},{7,3},{8,12},{9,13},{10,... | collective-permute-start | bytes 1572872 | tf_op jit(solution)/shard_map/ppermute | solution.py:250
  22.1 3.2 %vector.1.refs_2_ = f32[16,128]{1,0:T(8,128)S(1)} custom-call(bf16[2048,1280]{1,0:T(8,128)(2,1)S(1)} %get-tuple-element.46.refs_0_.refs_2_, bf16[1280,2560]{1,0:T(8,128)(2,1)S(1)} %get-tuple-element.47.refs_1_, bf16[1,2048]{1,0:T(2,128)(2,1)S(1)} %reshape.10.refs_2_, f32[1024,128]{1,0:T(8,128)S(1)} %fold_a.1.refs_3_.refs_0_), custom_call_target="tpu_custom_call" | custom-call | tf_op jit(solution)/shard_map/vector/pallas_call | solution.py:229
  25.7 0.9 multiply_c.3
  26.6 0.6 collective-permute-start.13
  27.3 7.8 %collective-permute-done.8.refs_2_ = f32[1536,128]{1,0:T(8,128)S(1)} collective-permute-done((f32[1536,128]{1,0:T(8,128)S(1)}, f32[1536,128]{1,0:T(8,128)S(1)}, u32[]{:S(2)}, u32[]{:S(2)}) %collective-permute-start.8) | collective-permute-done | bytes 786464 | tf_op jit(solution)/shard_map/ppermute | solution.py:250
  35.2 2.2 %collective-permute-start.14 = (f32[768,128]{1,0:T(8,128)S(1)}, f32[768,128]{1,0:T(8,128)S(1)}, u32[]{:S(2)}, u32[]{:S(2)}) collective-permute-start(f32[768,128]{1,0:T(8,128)S(1)} %get-tuple-element.63.refs_3_.refs_1_), channel_id=1, source_target_pairs={{0,4},{1,5},{2,6},{3,7},{4,0},{5,1},{6,2},{7,3},{8,12},{9,13},{10,... | collective-permute-start | bytes 1179656 | tf_op jit(solution)/shard_map/ppermute | solution.py:250
  37.4 1.5 %collective-permute-start.5 = (f32[1024,128]{1,0:T(8,128)S(1)}, f32[1024,128]{1,0:T(8,128)S(1)}, u32[]{:S(2)}, u32[]{:S(2)}) collective-permute-start(f32[1024,128]{1,0:T(8,128)S(1)} %sum1_a.1.refs_2_.refs_1_), channel_id=1, source_target_pairs={{0,2},{1,3},{2,0},{3,1},{4,6},{5,7},{6,4},{7,5},{8,10},{9,11},{10,... | collective-permute-start | bytes 1572872 | tf_op jit(solution)/shard_map/ppermute | solution.py:250
  39.0 2.7 %collective-permute-start.11 = (f32[512,128]{1,0:T(8,128)S(1)}, f32[512,128]{1,0:T(8,128)S(1)}, u32[]{:S(2)}, u32[]{:S(2)}) collective-permute-start(f32[512,128]{1,0:T(8,128)S(1)} %get-tuple-element.65.refs_2_.refs_1_), channel_id=1, source_target_pairs={{0,8},{1,9},{2,10},{3,11},{4,12},{5,13},{6,14},{7,15},{8,0},{9,1},... | collective-permute-start | bytes 786440 | tf_op jit(solution)/shard_map/ppermute | solution.py:250
  41.8 9.2 %collective-permute-done.14.refs_2_ = f32[768,128]{1,0:T(8,128)S(1)} collective-permute-done((f32[768,128]{1,0:T(8,128)S(1)}, f32[768,128]{1,0:T(8,128)S(1)}, u32[]{:S(2)}, u32[]{:S(2)}) %collective-permute-start.14) | collective-permute-done | bytes 393248 | tf_op jit(solution)/shard_map/ppermute | solution.py:250
  51.2 4.0 %collective-permute-start.17 = (f32[512,128]{1,0:T(8,128)S(1)}, f32[512,128]{1,0:T(8,128)S(1)}, u32[]{:S(2)}, u32[]{:S(2)}) collective-permute-start(f32[512,128]{1,0:T(8,128)S(1)} %get-tuple-element.68.refs_3_.refs_1_), channel_id=1, source_target_pairs={{0,8},{1,9},{2,10},{3,11},{4,12},{5,13},{6,14},{7,15},{8,0},{9,1},... | collective-permute-start | bytes 786440 | tf_op jit(solution)/shard_map/ppermute | solution.py:250
  55.3 1.9 %collective-permute-done.5.refs_2_ = f32[1024,128]{1,0:T(8,128)S(1)} collective-permute-done((f32[1024,128]{1,0:T(8,128)S(1)}, f32[1024,128]{1,0:T(8,128)S(1)}, u32[]{:S(2)}, u32[]{:S(2)}) %collective-permute-start.5) | collective-permute-done | bytes 524320 | tf_op jit(solution)/shard_map/ppermute | solution.py:250
  57.3 1.9 %collective-permute-start.15 = (f32[512,128]{1,0:T(8,128)S(1)}, f32[512,128]{1,0:T(8,128)S(1)}, u32[]{:S(2)}, u32[]{:S(2)}) collective-permute-start(f32[512,128]{1,0:T(8,128)S(1)} %get-tuple-element.72.refs_3_.refs_1_), channel_id=1, source_target_pairs={{0,4},{1,5},{2,6},{3,7},{4,0},{5,1},{6,2},{7,3},{8,12},{9,13},{10,... | collective-permute-start | bytes 786440 | tf_op jit(solution)/shard_map/ppermute | solution.py:250
  59.2 6.0 %collective-permute-done.18.refs_2_ = f32[528,128]{1,0:T(8,128)S(1)} collective-permute-done((f32[528,128]{1,0:T(8,128)S(1)}, f32[528,128]{1,0:T(8,128)S(1)}, u32[]{:S(2)}, u32[]{:S(2)}) %collective-permute-start.18) | collective-permute-done | bytes 270368 | tf_op jit(solution)/shard_map/ppermute | solution.py:250
  65.2 0.6 collective-permute-start.20
  65.7 2.0 %collective-permute-start.16 = (f32[256,128]{1,0:T(8,128)S(1)}, f32[256,128]{1,0:T(8,128)S(1)}, u32[]{:S(2)}, u32[]{:S(2)}) collective-permute-start(f32[256,128]{1,0:T(8,128)S(1)} %get-tuple-element.70.refs_3_.refs_1_), channel_id=1, source_target_pairs={{0,2},{1,3},{2,0},{3,1},{4,6},{5,7},{6,4},{7,5},{8,10},{9,11},{10,... | collective-permute-start | bytes 393224 | tf_op jit(solution)/shard_map/ppermute | solution.py:250
  68.0 2.8 %collective-permute-done.16.refs_2_ = f32[256,128]{1,0:T(8,128)S(1)} collective-permute-done((f32[256,128]{1,0:T(8,128)S(1)}, f32[256,128]{1,0:T(8,128)S(1)}, u32[]{:S(2)}, u32[]{:S(2)}) %collective-permute-start.16) | collective-permute-done | bytes 131104 | tf_op jit(solution)/shard_map/ppermute | solution.py:250
  70.7 4.6 %collective-permute-start.23 = (f32[256,128]{1,0:T(8,128)S(1)}, f32[256,128]{1,0:T(8,128)S(1)}, u32[]{:S(2)}, u32[]{:S(2)}) collective-permute-start(f32[256,128]{1,0:T(8,128)S(1)} %get-tuple-element.78.refs_3_.refs_0_), channel_id=1, source_target_pairs={{0,4},{1,5},{2,6},{3,7},{4,8},{5,9},{6,10},{7,11},{8,12},{9,13},{1... | collective-permute-start | bytes 393224 | tf_op jit(solution)/shard_map/ppermute | solution.py:250
  75.5 1.7 %collective-permute-start.21 = (f32[256,128]{1,0:T(8,128)S(1)}, f32[256,128]{1,0:T(8,128)S(1)}, u32[]{:S(2)}, u32[]{:S(2)}) collective-permute-start(f32[256,128]{1,0:T(8,128)S(1)} %get-tuple-element.82.refs_4_.refs_0_), channel_id=1, source_target_pairs={{0,6},{1,7},{2,8},{3,9},{4,10},{5,11},{6,12},{7,13},{8,14},{9,15},... | collective-permute-start | bytes 393224 | tf_op jit(solution)/shard_map/ppermute | solution.py:250
  77.2 1.9 %collective-permute-start.19 = (f32[256,128]{1,0:T(8,128)S(1)}, f32[256,128]{1,0:T(8,128)S(1)}, u32[]{:S(2)}, u32[]{:S(2)}) collective-permute-start(f32[256,128]{1,0:T(8,128)S(1)} %get-tuple-element.80.refs_3_.refs_1_), channel_id=1, source_target_pairs={{0,8},{1,9},{2,10},{3,11},{4,12},{5,13},{6,14},{7,15},{8,0},{9,1},... | collective-permute-start | bytes 393224 | tf_op jit(solution)/shard_map/ppermute | solution.py:250
  79.1 0.5 collective-permute-start.22
  80.6 8.7 %collective-permute-done.21.refs_1_ = f32[256,128]{1,0:T(8,128)S(1)} collective-permute-done((f32[256,128]{1,0:T(8,128)S(1)}, f32[256,128]{1,0:T(8,128)S(1)}, u32[]{:S(2)}, u32[]{:S(2)}) %collective-permute-start.21) | collective-permute-done | bytes 131104 | tf_op jit(solution)/shard_map/ppermute | solution.py:250
  89.5 1.1 %place_a.1 = (f32[128,2048]{1,0:T(8,128)S(1)}, f32[128,2048]{1,0:T(8,128)}, f32[16,128]{1,0:T(8,128)}) custom-call(f32[256,128]{1,0:T(8,128)S(1)} %done_a.1.refs_0_.refs_3_, f32[16,128]{1,0:T(8,128)S(1)} %get-tuple-element.87.refs_1_, f32[128,2048]{1,0:T(8,128)S(1)} %place_c.1.refs_3_.refs_2_, ...), custom_call_target="tpu_custom_call", output_to_operand_aliasing={{0}: (2, {})} | custom-call | tf_op jit(solution)/shard_map/place_a/pallas_call | solution.py:229
  (60 shorter events, 3.8 us)
Async XLA Ops:
  9.2 2.8 %collective-permute-start.2 = (f32[1536,128]{1,0:T(8,128)S(1)}, f32[1536,128]{1,0:T(8,128)S(1)}, u32[]{:S(2)}, u32[]{:S(2)}) collective-permute-start(f32[1536,128]{1,0:T(8,128)S(1)} %get-tuple-element.53), channel_id=1, source_target_pairs={{0,1},{1,0},{2,3},{3,2},{4,5},{5,4},{6,7},{7,6},{8,9},{9,8},{10,11... | collective-permute-start | bytes 2359304 | tf_op jit(solution)/shard_map/ppermute | solution.py:250
  11.5 5.3 %collective-permute-start.1 = (f32[1024,128]{1,0:T(8,128)S(1)}, f32[1024,128]{1,0:T(8,128)S(1)}, u32[]{:S(2)}, u32[]{:S(2)}) collective-permute-start(f32[1024,128]{1,0:T(8,128)S(1)} %get-tuple-element.51.refs_2_), channel_id=1, source_target_pairs={{0,1},{1,0},{2,3},{3,2},{4,5},{5,4},{6,7},{7,6},{8,9},{9,8},{10,11... | collective-permute-start | bytes 1572872 | tf_op jit(solution)/shard_map/ppermute | solution.py:250
  11.6 5.3 %collective-permute-start = (f32[1024,128]{1,0:T(8,128)S(1)}, f32[1024,128]{1,0:T(8,128)S(1)}, u32[]{:S(2)}, u32[]{:S(2)}) collective-permute-start(f32[1024,128]{1,0:T(8,128)S(1)} %get-tuple-element.49.refs_2_), channel_id=1, source_target_pairs={{0,1},{1,0},{2,3},{3,2},{4,5},{5,4},{6,7},{7,6},{8,9},{9,8},{10,11... | collective-permute-start | bytes 1572872 | tf_op jit(solution)/shard_map/ppermute | solution.py:250
  13.7 11.9 %collective-permute-start.7 = (f32[1536,128]{1,0:T(8,128)S(1)}, f32[1536,128]{1,0:T(8,128)S(1)}, u32[]{:S(2)}, u32[]{:S(2)}) collective-permute-start(f32[1536,128]{1,0:T(8,128)S(1)} %get-tuple-element.54.refs_2_), channel_id=1, source_target_pairs={{0,1},{1,0},{2,3},{3,2},{4,5},{5,4},{6,7},{7,6},{8,9},{9,8},{10,11... | collective-permute-start | bytes 2359304 | tf_op jit(solution)/shard_map/ppermute | solution.py:250
  13.8 21.3 %collective-permute-start.8 = (f32[1536,128]{1,0:T(8,128)S(1)}, f32[1536,128]{1,0:T(8,128)S(1)}, u32[]{:S(2)}, u32[]{:S(2)}) collective-permute-start(f32[1536,128]{1,0:T(8,128)S(1)} %sum1_d.1.refs_2_.refs_1_), channel_id=1, source_target_pairs={{0,2},{1,3},{2,0},{3,1},{4,6},{5,7},{6,4},{7,5},{8,10},{9,11},{10,... | collective-permute-start | bytes 2359304 | tf_op jit(solution)/shard_map/ppermute | solution.py:250
  17.8 2.4 %collective-permute-start.4 = (f32[1024,128]{1,0:T(8,128)S(1)}, f32[1024,128]{1,0:T(8,128)S(1)}, u32[]{:S(2)}, u32[]{:S(2)}) collective-permute-start(f32[1024,128]{1,0:T(8,128)S(1)} %get-tuple-element.55.refs_2_), channel_id=1, source_target_pairs={{0,1},{1,0},{2,3},{3,2},{4,5},{5,4},{6,7},{7,6},{8,9},{9,8},{10,11... | collective-permute-start | bytes 1572872 | tf_op jit(solution)/shard_map/ppermute | solution.py:250
  18.8 3.1 %copy-start = (bf16[2048]{0:T(1024)(128)(2,1)S(1)}, bf16[2048]{0:T(1024)(128)(2,1)}, u32[]{:S(2)}) copy-start(bf16[2048]{0:T(1024)(128)(2,1)} %param.7) | copy-start | bytes 12292
  18.8 3.2 %collective-permute-start.3 = (f32[1024,128]{1,0:T(8,128)S(1)}, f32[1024,128]{1,0:T(8,128)S(1)}, u32[]{:S(2)}, u32[]{:S(2)}) collective-permute-start(f32[1024,128]{1,0:T(8,128)S(1)} %get-tuple-element.57.refs_2_), channel_id=1, source_target_pairs={{0,1},{1,0},{2,3},{3,2},{4,5},{5,4},{6,7},{7,6},{8,9},{9,8},{10,11... | collective-permute-start | bytes 1572872 | tf_op jit(solution)/shard_map/ppermute | solution.py:250
  20.2 6.4 %collective-permute-start.9 = (f32[1024,128]{1,0:T(8,128)S(1)}, f32[1024,128]{1,0:T(8,128)S(1)}, u32[]{:S(2)}, u32[]{:S(2)}) collective-permute-start(f32[1024,128]{1,0:T(8,128)S(1)} %get-tuple-element.59.refs_2_), channel_id=1, source_target_pairs={{0,1},{1,0},{2,3},{3,2},{4,5},{5,4},{6,7},{7,6},{8,9},{9,8},{10,11... | collective-permute-start | bytes 1572872 | tf_op jit(solution)/shard_map/ppermute | solution.py:250
  20.3 18.7 %collective-permute-start.6 = (f32[1024,128]{1,0:T(8,128)S(1)}, f32[1024,128]{1,0:T(8,128)S(1)}, u32[]{:S(2)}, u32[]{:S(2)}) collective-permute-start(f32[1024,128]{1,0:T(8,128)S(1)} %sum1_b.1.refs_2_.refs_1_), channel_id=1, source_target_pairs={{0,4},{1,5},{2,6},{3,7},{4,0},{5,1},{6,2},{7,3},{8,12},{9,13},{10,... | collective-permute-start | bytes 1572872 | tf_op jit(solution)/shard_map/ppermute | solution.py:250
  25.4 1.2 %collective-permute-start.10 = (f32[16,128]{1,0:T(8,128)S(1)}, f32[16,128]{1,0:T(8,128)S(1)}, u32[]{:S(2)}, u32[]{:S(2)}) collective-permute-start(f32[16,128]{1,0:T(8,128)S(1)} %vector.1.refs_2_), channel_id=1, source_target_pairs={{0,1},{1,0},{2,3},{3,2},{4,5},{5,4},{6,7},{7,6},{8,9},{9,8},{10,11... | collective-permute-start | bytes 24584 | tf_op jit(solution)/shard_map/ppermute | solution.py:250
  26.6 24.4 %collective-permute-start.13 = (f32[1040,128]{1,0:T(8,128)S(1)}, f32[1040,128]{1,0:T(8,128)S(1)}, u32[]{:S(2)}, u32[]{:S(2)}) collective-permute-start(f32[1040,128]{1,0:T(8,128)S(1)} %sum1_c.1.refs_3_.refs_1_), channel_id=1, source_target_pairs={{0,2},{1,3},{2,0},{3,1},{4,6},{5,7},{6,4},{7,5},{8,10},{9,11},{10,... | collective-permute-start | bytes 1597448 | tf_op jit(solution)/shard_map/ppermute | solution.py:250
  27.2 14.5 %collective-permute-start.12 = (f32[1024,128]{1,0:T(8,128)S(1)}, f32[1024,128]{1,0:T(8,128)S(1)}, u32[]{:S(2)}, u32[]{:S(2)}) collective-permute-start(f32[1024,128]{1,0:T(8,128)S(1)} %get-tuple-element.62.refs_4_), channel_id=1, source_target_pairs={{0,1},{1,0},{2,3},{3,2},{4,5},{5,4},{6,7},{7,6},{8,9},{9,8},{10,11... | collective-permute-start | bytes 1572872 | tf_op jit(solution)/shard_map/ppermute | solution.py:250
  35.2 15.7 %collective-permute-start.14 = (f32[768,128]{1,0:T(8,128)S(1)}, f32[768,128]{1,0:T(8,128)S(1)}, u32[]{:S(2)}, u32[]{:S(2)}) collective-permute-start(f32[768,128]{1,0:T(8,128)S(1)} %get-tuple-element.63.refs_3_.refs_1_), channel_id=1, source_target_pairs={{0,4},{1,5},{2,6},{3,7},{4,0},{5,1},{6,2},{7,3},{8,12},{9,13},{10,... | collective-permute-start | bytes 1179656 | tf_op jit(solution)/shard_map/ppermute | solution.py:250
  37.4 19.8 %collective-permute-start.5 = (f32[1024,128]{1,0:T(8,128)S(1)}, f32[1024,128]{1,0:T(8,128)S(1)}, u32[]{:S(2)}, u32[]{:S(2)}) collective-permute-start(f32[1024,128]{1,0:T(8,128)S(1)} %sum1_a.1.refs_2_.refs_1_), channel_id=1, source_target_pairs={{0,2},{1,3},{2,0},{3,1},{4,6},{5,7},{6,4},{7,5},{8,10},{9,11},{10,... | collective-permute-start | bytes 1572872 | tf_op jit(solution)/shard_map/ppermute | solution.py:250
  39.0 16.2 %collective-permute-start.11 = (f32[512,128]{1,0:T(8,128)S(1)}, f32[512,128]{1,0:T(8,128)S(1)}, u32[]{:S(2)}, u32[]{:S(2)}) collective-permute-start(f32[512,128]{1,0:T(8,128)S(1)} %get-tuple-element.65.refs_2_.refs_1_), channel_id=1, source_target_pairs={{0,8},{1,9},{2,10},{3,11},{4,12},{5,13},{6,14},{7,15},{8,0},{9,1},... | collective-permute-start | bytes 786440 | tf_op jit(solution)/shard_map/ppermute | solution.py:250
  51.1 14.0 %collective-permute-start.18 = (f32[528,128]{1,0:T(8,128)S(1)}, f32[528,128]{1,0:T(8,128)S(1)}, u32[]{:S(2)}, u32[]{:S(2)}) collective-permute-start(f32[528,128]{1,0:T(8,128)S(1)} %get-tuple-element.69.refs_3_.refs_1_), channel_id=1, source_target_pairs={{0,4},{1,5},{2,6},{3,7},{4,0},{5,1},{6,2},{7,3},{8,12},{9,13},{10,... | collective-permute-start | bytes 811016 | tf_op jit(solution)/shard_map/ppermute | solution.py:250
  51.2 16.6 %collective-permute-start.17 = (f32[512,128]{1,0:T(8,128)S(1)}, f32[512,128]{1,0:T(8,128)S(1)}, u32[]{:S(2)}, u32[]{:S(2)}) collective-permute-start(f32[512,128]{1,0:T(8,128)S(1)} %get-tuple-element.68.refs_3_.refs_1_), channel_id=1, source_target_pairs={{0,8},{1,9},{2,10},{3,11},{4,12},{5,13},{6,14},{7,15},{8,0},{9,1},... | collective-permute-start | bytes 786440 | tf_op jit(solution)/shard_map/ppermute | solution.py:250
  57.3 18.1 %collective-permute-start.15 = (f32[512,128]{1,0:T(8,128)S(1)}, f32[512,128]{1,0:T(8,128)S(1)}, u32[]{:S(2)}, u32[]{:S(2)}) collective-permute-start(f32[512,128]{1,0:T(8,128)S(1)} %get-tuple-element.72.refs_3_.refs_1_), channel_id=1, source_target_pairs={{0,4},{1,5},{2,6},{3,7},{4,0},{5,1},{6,2},{7,3},{8,12},{9,13},{10,... | collective-permute-start | bytes 786440 | tf_op jit(solution)/shard_map/ppermute | solution.py:250
  65.2 10.3 %collective-permute-start.20 = (f32[272,128]{1,0:T(8,128)S(1)}, f32[272,128]{1,0:T(8,128)S(1)}, u32[]{:S(2)}, u32[]{:S(2)}) collective-permute-start(f32[272,128]{1,0:T(8,128)S(1)} %get-tuple-element.76.refs_3_.refs_1_), channel_id=1, source_target_pairs={{0,8},{1,9},{2,10},{3,11},{4,12},{5,13},{6,14},{7,15},{8,0},{9,1},... | collective-permute-start | bytes 417800 | tf_op jit(solution)/shard_map/ppermute | solution.py:250
  65.7 5.0 %collective-permute-start.16 = (f32[256,128]{1,0:T(8,128)S(1)}, f32[256,128]{1,0:T(8,128)S(1)}, u32[]{:S(2)}, u32[]{:S(2)}) collective-permute-start(f32[256,128]{1,0:T(8,128)S(1)} %get-tuple-element.70.refs_3_.refs_1_), channel_id=1, source_target_pairs={{0,2},{1,3},{2,0},{3,1},{4,6},{5,7},{6,4},{7,5},{8,10},{9,11},{10,... | collective-permute-start | bytes 393224 | tf_op jit(solution)/shard_map/ppermute | solution.py:250
  67.8 11.3 %collective-permute-start.25 = (f32[256,128]{1,0:T(8,128)S(1)}, f32[256,128]{1,0:T(8,128)S(1)}, u32[]{:S(2)}, u32[]{:S(2)}) collective-permute-start(f32[256,128]{1,0:T(8,128)S(1)} %get-tuple-element.77.refs_3_.refs_0_), channel_id=1, source_target_pairs={{0,2},{1,3},{2,4},{3,5},{4,6},{5,7},{6,8},{7,9},{8,10},{9,11},{10,... | collective-permute-start | bytes 393224 | tf_op jit(solution)/shard_map/ppermute | solution.py:250
  67.9 11.2 %collective-permute-start.26 = (f32[256,128]{1,0:T(8,128)S(1)}, f32[256,128]{1,0:T(8,128)S(1)}, u32[]{:S(2)}, u32[]{:S(2)}) collective-permute-start(f32[256,128]{1,0:T(8,128)S(1)} %get-tuple-element.86), channel_id=1, source_target_pairs={{0,1},{1,0},{2,3},{3,2},{4,5},{5,4},{6,7},{7,6},{8,9},{9,8},{10,11... | collective-permute-start | bytes 393224 | tf_op jit(solution)/shard_map/ppermute | solution.py:250
  70.7 9.6 %collective-permute-start.23 = (f32[256,128]{1,0:T(8,128)S(1)}, f32[256,128]{1,0:T(8,128)S(1)}, u32[]{:S(2)}, u32[]{:S(2)}) collective-permute-start(f32[256,128]{1,0:T(8,128)S(1)} %get-tuple-element.78.refs_3_.refs_0_), channel_id=1, source_target_pairs={{0,4},{1,5},{2,6},{3,7},{4,8},{5,9},{6,10},{7,11},{8,12},{9,13},{1... | collective-permute-start | bytes 393224 | tf_op jit(solution)/shard_map/ppermute | solution.py:250
  75.5 13.8 %collective-permute-start.21 = (f32[256,128]{1,0:T(8,128)S(1)}, f32[256,128]{1,0:T(8,128)S(1)}, u32[]{:S(2)}, u32[]{:S(2)}) collective-permute-start(f32[256,128]{1,0:T(8,128)S(1)} %get-tuple-element.82.refs_4_.refs_0_), channel_id=1, source_target_pairs={{0,6},{1,7},{2,8},{3,9},{4,10},{5,11},{6,12},{7,13},{8,14},{9,15},... | collective-permute-start | bytes 393224 | tf_op jit(solution)/shard_map/ppermute | solution.py:250
  77.2 12.3 %collective-permute-start.19 = (f32[256,128]{1,0:T(8,128)S(1)}, f32[256,128]{1,0:T(8,128)S(1)}, u32[]{:S(2)}, u32[]{:S(2)}) collective-permute-start(f32[256,128]{1,0:T(8,128)S(1)} %get-tuple-element.80.refs_3_.refs_1_), channel_id=1, source_target_pairs={{0,8},{1,9},{2,10},{3,11},{4,12},{5,13},{6,14},{7,15},{8,0},{9,1},... | collective-permute-start | bytes 393224 | tf_op jit(solution)/shard_map/ppermute | solution.py:250
  79.1 1.3 %collective-permute-start.24 = (f32[128,128]{1,0:T(8,128)S(1)}, f32[128,128]{1,0:T(8,128)S(1)}, u32[]{:S(2)}, u32[]{:S(2)}) collective-permute-start(f32[128,128]{1,0:T(8,128)S(1)} %get-tuple-element.84), channel_id=1, source_target_pairs={{0,1},{1,0},{2,3},{3,2},{4,5},{5,4},{6,7},{7,6},{8,9},{9,8},{10,11... | collective-permute-start | bytes 196616 | tf_op jit(solution)/shard_map/ppermute | solution.py:250
  79.1 1.5 %collective-permute-start.22 = (f32[128,128]{1,0:T(8,128)S(1)}, f32[128,128]{1,0:T(8,128)S(1)}, u32[]{:S(2)}, u32[]{:S(2)}) collective-permute-start(f32[128,128]{1,0:T(8,128)S(1)} %get-tuple-element.83), channel_id=1, source_target_pairs={{0,1},{1,0},{2,3},{3,2},{4,5},{5,4},{6,7},{7,6},{8,9},{9,8},{10,11... | collective-permute-start | bytes 196616 | tf_op jit(solution)/shard_map/ppermute | solution.py:250

commit v5 on v4

--- a/solution.py
+++ b/solution.py
@@ -109,9 +109,10 @@
             for c in range(CORES):
                 cols = pl.ds(pl.multiple_of(i * wide + c * unit, unit), unit)
                 mine = pl.ds(pl.multiple_of(i * wide + (c ^ core) * unit, unit), unit)
+                block = raw[:, here, cols]
+                turned = block.reshape(sz.count * sz.chunk, unit).T
                 for p in range(per):
-                    rows = pl.ds(pl.multiple_of(g * sz.chunk + p * TILE, TILE), TILE)
-                    f = [raw[k, rows, cols].astype(jnp.float32) for k in range(sz.count)]
+                    f = [block[k, p * TILE : (p + 1) * TILE].astype(jnp.float32) for k in range(sz.count)]
                     for k in range(sz.count):
                         total = None
                         for l in range(sz.count):
@@ -120,11 +121,10 @@
                                 total = term if total is None else total + term
                         to = pl.ds(pl.multiple_of(base + k * sz.chunk + p * TILE, TILE), TILE)
                         right_ref[to, mine] = jnp.where(used[p], total, 0.0).astype(jnp.bfloat16)
-                block = raw[:, here, cols].reshape(sz.count * sz.chunk, unit)
-                left_ref[mine, pl.ds(pl.multiple_of(base, LANES), sz.count * sz.chunk)] = block.T
+                left_ref[mine, pl.ds(pl.multiple_of(base, LANES), sz.count * sz.chunk)] = turned
             return carry
 
-        lax.fori_loop(0, sz.chips, one_chip, 0)
+        lax.fori_loop(0, sz.chips, one_chip, 0, unroll=4)
         rows = pl.ds(pl.multiple_of(base, LANES), sz.count * sz.chunk)
         right_ref[rows, sz.width :] = right_ref[rows, : sz.extended - sz.width]
         return carry

time: 91 us -> 89.8 us (0.987)
  Pallas kernels: 21.2 us -> 20 us
    pallas_call x33, Pallas kernels: 21.2 us -> 20 us  [call(): pl.pallas_call(kernel, in_specs=specs, out_specs=outs or [VMEM] * len(sha...]
where the time goes in v5:
time: 89.8 us; the launch traced here: 89.3 us
  waiting for transfers between devices  37 us (41%)
  starting transfers between devices  31.2 us (35%)
  Pallas kernels  20 us (22%)
  between operations  0.98 us (1%)
    ppermute x27, waiting for transfers between devices, send(): return lax.ppermute(x, AXIS, pairs)  37 us
    ppermute x27, starting transfers between devices, send(): return lax.ppermute(x, AXIS, pairs)  31.2 us
    pallas_call x33, Pallas kernels, call(): pl.pallas_call(kernel, in_specs=specs, out_specs=outs or [VMEM] * len(sha...  20 us
  transfers between devices with their start and end apart: 27, of which 7 were waited for; matrix products, arithmetic and copies ran while one was open for 0% of the time, Pallas kernels for 13%

profile of v5, /device:TPU:0, one launch (start us, length us, event | category | flops | bytes accessed | tf_op | source)
XLA Modules:
  0.0 89.3 jit_solution(8420927635279683820)
XLA Ops:
  0.6 7.4 %first.1 = (bf16[2048,1280]{1,0:T(8,128)(2,1)S(1)}, bf16[1280,2560]{1,0:T(8,128)(2,1)S(1)}, f32[1536,128]{1,0:T(8,128)S(1)}, f32[1536,128]{1,0:T(8,128)S(1)}) custom-call(f32[4,4]{1,0:T(4,128)} %refs_0_.1, s32[1,4]{1,0:T(1,128)} %refs_1_.1, bf16[4,384,2048]{2,1,0:T(8,128)(2,1)} %refs_2_.1), custom_call_target="tpu_custom_call" | custom-call | flops 1342177280 | tf_op jit(solution)/shard_map/first/pallas_call | solution.py:229
  8.0 0.5 collective-permute-start.2
  8.5 0.8 multiply_b.2
  9.4 0.9 multiply_a.2
  10.9 1.5 %multiply_d.1 = (f32[1536,128]{1,0:T(8,128)S(1)}, f32[1536,128]{1,0:T(8,128)S(1)}) custom-call(bf16[2048,1280]{1,0:T(8,128)(2,1)S(1)} %get-tuple-element.46.refs_0_.refs_2_, bf16[1280,2560]{1,0:T(8,128)(2,1)S(1)} %get-tuple-element.47.refs_1_, f32[1536,128]{1,0:T(8,128)S(1)} %sum1_d.1.refs_2_.refs_1_), custom_call_target="tpu_custom_call" | custom-call | flops 1342177280 | tf_op jit(solution)/shard_map/multiply_d/pallas_call | solution.py:229
  12.6 2.9 %collective-permute-start.8 = (f32[1536,128]{1,0:T(8,128)S(1)}, f32[1536,128]{1,0:T(8,128)S(1)}, u32[]{:S(2)}, u32[]{:S(2)}) collective-permute-start(f32[1536,128]{1,0:T(8,128)S(1)} %sum1_d.1.refs_2_.refs_1_), channel_id=1, source_target_pairs={{0,2},{1,3},{2,0},{3,1},{4,6},{5,7},{6,4},{7,5},{8,10},{9,11},{10,... | collective-permute-start | bytes 2359304 | tf_op jit(solution)/shard_map/ppermute | solution.py:250
  15.8 0.9 multiply_b.3
  16.7 0.9 multiply_a.3
  17.6 0.5 collective-permute-start.3
  18.1 0.8 multiply_c.2
  19.1 1.6 %collective-permute-start.6 = (f32[1024,128]{1,0:T(8,128)S(1)}, f32[1024,128]{1,0:T(8,128)S(1)}, u32[]{:S(2)}, u32[]{:S(2)}) collective-permute-start(f32[1024,128]{1,0:T(8,128)S(1)} %sum1_b.1.refs_2_.refs_1_), channel_id=1, source_target_pairs={{0,4},{1,5},{2,6},{3,7},{4,0},{5,1},{6,2},{7,3},{8,12},{9,13},{10,... | collective-permute-start | bytes 1572872 | tf_op jit(solution)/shard_map/ppermute | solution.py:250
  20.9 3.2 %vector.1.refs_2_ = f32[16,128]{1,0:T(8,128)S(1)} custom-call(bf16[2048,1280]{1,0:T(8,128)(2,1)S(1)} %get-tuple-element.46.refs_0_.refs_2_, bf16[1280,2560]{1,0:T(8,128)(2,1)S(1)} %get-tuple-element.47.refs_1_, bf16[1,2048]{1,0:T(2,128)(2,1)S(1)} %reshape.10.refs_2_, f32[1024,128]{1,0:T(8,128)S(1)} %fold_a.1.refs_3_.refs_0_), custom_call_target="tpu_custom_call" | custom-call | tf_op jit(solution)/shard_map/vector/pallas_call | solution.py:229
  24.5 0.9 multiply_c.3
  25.4 0.6 collective-permute-start.13
  26.1 7.8 %collective-permute-done.8.refs_2_ = f32[1536,128]{1,0:T(8,128)S(1)} collective-permute-done((f32[1536,128]{1,0:T(8,128)S(1)}, f32[1536,128]{1,0:T(8,128)S(1)}, u32[]{:S(2)}, u32[]{:S(2)}) %collective-permute-start.8) | collective-permute-done | bytes 786464 | tf_op jit(solution)/shard_map/ppermute | solution.py:250
  34.0 2.2 %collective-permute-start.14 = (f32[768,128]{1,0:T(8,128)S(1)}, f32[768,128]{1,0:T(8,128)S(1)}, u32[]{:S(2)}, u32[]{:S(2)}) collective-permute-start(f32[768,128]{1,0:T(8,128)S(1)} %get-tuple-element.63.refs_3_.refs_1_), channel_id=1, source_target_pairs={{0,4},{1,5},{2,6},{3,7},{4,0},{5,1},{6,2},{7,3},{8,12},{9,13},{10,... | collective-permute-start | bytes 1179656 | tf_op jit(solution)/shard_map/ppermute | solution.py:250
  36.2 1.5 %collective-permute-start.5 = (f32[1024,128]{1,0:T(8,128)S(1)}, f32[1024,128]{1,0:T(8,128)S(1)}, u32[]{:S(2)}, u32[]{:S(2)}) collective-permute-start(f32[1024,128]{1,0:T(8,128)S(1)} %sum1_a.1.refs_2_.refs_1_), channel_id=1, source_target_pairs={{0,2},{1,3},{2,0},{3,1},{4,6},{5,7},{6,4},{7,5},{8,10},{9,11},{10,... | collective-permute-start | bytes 1572872 | tf_op jit(solution)/shard_map/ppermute | solution.py:250
  37.8 2.7 %collective-permute-start.11 = (f32[512,128]{1,0:T(8,128)S(1)}, f32[512,128]{1,0:T(8,128)S(1)}, u32[]{:S(2)}, u32[]{:S(2)}) collective-permute-start(f32[512,128]{1,0:T(8,128)S(1)} %get-tuple-element.65.refs_2_.refs_1_), channel_id=1, source_target_pairs={{0,8},{1,9},{2,10},{3,11},{4,12},{5,13},{6,14},{7,15},{8,0},{9,1},... | collective-permute-start | bytes 786440 | tf_op jit(solution)/shard_map/ppermute | solution.py:250
  40.6 9.2 %collective-permute-done.14.refs_2_ = f32[768,128]{1,0:T(8,128)S(1)} collective-permute-done((f32[768,128]{1,0:T(8,128)S(1)}, f32[768,128]{1,0:T(8,128)S(1)}, u32[]{:S(2)}, u32[]{:S(2)}) %collective-permute-start.14) | collective-permute-done | bytes 393248 | tf_op jit(solution)/shard_map/ppermute | solution.py:250
  50.0 4.0 %collective-permute-start.17 = (f32[512,128]{1,0:T(8,128)S(1)}, f32[512,128]{1,0:T(8,128)S(1)}, u32[]{:S(2)}, u32[]{:S(2)}) collective-permute-start(f32[512,128]{1,0:T(8,128)S(1)} %get-tuple-element.68.refs_3_.refs_1_), channel_id=1, source_target_pairs={{0,8},{1,9},{2,10},{3,11},{4,12},{5,13},{6,14},{7,15},{8,0},{9,1},... | collective-permute-start | bytes 786440 | tf_op jit(solution)/shard_map/ppermute | solution.py:250
  54.1 1.9 %collective-permute-done.5.refs_2_ = f32[1024,128]{1,0:T(8,128)S(1)} collective-permute-done((f32[1024,128]{1,0:T(8,128)S(1)}, f32[1024,128]{1,0:T(8,128)S(1)}, u32[]{:S(2)}, u32[]{:S(2)}) %collective-permute-start.5) | collective-permute-done | bytes 524320 | tf_op jit(solution)/shard_map/ppermute | solution.py:250
  56.1 1.9 %collective-permute-start.15 = (f32[512,128]{1,0:T(8,128)S(1)}, f32[512,128]{1,0:T(8,128)S(1)}, u32[]{:S(2)}, u32[]{:S(2)}) collective-permute-start(f32[512,128]{1,0:T(8,128)S(1)} %get-tuple-element.72.refs_3_.refs_1_), channel_id=1, source_target_pairs={{0,4},{1,5},{2,6},{3,7},{4,0},{5,1},{6,2},{7,3},{8,12},{9,13},{10,... | collective-permute-start | bytes 786440 | tf_op jit(solution)/shard_map/ppermute | solution.py:250
  58.0 6.0 %collective-permute-done.18.refs_2_ = f32[528,128]{1,0:T(8,128)S(1)} collective-permute-done((f32[528,128]{1,0:T(8,128)S(1)}, f32[528,128]{1,0:T(8,128)S(1)}, u32[]{:S(2)}, u32[]{:S(2)}) %collective-permute-start.18) | collective-permute-done | bytes 270368 | tf_op jit(solution)/shard_map/ppermute | solution.py:250
  64.0 0.6 collective-permute-start.20
  64.5 2.0 %collective-permute-start.16 = (f32[256,128]{1,0:T(8,128)S(1)}, f32[256,128]{1,0:T(8,128)S(1)}, u32[]{:S(2)}, u32[]{:S(2)}) collective-permute-start(f32[256,128]{1,0:T(8,128)S(1)} %get-tuple-element.70.refs_3_.refs_1_), channel_id=1, source_target_pairs={{0,2},{1,3},{2,0},{3,1},{4,6},{5,7},{6,4},{7,5},{8,10},{9,11},{10,... | collective-permute-start | bytes 393224 | tf_op jit(solution)/shard_map/ppermute | solution.py:250
  66.7 2.8 %collective-permute-done.16.refs_2_ = f32[256,128]{1,0:T(8,128)S(1)} collective-permute-done((f32[256,128]{1,0:T(8,128)S(1)}, f32[256,128]{1,0:T(8,128)S(1)}, u32[]{:S(2)}, u32[]{:S(2)}) %collective-permute-start.16) | collective-permute-done | bytes 131104 | tf_op jit(solution)/shard_map/ppermute | solution.py:250
  69.5 4.6 %collective-permute-start.23 = (f32[256,128]{1,0:T(8,128)S(1)}, f32[256,128]{1,0:T(8,128)S(1)}, u32[]{:S(2)}, u32[]{:S(2)}) collective-permute-start(f32[256,128]{1,0:T(8,128)S(1)} %get-tuple-element.78.refs_3_.refs_0_), channel_id=1, source_target_pairs={{0,4},{1,5},{2,6},{3,7},{4,8},{5,9},{6,10},{7,11},{8,12},{9,13},{1... | collective-permute-start | bytes 393224 | tf_op jit(solution)/shard_map/ppermute | solution.py:250
  74.3 1.7 %collective-permute-start.21 = (f32[256,128]{1,0:T(8,128)S(1)}, f32[256,128]{1,0:T(8,128)S(1)}, u32[]{:S(2)}, u32[]{:S(2)}) collective-permute-start(f32[256,128]{1,0:T(8,128)S(1)} %get-tuple-element.82.refs_4_.refs_0_), channel_id=1, source_target_pairs={{0,6},{1,7},{2,8},{3,9},{4,10},{5,11},{6,12},{7,13},{8,14},{9,15},... | collective-permute-start | bytes 393224 | tf_op jit(solution)/shard_map/ppermute | solution.py:250
  76.0 1.9 %collective-permute-start.19 = (f32[256,128]{1,0:T(8,128)S(1)}, f32[256,128]{1,0:T(8,128)S(1)}, u32[]{:S(2)}, u32[]{:S(2)}) collective-permute-start(f32[256,128]{1,0:T(8,128)S(1)} %get-tuple-element.80.refs_3_.refs_1_), channel_id=1, source_target_pairs={{0,8},{1,9},{2,10},{3,11},{4,12},{5,13},{6,14},{7,15},{8,0},{9,1},... | collective-permute-start | bytes 393224 | tf_op jit(solution)/shard_map/ppermute | solution.py:250
  77.9 0.5 collective-permute-start.22
  79.4 8.7 %collective-permute-done.21.refs_1_ = f32[256,128]{1,0:T(8,128)S(1)} collective-permute-done((f32[256,128]{1,0:T(8,128)S(1)}, f32[256,128]{1,0:T(8,128)S(1)}, u32[]{:S(2)}, u32[]{:S(2)}) %collective-permute-start.21) | collective-permute-done | bytes 131104 | tf_op jit(solution)/shard_map/ppermute | solution.py:250
  88.3 1.1 %place_a.1 = (f32[128,2048]{1,0:T(8,128)S(1)}, f32[128,2048]{1,0:T(8,128)}, f32[16,128]{1,0:T(8,128)}) custom-call(f32[256,128]{1,0:T(8,128)S(1)} %done_a.1.refs_0_.refs_3_, f32[16,128]{1,0:T(8,128)S(1)} %get-tuple-element.87.refs_1_, f32[128,2048]{1,0:T(8,128)S(1)} %place_c.1.refs_3_.refs_2_, ...), custom_call_target="tpu_custom_call", output_to_operand_aliasing={{0}: (2, {})} | custom-call | tf_op jit(solution)/shard_map/place_a/pallas_call | solution.py:229
  (60 shorter events, 3.8 us)
Async XLA Ops:
  8.0 2.8 %collective-permute-start.2 = (f32[1536,128]{1,0:T(8,128)S(1)}, f32[1536,128]{1,0:T(8,128)S(1)}, u32[]{:S(2)}, u32[]{:S(2)}) collective-permute-start(f32[1536,128]{1,0:T(8,128)S(1)} %get-tuple-element.53), channel_id=1, source_target_pairs={{0,1},{1,0},{2,3},{3,2},{4,5},{5,4},{6,7},{7,6},{8,9},{9,8},{10,11... | collective-permute-start | bytes 2359304 | tf_op jit(solution)/shard_map/ppermute | solution.py:250
  10.2 5.3 %collective-permute-start.1 = (f32[1024,128]{1,0:T(8,128)S(1)}, f32[1024,128]{1,0:T(8,128)S(1)}, u32[]{:S(2)}, u32[]{:S(2)}) collective-permute-start(f32[1024,128]{1,0:T(8,128)S(1)} %get-tuple-element.51.refs_2_), channel_id=1, source_target_pairs={{0,1},{1,0},{2,3},{3,2},{4,5},{5,4},{6,7},{7,6},{8,9},{9,8},{10,11... | collective-permute-start | bytes 1572872 | tf_op jit(solution)/shard_map/ppermute | solution.py:250
  10.4 5.3 %collective-permute-start = (f32[1024,128]{1,0:T(8,128)S(1)}, f32[1024,128]{1,0:T(8,128)S(1)}, u32[]{:S(2)}, u32[]{:S(2)}) collective-permute-start(f32[1024,128]{1,0:T(8,128)S(1)} %get-tuple-element.49.refs_2_), channel_id=1, source_target_pairs={{0,1},{1,0},{2,3},{3,2},{4,5},{5,4},{6,7},{7,6},{8,9},{9,8},{10,11... | collective-permute-start | bytes 1572872 | tf_op jit(solution)/shard_map/ppermute | solution.py:250
  12.5 11.9 %collective-permute-start.7 = (f32[1536,128]{1,0:T(8,128)S(1)}, f32[1536,128]{1,0:T(8,128)S(1)}, u32[]{:S(2)}, u32[]{:S(2)}) collective-permute-start(f32[1536,128]{1,0:T(8,128)S(1)} %get-tuple-element.54.refs_2_), channel_id=1, source_target_pairs={{0,1},{1,0},{2,3},{3,2},{4,5},{5,4},{6,7},{7,6},{8,9},{9,8},{10,11... | collective-permute-start | bytes 2359304 | tf_op jit(solution)/shard_map/ppermute | solution.py:250
  12.6 21.3 %collective-permute-start.8 = (f32[1536,128]{1,0:T(8,128)S(1)}, f32[1536,128]{1,0:T(8,128)S(1)}, u32[]{:S(2)}, u32[]{:S(2)}) collective-permute-start(f32[1536,128]{1,0:T(8,128)S(1)} %sum1_d.1.refs_2_.refs_1_), channel_id=1, source_target_pairs={{0,2},{1,3},{2,0},{3,1},{4,6},{5,7},{6,4},{7,5},{8,10},{9,11},{10,... | collective-permute-start | bytes 2359304 | tf_op jit(solution)/shard_map/ppermute | solution.py:250
  16.6 2.4 %collective-permute-start.4 = (f32[1024,128]{1,0:T(8,128)S(1)}, f32[1024,128]{1,0:T(8,128)S(1)}, u32[]{:S(2)}, u32[]{:S(2)}) collective-permute-start(f32[1024,128]{1,0:T(8,128)S(1)} %get-tuple-element.55.refs_2_), channel_id=1, source_target_pairs={{0,1},{1,0},{2,3},{3,2},{4,5},{5,4},{6,7},{7,6},{8,9},{9,8},{10,11... | collective-permute-start | bytes 1572872 | tf_op jit(solution)/shard_map/ppermute | solution.py:250
  17.6 3.1 %copy-start = (bf16[2048]{0:T(1024)(128)(2,1)S(1)}, bf16[2048]{0:T(1024)(128)(2,1)}, u32[]{:S(2)}) copy-start(bf16[2048]{0:T(1024)(128)(2,1)} %param.7) | copy-start | bytes 12292
  17.6 3.2 %collective-permute-start.3 = (f32[1024,128]{1,0:T(8,128)S(1)}, f32[1024,128]{1,0:T(8,128)S(1)}, u32[]{:S(2)}, u32[]{:S(2)}) collective-permute-start(f32[1024,128]{1,0:T(8,128)S(1)} %get-tuple-element.57.refs_2_), channel_id=1, source_target_pairs={{0,1},{1,0},{2,3},{3,2},{4,5},{5,4},{6,7},{7,6},{8,9},{9,8},{10,11... | collective-permute-start | bytes 1572872 | tf_op jit(solution)/shard_map/ppermute | solution.py:250
  19.0 6.4 %collective-permute-start.9 = (f32[1024,128]{1,0:T(8,128)S(1)}, f32[1024,128]{1,0:T(8,128)S(1)}, u32[]{:S(2)}, u32[]{:S(2)}) collective-permute-start(f32[1024,128]{1,0:T(8,128)S(1)} %get-tuple-element.59.refs_2_), channel_id=1, source_target_pairs={{0,1},{1,0},{2,3},{3,2},{4,5},{5,4},{6,7},{7,6},{8,9},{9,8},{10,11... | collective-permute-start | bytes 1572872 | tf_op jit(solution)/shard_map/ppermute | solution.py:250
  19.1 18.7 %collective-permute-start.6 = (f32[1024,128]{1,0:T(8,128)S(1)}, f32[1024,128]{1,0:T(8,128)S(1)}, u32[]{:S(2)}, u32[]{:S(2)}) collective-permute-start(f32[1024,128]{1,0:T(8,128)S(1)} %sum1_b.1.refs_2_.refs_1_), channel_id=1, source_target_pairs={{0,4},{1,5},{2,6},{3,7},{4,0},{5,1},{6,2},{7,3},{8,12},{9,13},{10,... | collective-permute-start | bytes 1572872 | tf_op jit(solution)/shard_map/ppermute | solution.py:250
  24.1 1.2 %collective-permute-start.10 = (f32[16,128]{1,0:T(8,128)S(1)}, f32[16,128]{1,0:T(8,128)S(1)}, u32[]{:S(2)}, u32[]{:S(2)}) collective-permute-start(f32[16,128]{1,0:T(8,128)S(1)} %vector.1.refs_2_), channel_id=1, source_target_pairs={{0,1},{1,0},{2,3},{3,2},{4,5},{5,4},{6,7},{7,6},{8,9},{9,8},{10,11... | collective-permute-start | bytes 24584 | tf_op jit(solution)/shard_map/ppermute | solution.py:250
  25.4 24.4 %collective-permute-start.13 = (f32[1040,128]{1,0:T(8,128)S(1)}, f32[1040,128]{1,0:T(8,128)S(1)}, u32[]{:S(2)}, u32[]{:S(2)}) collective-permute-start(f32[1040,128]{1,0:T(8,128)S(1)} %sum1_c.1.refs_3_.refs_1_), channel_id=1, source_target_pairs={{0,2},{1,3},{2,0},{3,1},{4,6},{5,7},{6,4},{7,5},{8,10},{9,11},{10,... | collective-permute-start | bytes 1597448 | tf_op jit(solution)/shard_map/ppermute | solution.py:250
  26.0 14.5 %collective-permute-start.12 = (f32[1024,128]{1,0:T(8,128)S(1)}, f32[1024,128]{1,0:T(8,128)S(1)}, u32[]{:S(2)}, u32[]{:S(2)}) collective-permute-start(f32[1024,128]{1,0:T(8,128)S(1)} %get-tuple-element.62.refs_4_), channel_id=1, source_target_pairs={{0,1},{1,0},{2,3},{3,2},{4,5},{5,4},{6,7},{7,6},{8,9},{9,8},{10,11... | collective-permute-start | bytes 1572872 | tf_op jit(solution)/shard_map/ppermute | solution.py:250
  34.0 15.7 %collective-permute-start.14 = (f32[768,128]{1,0:T(8,128)S(1)}, f32[768,128]{1,0:T(8,128)S(1)}, u32[]{:S(2)}, u32[]{:S(2)}) collective-permute-start(f32[768,128]{1,0:T(8,128)S(1)} %get-tuple-element.63.refs_3_.refs_1_), channel_id=1, source_target_pairs={{0,4},{1,5},{2,6},{3,7},{4,0},{5,1},{6,2},{7,3},{8,12},{9,13},{10,... | collective-permute-start | bytes 1179656 | tf_op jit(solution)/shard_map/ppermute | solution.py:250
  36.2 19.8 %collective-permute-start.5 = (f32[1024,128]{1,0:T(8,128)S(1)}, f32[1024,128]{1,0:T(8,128)S(1)}, u32[]{:S(2)}, u32[]{:S(2)}) collective-permute-start(f32[1024,128]{1,0:T(8,128)S(1)} %sum1_a.1.refs_2_.refs_1_), channel_id=1, source_target_pairs={{0,2},{1,3},{2,0},{3,1},{4,6},{5,7},{6,4},{7,5},{8,10},{9,11},{10,... | collective-permute-start | bytes 1572872 | tf_op jit(solution)/shard_map/ppermute | solution.py:250
  37.8 16.2 %collective-permute-start.11 = (f32[512,128]{1,0:T(8,128)S(1)}, f32[512,128]{1,0:T(8,128)S(1)}, u32[]{:S(2)}, u32[]{:S(2)}) collective-permute-start(f32[512,128]{1,0:T(8,128)S(1)} %get-tuple-element.65.refs_2_.refs_1_), channel_id=1, source_target_pairs={{0,8},{1,9},{2,10},{3,11},{4,12},{5,13},{6,14},{7,15},{8,0},{9,1},... | collective-permute-start | bytes 786440 | tf_op jit(solution)/shard_map/ppermute | solution.py:250
  49.9 14.0 %collective-permute-start.18 = (f32[528,128]{1,0:T(8,128)S(1)}, f32[528,128]{1,0:T(8,128)S(1)}, u32[]{:S(2)}, u32[]{:S(2)}) collective-permute-start(f32[528,128]{1,0:T(8,128)S(1)} %get-tuple-element.69.refs_3_.refs_1_), channel_id=1, source_target_pairs={{0,4},{1,5},{2,6},{3,7},{4,0},{5,1},{6,2},{7,3},{8,12},{9,13},{10,... | collective-permute-start | bytes 811016 | tf_op jit(solution)/shard_map/ppermute | solution.py:250
  50.0 16.6 %collective-permute-start.17 = (f32[512,128]{1,0:T(8,128)S(1)}, f32[512,128]{1,0:T(8,128)S(1)}, u32[]{:S(2)}, u32[]{:S(2)}) collective-permute-start(f32[512,128]{1,0:T(8,128)S(1)} %get-tuple-element.68.refs_3_.refs_1_), channel_id=1, source_target_pairs={{0,8},{1,9},{2,10},{3,11},{4,12},{5,13},{6,14},{7,15},{8,0},{9,1},... | collective-permute-start | bytes 786440 | tf_op jit(solution)/shard_map/ppermute | solution.py:250
  56.1 18.1 %collective-permute-start.15 = (f32[512,128]{1,0:T(8,128)S(1)}, f32[512,128]{1,0:T(8,128)S(1)}, u32[]{:S(2)}, u32[]{:S(2)}) collective-permute-start(f32[512,128]{1,0:T(8,128)S(1)} %get-tuple-element.72.refs_3_.refs_1_), channel_id=1, source_target_pairs={{0,4},{1,5},{2,6},{3,7},{4,0},{5,1},{6,2},{7,3},{8,12},{9,13},{10,... | collective-permute-start | bytes 786440 | tf_op jit(solution)/shard_map/ppermute | solution.py:250
  64.0 10.3 %collective-permute-start.20 = (f32[272,128]{1,0:T(8,128)S(1)}, f32[272,128]{1,0:T(8,128)S(1)}, u32[]{:S(2)}, u32[]{:S(2)}) collective-permute-start(f32[272,128]{1,0:T(8,128)S(1)} %get-tuple-element.76.refs_3_.refs_1_), channel_id=1, source_target_pairs={{0,8},{1,9},{2,10},{3,11},{4,12},{5,13},{6,14},{7,15},{8,0},{9,1},... | collective-permute-start | bytes 417800 | tf_op jit(solution)/shard_map/ppermute | solution.py:250
  64.5 5.0 %collective-permute-start.16 = (f32[256,128]{1,0:T(8,128)S(1)}, f32[256,128]{1,0:T(8,128)S(1)}, u32[]{:S(2)}, u32[]{:S(2)}) collective-permute-start(f32[256,128]{1,0:T(8,128)S(1)} %get-tuple-element.70.refs_3_.refs_1_), channel_id=1, source_target_pairs={{0,2},{1,3},{2,0},{3,1},{4,6},{5,7},{6,4},{7,5},{8,10},{9,11},{10,... | collective-permute-start | bytes 393224 | tf_op jit(solution)/shard_map/ppermute | solution.py:250
  66.6 11.3 %collective-permute-start.25 = (f32[256,128]{1,0:T(8,128)S(1)}, f32[256,128]{1,0:T(8,128)S(1)}, u32[]{:S(2)}, u32[]{:S(2)}) collective-permute-start(f32[256,128]{1,0:T(8,128)S(1)} %get-tuple-element.77.refs_3_.refs_0_), channel_id=1, source_target_pairs={{0,2},{1,3},{2,4},{3,5},{4,6},{5,7},{6,8},{7,9},{8,10},{9,11},{10,... | collective-permute-start | bytes 393224 | tf_op jit(solution)/shard_map/ppermute | solution.py:250
  66.7 11.2 %collective-permute-start.26 = (f32[256,128]{1,0:T(8,128)S(1)}, f32[256,128]{1,0:T(8,128)S(1)}, u32[]{:S(2)}, u32[]{:S(2)}) collective-permute-start(f32[256,128]{1,0:T(8,128)S(1)} %get-tuple-element.86), channel_id=1, source_target_pairs={{0,1},{1,0},{2,3},{3,2},{4,5},{5,4},{6,7},{7,6},{8,9},{9,8},{10,11... | collective-permute-start | bytes 393224 | tf_op jit(solution)/shard_map/ppermute | solution.py:250
  69.5 9.6 %collective-permute-start.23 = (f32[256,128]{1,0:T(8,128)S(1)}, f32[256,128]{1,0:T(8,128)S(1)}, u32[]{:S(2)}, u32[]{:S(2)}) collective-permute-start(f32[256,128]{1,0:T(8,128)S(1)} %get-tuple-element.78.refs_3_.refs_0_), channel_id=1, source_target_pairs={{0,4},{1,5},{2,6},{3,7},{4,8},{5,9},{6,10},{7,11},{8,12},{9,13},{1... | collective-permute-start | bytes 393224 | tf_op jit(solution)/shard_map/ppermute | solution.py:250
  74.3 13.8 %collective-permute-start.21 = (f32[256,128]{1,0:T(8,128)S(1)}, f32[256,128]{1,0:T(8,128)S(1)}, u32[]{:S(2)}, u32[]{:S(2)}) collective-permute-start(f32[256,128]{1,0:T(8,128)S(1)} %get-tuple-element.82.refs_4_.refs_0_), channel_id=1, source_target_pairs={{0,6},{1,7},{2,8},{3,9},{4,10},{5,11},{6,12},{7,13},{8,14},{9,15},... | collective-permute-start | bytes 393224 | tf_op jit(solution)/shard_map/ppermute | solution.py:250
  76.0 12.3 %collective-permute-start.19 = (f32[256,128]{1,0:T(8,128)S(1)}, f32[256,128]{1,0:T(8,128)S(1)}, u32[]{:S(2)}, u32[]{:S(2)}) collective-permute-start(f32[256,128]{1,0:T(8,128)S(1)} %get-tuple-element.80.refs_3_.refs_1_), channel_id=1, source_target_pairs={{0,8},{1,9},{2,10},{3,11},{4,12},{5,13},{6,14},{7,15},{8,0},{9,1},... | collective-permute-start | bytes 393224 | tf_op jit(solution)/shard_map/ppermute | solution.py:250
  77.9 1.3 %collective-permute-start.24 = (f32[128,128]{1,0:T(8,128)S(1)}, f32[128,128]{1,0:T(8,128)S(1)}, u32[]{:S(2)}, u32[]{:S(2)}) collective-permute-start(f32[128,128]{1,0:T(8,128)S(1)} %get-tuple-element.84), channel_id=1, source_target_pairs={{0,1},{1,0},{2,3},{3,2},{4,5},{5,4},{6,7},{7,6},{8,9},{9,8},{10,11... | collective-permute-start | bytes 196616 | tf_op jit(solution)/shard_map/ppermute | solution.py:250
  77.9 1.5 %collective-permute-start.22 = (f32[128,128]{1,0:T(8,128)S(1)}, f32[128,128]{1,0:T(8,128)S(1)}, u32[]{:S(2)}, u32[]{:S(2)}) collective-permute-start(f32[128,128]{1,0:T(8,128)S(1)} %get-tuple-element.83), channel_id=1, source_target_pairs={{0,1},{1,0},{2,3},{3,2},{4,5},{5,4},{6,7},{7,6},{8,9},{9,8},{10,11... | collective-permute-start | bytes 196616 | tf_op jit(solution)/shard_map/ppermute | solution.py:250

commit v6 on v5

--- a/solution.py
+++ b/solution.py
@@ -26,11 +26,11 @@
 SPLIT = "abcd"
 SWAPPERS = "bcd"
 LAST = "a"
-CARRIER = "c"
+CARRIER = "b"
 ORDER = (
-    *("Kd1", "Kb1", "Ka1", "d1", "Kd0", "a1", "b1", "Kb0", "Ka0", "Kc1", "fb", "fa", "V", "fd"),
-    *("Kc0", "c1", "d2", "b2", "fc", "d3", "c2", "b3", "a2", "c3", "d4", "b4", "a3", "c4"),
-    *("d5", "b5", "c5", "a4", "a5"),
+    *("Kd1", "Kd0", "Kb1", "d1", "Kb0", "Ka1", "V", "Kc0", "fb", "b1", "fd", "Kc1", "c1", "Ka0"),
+    *("a1", "fc", "d2", "b2", "c2", "d3", "fa", "b3", "a2", "c3", "d4", "b4", "a3", "c4"),
+    *("b5", "c5", "d5", "a4", "a5"),
 )
 
 

time: 89.8 us -> 89.4 us (level)
  transfers between devices with their start and end apart: 27 -> 27, of which waited for: 7 -> 12; matrix products, arithmetic and copies ran while one was open for 0% -> 0% of each run, Pallas kernels for 13% -> 13%
where the time goes in v6:
time: 89.4 us; the launch traced here: 89.3 us
  waiting for transfers between devices  37.5 us (42%)
  starting transfers between devices  30.6 us (34%)
  Pallas kernels  20 us (22%)
  between operations  0.99 us (1%)
    ppermute x27, waiting for transfers between devices, send(): return lax.ppermute(x, AXIS, pairs)  37.5 us
    ppermute x27, starting transfers between devices, send(): return lax.ppermute(x, AXIS, pairs)  30.6 us
    pallas_call x33, Pallas kernels, call(): pl.pallas_call(kernel, in_specs=specs, out_specs=outs or [VMEM] * len(sha...  20 us
  transfers between devices with their start and end apart: 27, of which 12 were waited for; matrix products, arithmetic and copies ran while one was open for 0% of the time, Pallas kernels for 13%

profile of v6, /device:TPU:0, one launch (start us, length us, event | category | flops | bytes accessed | tf_op | source)
XLA Modules:
  0.0 89.3 jit_solution(9360253902006063227)
XLA Ops:
  0.6 7.4 %first.1 = (bf16[2048,1280]{1,0:T(8,128)(2,1)S(1)}, bf16[1280,2560]{1,0:T(8,128)(2,1)S(1)}, f32[1536,128]{1,0:T(8,128)S(1)}, f32[1536,128]{1,0:T(8,128)S(1)}) custom-call(f32[4,4]{1,0:T(4,128)} %refs_0_.1, s32[1,4]{1,0:T(1,128)} %refs_1_.1, bf16[4,384,2048]{2,1,0:T(8,128)(2,1)} %refs_2_.1), custom_call_target="tpu_custom_call" | custom-call | flops 1342177280 | tf_op jit(solution)/shard_map/first/pallas_call | solution.py:229
  8.5 1.5 %multiply_d.1 = (f32[1536,128]{1,0:T(8,128)S(1)}, f32[1536,128]{1,0:T(8,128)S(1)}) custom-call(bf16[2048,1280]{1,0:T(8,128)(2,1)S(1)} %get-tuple-element.46.refs_0_.refs_2_, bf16[1280,2560]{1,0:T(8,128)(2,1)S(1)} %get-tuple-element.47.refs_1_, bf16[2048,1280]{1,0:T(8,128)(2,1)S(1)} %get-tuple-element.46.refs_0_.refs_2_), custom_call_target="tpu_custom_call" | custom-call | flops 1342177280 | tf_op jit(solution)/shard_map/multiply_d/pallas_call | solution.py:229
  10.2 0.8 multiply_b.2
  11.2 0.9 multiply_b.3
  12.6 3.0 %collective-permute-start.7 = (f32[1536,128]{1,0:T(8,128)S(1)}, f32[1536,128]{1,0:T(8,128)S(1)}, u32[]{:S(2)}, u32[]{:S(2)}) collective-permute-start(f32[1536,128]{1,0:T(8,128)S(1)} %sum1_d.1.refs_2_.refs_1_), channel_id=1, source_target_pairs={{0,2},{1,3},{2,0},{3,1},{4,6},{5,7},{6,4},{7,5},{8,10},{9,11},{10,... | collective-permute-start | bytes 2359304 | tf_op jit(solution)/shard_map/ppermute | solution.py:250
  15.7 0.8 multiply_a.2
  16.5 3.2 %vector.1.refs_2_ = f32[16,128]{1,0:T(8,128)S(1)} custom-call(bf16[2048,1280]{1,0:T(8,128)(2,1)S(1)} %get-tuple-element.46.refs_0_.refs_2_, bf16[1280,2560]{1,0:T(8,128)(2,1)S(1)} %get-tuple-element.47.refs_1_, bf16[1,2048]{1,0:T(2,128)(2,1)S(1)} %reshape.10.refs_2_, f32[1024,128]{1,0:T(8,128)S(1)} %get-tuple-element.55.refs_3_), custom_call_target="tpu_custom_call" | custom-call | tf_op jit(solution)/shard_map/vector/pallas_call | solution.py:229
  19.8 0.9 multiply_c.2
  21.2 0.9 multiply_c.3
  22.9 1.6 %collective-permute-start.12 = (f32[1040,128]{1,0:T(8,128)S(1)}, f32[1040,128]{1,0:T(8,128)S(1)}, u32[]{:S(2)}, u32[]{:S(2)}) collective-permute-start(f32[1040,128]{1,0:T(8,128)S(1)} %sum1_b.1.refs_2_.refs_1_), channel_id=1, source_target_pairs={{0,4},{1,5},{2,6},{3,7},{4,0},{5,1},{6,2},{7,3},{8,12},{9,13},{10,... | collective-permute-start | bytes 1597448 | tf_op jit(solution)/shard_map/ppermute | solution.py:250
  25.2 0.8 multiply_a.3
  26.2 1.6 %collective-permute-start.13 = (f32[1024,128]{1,0:T(8,128)S(1)}, f32[1024,128]{1,0:T(8,128)S(1)}, u32[]{:S(2)}, u32[]{:S(2)}) collective-permute-start(f32[1024,128]{1,0:T(8,128)S(1)} %sum1_a.1.refs_2_.refs_1_), channel_id=1, source_target_pairs={{0,2},{1,3},{2,0},{3,1},{4,6},{5,7},{6,4},{7,5},{8,10},{9,11},{10,... | collective-permute-start | bytes 1572872 | tf_op jit(solution)/shard_map/ppermute | solution.py:250
  27.9 6.1 %collective-permute-done.7.refs_2_ = f32[1536,128]{1,0:T(8,128)S(1)} collective-permute-done((f32[1536,128]{1,0:T(8,128)S(1)}, f32[1536,128]{1,0:T(8,128)S(1)}, u32[]{:S(2)}, u32[]{:S(2)}) %collective-permute-start.7) | collective-permute-done | bytes 786464 | tf_op jit(solution)/shard_map/ppermute | solution.py:250
  34.1 2.2 %collective-permute-start.10 = (f32[768,128]{1,0:T(8,128)S(1)}, f32[768,128]{1,0:T(8,128)S(1)}, u32[]{:S(2)}, u32[]{:S(2)}) collective-permute-start(f32[768,128]{1,0:T(8,128)S(1)} %get-tuple-element.65.refs_3_.refs_1_), channel_id=1, source_target_pairs={{0,4},{1,5},{2,6},{3,7},{4,0},{5,1},{6,2},{7,3},{8,12},{9,13},{10,... | collective-permute-start | bytes 1179656 | tf_op jit(solution)/shard_map/ppermute | solution.py:250
  36.3 1.6 %collective-permute-done.12.refs_2_ = f32[1040,128]{1,0:T(8,128)S(1)} collective-permute-done((f32[1040,128]{1,0:T(8,128)S(1)}, f32[1040,128]{1,0:T(8,128)S(1)}, u32[]{:S(2)}, u32[]{:S(2)}) %collective-permute-start.12) | collective-permute-done | bytes 532512 | tf_op jit(solution)/shard_map/ppermute | solution.py:250
  37.9 2.7 %collective-permute-start.14 = (f32[528,128]{1,0:T(8,128)S(1)}, f32[528,128]{1,0:T(8,128)S(1)}, u32[]{:S(2)}, u32[]{:S(2)}) collective-permute-start(f32[528,128]{1,0:T(8,128)S(1)} %get-tuple-element.66.refs_3_.refs_1_), channel_id=1, source_target_pairs={{0,8},{1,9},{2,10},{3,11},{4,12},{5,13},{6,14},{7,15},{8,0},{9,1},... | collective-permute-start | bytes 811016 | tf_op jit(solution)/shard_map/ppermute | solution.py:250
  40.6 4.6 %collective-permute-done.11.refs_2_ = f32[1024,128]{1,0:T(8,128)S(1)} collective-permute-done((f32[1024,128]{1,0:T(8,128)S(1)}, f32[1024,128]{1,0:T(8,128)S(1)}, u32[]{:S(2)}, u32[]{:S(2)}) %collective-permute-start.11) | collective-permute-done | bytes 524320 | tf_op jit(solution)/shard_map/ppermute | solution.py:250
  45.3 2.2 %collective-permute-start.18 = (f32[512,128]{1,0:T(8,128)S(1)}, f32[512,128]{1,0:T(8,128)S(1)}, u32[]{:S(2)}, u32[]{:S(2)}) collective-permute-start(f32[512,128]{1,0:T(8,128)S(1)} %get-tuple-element.67.refs_3_.refs_1_), channel_id=1, source_target_pairs={{0,4},{1,5},{2,6},{3,7},{4,0},{5,1},{6,2},{7,3},{8,12},{9,13},{10,... | collective-permute-start | bytes 786440 | tf_op jit(solution)/shard_map/ppermute | solution.py:250
  47.5 4.6 %collective-permute-done.10.refs_2_ = f32[768,128]{1,0:T(8,128)S(1)} collective-permute-done((f32[768,128]{1,0:T(8,128)S(1)}, f32[768,128]{1,0:T(8,128)S(1)}, u32[]{:S(2)}, u32[]{:S(2)}) %collective-permute-start.10) | collective-permute-done | bytes 393248 | tf_op jit(solution)/shard_map/ppermute | solution.py:250
  52.1 2.2 %collective-permute-start.17 = (f32[512,128]{1,0:T(8,128)S(1)}, f32[512,128]{1,0:T(8,128)S(1)}, u32[]{:S(2)}, u32[]{:S(2)}) collective-permute-start(f32[512,128]{1,0:T(8,128)S(1)} %get-tuple-element.68.refs_2_.refs_1_), channel_id=1, source_target_pairs={{0,8},{1,9},{2,10},{3,11},{4,12},{5,13},{6,14},{7,15},{8,0},{9,1},... | collective-permute-start | bytes 786440 | tf_op jit(solution)/shard_map/ppermute | solution.py:250
  54.5 1.4 %collective-permute-done.13.refs_2_ = f32[1024,128]{1,0:T(8,128)S(1)} collective-permute-done((f32[1024,128]{1,0:T(8,128)S(1)}, f32[1024,128]{1,0:T(8,128)S(1)}, u32[]{:S(2)}, u32[]{:S(2)}) %collective-permute-start.13) | collective-permute-done | bytes 524320 | tf_op jit(solution)/shard_map/ppermute | solution.py:250
  56.0 1.9 %collective-permute-start.15 = (f32[512,128]{1,0:T(8,128)S(1)}, f32[512,128]{1,0:T(8,128)S(1)}, u32[]{:S(2)}, u32[]{:S(2)}) collective-permute-start(f32[512,128]{1,0:T(8,128)S(1)} %get-tuple-element.72.refs_3_.refs_1_), channel_id=1, source_target_pairs={{0,4},{1,5},{2,6},{3,7},{4,0},{5,1},{6,2},{7,3},{8,12},{9,13},{10,... | collective-permute-start | bytes 786440 | tf_op jit(solution)/shard_map/ppermute | solution.py:250
  57.9 3.2 %collective-permute-start.16 = (f32[272,128]{1,0:T(8,128)S(1)}, f32[272,128]{1,0:T(8,128)S(1)}, u32[]{:S(2)}, u32[]{:S(2)}) collective-permute-start(f32[272,128]{1,0:T(8,128)S(1)} %get-tuple-element.70.refs_3_.refs_1_), channel_id=1, source_target_pairs={{0,2},{1,3},{2,0},{3,1},{4,6},{5,7},{6,4},{7,5},{8,10},{9,11},{10,... | collective-permute-start | bytes 417800 | tf_op jit(solution)/shard_map/ppermute | solution.py:250
  61.0 1.2 %collective-permute-done.18.refs_2_ = f32[512,128]{1,0:T(8,128)S(1)} collective-permute-done((f32[512,128]{1,0:T(8,128)S(1)}, f32[512,128]{1,0:T(8,128)S(1)}, u32[]{:S(2)}, u32[]{:S(2)}) %collective-permute-start.18) | collective-permute-done | bytes 262176 | tf_op jit(solution)/shard_map/ppermute | solution.py:250
  62.3 1.0 %collective-permute-start.22 = (f32[256,128]{1,0:T(8,128)S(1)}, f32[256,128]{1,0:T(8,128)S(1)}, u32[]{:S(2)}, u32[]{:S(2)}) collective-permute-start(f32[256,128]{1,0:T(8,128)S(1)} %get-tuple-element.76.refs_3_.refs_1_), channel_id=1, source_target_pairs={{0,8},{1,9},{2,10},{3,11},{4,12},{5,13},{6,14},{7,15},{8,0},{9,1},... | collective-permute-start | bytes 393224 | tf_op jit(solution)/shard_map/ppermute | solution.py:250
  63.3 3.0 %collective-permute-done.17.refs_2_ = f32[512,128]{1,0:T(8,128)S(1)} collective-permute-done((f32[512,128]{1,0:T(8,128)S(1)}, f32[512,128]{1,0:T(8,128)S(1)}, u32[]{:S(2)}, u32[]{:S(2)}) %collective-permute-start.17) | collective-permute-done | bytes 262176 | tf_op jit(solution)/shard_map/ppermute | solution.py:250
  67.2 3.8 %collective-permute-done.15.refs_2_ = f32[512,128]{1,0:T(8,128)S(1)} collective-permute-done((f32[512,128]{1,0:T(8,128)S(1)}, f32[512,128]{1,0:T(8,128)S(1)}, u32[]{:S(2)}, u32[]{:S(2)}) %collective-permute-start.15) | collective-permute-done | bytes 262176 | tf_op jit(solution)/shard_map/ppermute | solution.py:250
  71.4 3.6 %collective-permute-start.23 = (f32[256,128]{1,0:T(8,128)S(1)}, f32[256,128]{1,0:T(8,128)S(1)}, u32[]{:S(2)}, u32[]{:S(2)}) collective-permute-start(f32[256,128]{1,0:T(8,128)S(1)} %get-tuple-element.84.refs_3_.refs_0_), channel_id=1, source_target_pairs={{0,6},{1,7},{2,8},{3,9},{4,10},{5,11},{6,12},{7,13},{8,14},{9,15},... | collective-permute-start | bytes 393224 | tf_op jit(solution)/shard_map/ppermute | solution.py:250
  75.1 1.3 %collective-permute-start.20 = (f32[256,128]{1,0:T(8,128)S(1)}, f32[256,128]{1,0:T(8,128)S(1)}, u32[]{:S(2)}, u32[]{:S(2)}) collective-permute-start(f32[256,128]{1,0:T(8,128)S(1)} %get-tuple-element.77.refs_3_.refs_0_), channel_id=1, source_target_pairs={{0,2},{1,3},{2,4},{3,5},{4,6},{5,7},{6,8},{7,9},{8,10},{9,11},{10,... | collective-permute-start | bytes 393224 | tf_op jit(solution)/shard_map/ppermute | solution.py:250
  77.1 0.8 collective-permute-done.24.refs_2_
  78.0 9.8 %collective-permute-done.23.refs_1_ = f32[256,128]{1,0:T(8,128)S(1)} collective-permute-done((f32[256,128]{1,0:T(8,128)S(1)}, f32[256,128]{1,0:T(8,128)S(1)}, u32[]{:S(2)}, u32[]{:S(2)}) %collective-permute-start.23) | collective-permute-done | bytes 131104 | tf_op jit(solution)/shard_map/ppermute | solution.py:250
  88.2 1.1 %place_a.1 = (f32[128,2048]{1,0:T(8,128)S(1)}, f32[128,2048]{1,0:T(8,128)}, f32[16,128]{1,0:T(8,128)}) custom-call(f32[256,128]{1,0:T(8,128)S(1)} %done_a.1.refs_0_.refs_3_, f32[16,128]{1,0:T(8,128)S(1)} %get-tuple-element.87.refs_1_, f32[128,2048]{1,0:T(8,128)S(1)} %place_d.1.refs_3_.refs_2_, ...), custom_call_target="tpu_custom_call", output_to_operand_aliasing={{0}: (2, {})} | custom-call | tf_op jit(solution)/shard_map/place_a/pallas_call | solution.py:229
  (60 shorter events, 6.6 us)
Async XLA Ops:
  8.0 3.0 %collective-permute-start.2 = (f32[1536,128]{1,0:T(8,128)S(1)}, f32[1536,128]{1,0:T(8,128)S(1)}, u32[]{:S(2)}, u32[]{:S(2)}) collective-permute-start(f32[1536,128]{1,0:T(8,128)S(1)} %get-tuple-element.53), channel_id=1, source_target_pairs={{0,1},{1,0},{2,3},{3,2},{4,5},{5,4},{6,7},{7,6},{8,9},{9,8},{10,11... | collective-permute-start | bytes 2359304 | tf_op jit(solution)/shard_map/ppermute | solution.py:250
  10.1 11.0 %collective-permute-start = (f32[1536,128]{1,0:T(8,128)S(1)}, f32[1536,128]{1,0:T(8,128)S(1)}, u32[]{:S(2)}, u32[]{:S(2)}) collective-permute-start(f32[1536,128]{1,0:T(8,128)S(1)} %get-tuple-element.49.refs_2_), channel_id=1, source_target_pairs={{0,1},{1,0},{2,3},{3,2},{4,5},{5,4},{6,7},{7,6},{8,9},{9,8},{10,11... | collective-permute-start | bytes 2359304 | tf_op jit(solution)/shard_map/ppermute | solution.py:250
  11.2 1.5 %copy-start = (bf16[2048]{0:T(1024)(128)(2,1)S(1)}, bf16[2048]{0:T(1024)(128)(2,1)}, u32[]{:S(2)}) copy-start(bf16[2048]{0:T(1024)(128)(2,1)} %param.7) | copy-start | bytes 12292
  12.0 8.6 %collective-permute-start.4 = (f32[1024,128]{1,0:T(8,128)S(1)}, f32[1024,128]{1,0:T(8,128)S(1)}, u32[]{:S(2)}, u32[]{:S(2)}) collective-permute-start(f32[1024,128]{1,0:T(8,128)S(1)} %get-tuple-element.54.refs_2_), channel_id=1, source_target_pairs={{0,1},{1,0},{2,3},{3,2},{4,5},{5,4},{6,7},{7,6},{8,9},{9,8},{10,11... | collective-permute-start | bytes 1572872 | tf_op jit(solution)/shard_map/ppermute | solution.py:250
  12.6 8.2 %collective-permute-start.1 = (f32[1024,128]{1,0:T(8,128)S(1)}, f32[1024,128]{1,0:T(8,128)S(1)}, u32[]{:S(2)}, u32[]{:S(2)}) collective-permute-start(f32[1024,128]{1,0:T(8,128)S(1)} %get-tuple-element.51.refs_2_), channel_id=1, source_target_pairs={{0,1},{1,0},{2,3},{3,2},{4,5},{5,4},{6,7},{7,6},{8,9},{9,8},{10,11... | collective-permute-start | bytes 1572872 | tf_op jit(solution)/shard_map/ppermute | solution.py:250
  12.6 21.3 %collective-permute-start.7 = (f32[1536,128]{1,0:T(8,128)S(1)}, f32[1536,128]{1,0:T(8,128)S(1)}, u32[]{:S(2)}, u32[]{:S(2)}) collective-permute-start(f32[1536,128]{1,0:T(8,128)S(1)} %sum1_d.1.refs_2_.refs_1_), channel_id=1, source_target_pairs={{0,2},{1,3},{2,0},{3,1},{4,6},{5,7},{6,4},{7,5},{8,10},{9,11},{10,... | collective-permute-start | bytes 2359304 | tf_op jit(solution)/shard_map/ppermute | solution.py:250
  19.8 1.2 %collective-permute-start.3 = (f32[16,128]{1,0:T(8,128)S(1)}, f32[16,128]{1,0:T(8,128)S(1)}, u32[]{:S(2)}, u32[]{:S(2)}) collective-permute-start(f32[16,128]{1,0:T(8,128)S(1)} %vector.1.refs_2_), channel_id=1, source_target_pairs={{0,1},{1,0},{2,3},{3,2},{4,5},{5,4},{6,7},{7,6},{8,9},{9,8},{10,11... | collective-permute-start | bytes 24584 | tf_op jit(solution)/shard_map/ppermute | solution.py:250
  22.0 2.5 %collective-permute-start.5 = (f32[1024,128]{1,0:T(8,128)S(1)}, f32[1024,128]{1,0:T(8,128)S(1)}, u32[]{:S(2)}, u32[]{:S(2)}) collective-permute-start(f32[1024,128]{1,0:T(8,128)S(1)} %get-tuple-element.59.refs_2_), channel_id=1, source_target_pairs={{0,1},{1,0},{2,3},{3,2},{4,5},{5,4},{6,7},{7,6},{8,9},{9,8},{10,11... | collective-permute-start | bytes 1572872 | tf_op jit(solution)/shard_map/ppermute | solution.py:250
  22.4 3.6 %collective-permute-start.9 = (f32[1024,128]{1,0:T(8,128)S(1)}, f32[1024,128]{1,0:T(8,128)S(1)}, u32[]{:S(2)}, u32[]{:S(2)}) collective-permute-start(f32[1024,128]{1,0:T(8,128)S(1)} %get-tuple-element.55.refs_3_), channel_id=1, source_target_pairs={{0,1},{1,0},{2,3},{3,2},{4,5},{5,4},{6,7},{7,6},{8,9},{9,8},{10,11... | collective-permute-start | bytes 1572872 | tf_op jit(solution)/shard_map/ppermute | solution.py:250
  22.6 3.6 %collective-permute-start.8 = (f32[1024,128]{1,0:T(8,128)S(1)}, f32[1024,128]{1,0:T(8,128)S(1)}, u32[]{:S(2)}, u32[]{:S(2)}) collective-permute-start(f32[1024,128]{1,0:T(8,128)S(1)} %get-tuple-element.57.refs_2_), channel_id=1, source_target_pairs={{0,1},{1,0},{2,3},{3,2},{4,5},{5,4},{6,7},{7,6},{8,9},{9,8},{10,11... | collective-permute-start | bytes 1572872 | tf_op jit(solution)/shard_map/ppermute | solution.py:250
  22.9 14.9 %collective-permute-start.12 = (f32[1040,128]{1,0:T(8,128)S(1)}, f32[1040,128]{1,0:T(8,128)S(1)}, u32[]{:S(2)}, u32[]{:S(2)}) collective-permute-start(f32[1040,128]{1,0:T(8,128)S(1)} %sum1_b.1.refs_2_.refs_1_), channel_id=1, source_target_pairs={{0,4},{1,5},{2,6},{3,7},{4,0},{5,1},{6,2},{7,3},{8,12},{9,13},{10,... | collective-permute-start | bytes 1597448 | tf_op jit(solution)/shard_map/ppermute | solution.py:250
  24.6 20.6 %collective-permute-start.11 = (f32[1024,128]{1,0:T(8,128)S(1)}, f32[1024,128]{1,0:T(8,128)S(1)}, u32[]{:S(2)}, u32[]{:S(2)}) collective-permute-start(f32[1024,128]{1,0:T(8,128)S(1)} %sum1_c.1.refs_2_.refs_1_), channel_id=1, source_target_pairs={{0,2},{1,3},{2,0},{3,1},{4,6},{5,7},{6,4},{7,5},{8,10},{9,11},{10,... | collective-permute-start | bytes 1572872 | tf_op jit(solution)/shard_map/ppermute | solution.py:250
  26.0 28.4 %collective-permute-start.6 = (f32[1024,128]{1,0:T(8,128)S(1)}, f32[1024,128]{1,0:T(8,128)S(1)}, u32[]{:S(2)}, u32[]{:S(2)}) collective-permute-start(f32[1024,128]{1,0:T(8,128)S(1)} %get-tuple-element.61.refs_2_), channel_id=1, source_target_pairs={{0,1},{1,0},{2,3},{3,2},{4,5},{5,4},{6,7},{7,6},{8,9},{9,8},{10,11... | collective-permute-start | bytes 1572872 | tf_op jit(solution)/shard_map/ppermute | solution.py:250
  26.2 29.7 %collective-permute-start.13 = (f32[1024,128]{1,0:T(8,128)S(1)}, f32[1024,128]{1,0:T(8,128)S(1)}, u32[]{:S(2)}, u32[]{:S(2)}) collective-permute-start(f32[1024,128]{1,0:T(8,128)S(1)} %sum1_a.1.refs_2_.refs_1_), channel_id=1, source_target_pairs={{0,2},{1,3},{2,0},{3,1},{4,6},{5,7},{6,4},{7,5},{8,10},{9,11},{10,... | collective-permute-start | bytes 1572872 | tf_op jit(solution)/shard_map/ppermute | solution.py:250
  34.1 18.0 %collective-permute-start.10 = (f32[768,128]{1,0:T(8,128)S(1)}, f32[768,128]{1,0:T(8,128)S(1)}, u32[]{:S(2)}, u32[]{:S(2)}) collective-permute-start(f32[768,128]{1,0:T(8,128)S(1)} %get-tuple-element.65.refs_3_.refs_1_), channel_id=1, source_target_pairs={{0,4},{1,5},{2,6},{3,7},{4,0},{5,1},{6,2},{7,3},{8,12},{9,13},{10,... | collective-permute-start | bytes 1179656 | tf_op jit(solution)/shard_map/ppermute | solution.py:250
  37.9 16.5 %collective-permute-start.14 = (f32[528,128]{1,0:T(8,128)S(1)}, f32[528,128]{1,0:T(8,128)S(1)}, u32[]{:S(2)}, u32[]{:S(2)}) collective-permute-start(f32[528,128]{1,0:T(8,128)S(1)} %get-tuple-element.66.refs_3_.refs_1_), channel_id=1, source_target_pairs={{0,8},{1,9},{2,10},{3,11},{4,12},{5,13},{6,14},{7,15},{8,0},{9,1},... | collective-permute-start | bytes 811016 | tf_op jit(solution)/shard_map/ppermute | solution.py:250
  45.3 17.0 %collective-permute-start.18 = (f32[512,128]{1,0:T(8,128)S(1)}, f32[512,128]{1,0:T(8,128)S(1)}, u32[]{:S(2)}, u32[]{:S(2)}) collective-permute-start(f32[512,128]{1,0:T(8,128)S(1)} %get-tuple-element.67.refs_3_.refs_1_), channel_id=1, source_target_pairs={{0,4},{1,5},{2,6},{3,7},{4,0},{5,1},{6,2},{7,3},{8,12},{9,13},{10,... | collective-permute-start | bytes 786440 | tf_op jit(solution)/shard_map/ppermute | solution.py:250
  52.1 14.2 %collective-permute-start.17 = (f32[512,128]{1,0:T(8,128)S(1)}, f32[512,128]{1,0:T(8,128)S(1)}, u32[]{:S(2)}, u32[]{:S(2)}) collective-permute-start(f32[512,128]{1,0:T(8,128)S(1)} %get-tuple-element.68.refs_2_.refs_1_), channel_id=1, source_target_pairs={{0,8},{1,9},{2,10},{3,11},{4,12},{5,13},{6,14},{7,15},{8,0},{9,1},... | collective-permute-start | bytes 786440 | tf_op jit(solution)/shard_map/ppermute | solution.py:250
  56.0 15.0 %collective-permute-start.15 = (f32[512,128]{1,0:T(8,128)S(1)}, f32[512,128]{1,0:T(8,128)S(1)}, u32[]{:S(2)}, u32[]{:S(2)}) collective-permute-start(f32[512,128]{1,0:T(8,128)S(1)} %get-tuple-element.72.refs_3_.refs_1_), channel_id=1, source_target_pairs={{0,4},{1,5},{2,6},{3,7},{4,0},{5,1},{6,2},{7,3},{8,12},{9,13},{10,... | collective-permute-start | bytes 786440 | tf_op jit(solution)/shard_map/ppermute | solution.py:250
  57.9 8.5 %collective-permute-start.16 = (f32[272,128]{1,0:T(8,128)S(1)}, f32[272,128]{1,0:T(8,128)S(1)}, u32[]{:S(2)}, u32[]{:S(2)}) collective-permute-start(f32[272,128]{1,0:T(8,128)S(1)} %get-tuple-element.70.refs_3_.refs_1_), channel_id=1, source_target_pairs={{0,2},{1,3},{2,0},{3,1},{4,6},{5,7},{6,4},{7,5},{8,10},{9,11},{10,... | collective-permute-start | bytes 417800 | tf_op jit(solution)/shard_map/ppermute | solution.py:250
  62.3 9.1 %collective-permute-start.22 = (f32[256,128]{1,0:T(8,128)S(1)}, f32[256,128]{1,0:T(8,128)S(1)}, u32[]{:S(2)}, u32[]{:S(2)}) collective-permute-start(f32[256,128]{1,0:T(8,128)S(1)} %get-tuple-element.76.refs_3_.refs_1_), channel_id=1, source_target_pairs={{0,8},{1,9},{2,10},{3,11},{4,12},{5,13},{6,14},{7,15},{8,0},{9,1},... | collective-permute-start | bytes 393224 | tf_op jit(solution)/shard_map/ppermute | solution.py:250
  66.4 10.3 %collective-permute-start.25 = (f32[256,128]{1,0:T(8,128)S(1)}, f32[256,128]{1,0:T(8,128)S(1)}, u32[]{:S(2)}, u32[]{:S(2)}) collective-permute-start(f32[256,128]{1,0:T(8,128)S(1)} %get-tuple-element.78.refs_3_.refs_0_), channel_id=1, source_target_pairs={{0,4},{1,5},{2,6},{3,7},{4,8},{5,9},{6,10},{7,11},{8,12},{9,13},{1... | collective-permute-start | bytes 393224 | tf_op jit(solution)/shard_map/ppermute | solution.py:250
  67.2 9.1 %collective-permute-start.26 = (f32[128,128]{1,0:T(8,128)S(1)}, f32[128,128]{1,0:T(8,128)S(1)}, u32[]{:S(2)}, u32[]{:S(2)}) collective-permute-start(f32[128,128]{1,0:T(8,128)S(1)} %get-tuple-element.86), channel_id=1, source_target_pairs={{0,1},{1,0},{2,3},{3,2},{4,5},{5,4},{6,7},{7,6},{8,9},{9,8},{10,11... | collective-permute-start | bytes 196616 | tf_op jit(solution)/shard_map/ppermute | solution.py:250
  71.4 16.3 %collective-permute-start.23 = (f32[256,128]{1,0:T(8,128)S(1)}, f32[256,128]{1,0:T(8,128)S(1)}, u32[]{:S(2)}, u32[]{:S(2)}) collective-permute-start(f32[256,128]{1,0:T(8,128)S(1)} %get-tuple-element.84.refs_3_.refs_0_), channel_id=1, source_target_pairs={{0,6},{1,7},{2,8},{3,9},{4,10},{5,11},{6,12},{7,13},{8,14},{9,15},... | collective-permute-start | bytes 393224 | tf_op jit(solution)/shard_map/ppermute | solution.py:250
  75.1 12.9 %collective-permute-start.20 = (f32[256,128]{1,0:T(8,128)S(1)}, f32[256,128]{1,0:T(8,128)S(1)}, u32[]{:S(2)}, u32[]{:S(2)}) collective-permute-start(f32[256,128]{1,0:T(8,128)S(1)} %get-tuple-element.77.refs_3_.refs_0_), channel_id=1, source_target_pairs={{0,2},{1,3},{2,4},{3,5},{4,6},{5,7},{6,8},{7,9},{8,10},{9,11},{10,... | collective-permute-start | bytes 393224 | tf_op jit(solution)/shard_map/ppermute | solution.py:250
  76.3 11.6 %collective-permute-start.21 = (f32[256,128]{1,0:T(8,128)S(1)}, f32[256,128]{1,0:T(8,128)S(1)}, u32[]{:S(2)}, u32[]{:S(2)}) collective-permute-start(f32[256,128]{1,0:T(8,128)S(1)} %get-tuple-element.82), channel_id=1, source_target_pairs={{0,1},{1,0},{2,3},{3,2},{4,5},{5,4},{6,7},{7,6},{8,9},{9,8},{10,11... | collective-permute-start | bytes 393224 | tf_op jit(solution)/shard_map/ppermute | solution.py:250
  76.3 11.8 %collective-permute-start.19 = (f32[256,128]{1,0:T(8,128)S(1)}, f32[256,128]{1,0:T(8,128)S(1)}, u32[]{:S(2)}, u32[]{:S(2)}) collective-permute-start(f32[256,128]{1,0:T(8,128)S(1)} %get-tuple-element.80.refs_3_.refs_1_), channel_id=1, source_target_pairs={{0,8},{1,9},{2,10},{3,11},{4,12},{5,13},{6,14},{7,15},{8,0},{9,1},... | collective-permute-start | bytes 393224 | tf_op jit(solution)/shard_map/ppermute | solution.py:250
  76.7 1.3 %collective-permute-start.24 = (f32[128,128]{1,0:T(8,128)S(1)}, f32[128,128]{1,0:T(8,128)S(1)}, u32[]{:S(2)}, u32[]{:S(2)}) collective-permute-start(f32[128,128]{1,0:T(8,128)S(1)} %get-tuple-element.85), channel_id=1, source_target_pairs={{0,1},{1,0},{2,3},{3,2},{4,5},{5,4},{6,7},{7,6},{8,9},{9,8},{10,11... | collective-permute-start | bytes 196616 | tf_op jit(solution)/shard_map/ppermute | solution.py:250
